TPU v7x, 128 devices: a whole 4x4x4 slice. The times are simulated.
128 devices in a mesh: ctx: 16 (over x, y), exp: 8 (over z, core).
Axes of the slice: x: 4, y: 4, z: 4, core: 2. Of those that a mesh axis runs over, the one named last changes fastest.
Arguments:
- queries: bfloat16 [1024, 8192], P('ctx', 'exp'), may hold values from -6 to 6
- key_rows: bfloat16 [1024, 1024], P('ctx', 'exp'), may hold values from -8 to 8
- values: bfloat16 [1024, 1024], P('ctx', 'exp'), may hold values from -6 to 6
- span_order: int32 [16], replicated, may hold values from 0 to 15, each once
- residual: bfloat16 [1024, 4096], P(('ctx', 'exp')), may hold values from -3 to 3
- out_weight: bfloat16 [8192, 4096], P('exp', 'ctx'), may hold values from -0.0625 to 0.0625
- norm_gain: bfloat16 [4096], replicated, may hold values from 0.099609375 to 1.8984375
- routes: int32 [1024, 2], P(('ctx', 'exp')), may hold values from 0 to 7, all different within a row; in each aligned block of 8 rows (0 to 7, 8 to 15, ...) at most 4 rows name the same one
- route_gates: float32 [1024, 2], P(('ctx', 'exp')), may hold values from 0.2 to 1
- gate_proj: bfloat16 [8, 4096, 12288], P('exp', None, 'ctx'), may hold values from -0.09375 to 0.09375
- up_proj: bfloat16 [8, 4096, 12288], P('exp', None, 'ctx'), may hold values from -0.09375 to 0.09375
- down_proj: bfloat16 [8, 12288, 4096], P('exp', 'ctx'), may hold values from -0.0546875 to 0.0546875
Outputs:
- layer_out: bfloat16 [1024, 4096], P(('ctx', 'exp'))
Inputs may be any that keep to these rules, and one draw needn't show every extreme that they name: `routes`: each row names two different experts; among the 8 rows of one device no expert is named more than 4 times, and in some devices' rows one expert is named exactly 4 times. `span_order`: a permutation of the block numbers.
All inputs are finite; a program needn't handle non-finite values.
Results may differ from a plain program's by a relative error of at most 0.024.
Values may be sent and summed in bfloat16 or wider, within the bound.
No kernel may reach another device: no remote copies, remote signals or barrier semaphores. Data moves between devices by JAX's collectives and lax.ppermute only.
A program may use at most 128 MiB of HBM per device.

v0:
```python
import math

import jax
import jax.numpy as jnp
from jax import lax
from jax.sharding import PartitionSpec as P

HEADS = 64
KV_HEADS = 8
HD = 128
CYCLE_STEPS = 4
CAP = 4


def passed_along(shard, axis, by):
    length = lax.axis_size(axis)
    return lax.ppermute(shard, axis, [(i, (i + by) % length) for i in range(length)])


def per_device(
    queries,
    key_rows,
    values,
    span_order,
    residual,
    out_weight,
    norm_gain,
    routes,
    route_gates,
    gate_proj,
    up_proj,
    down_proj,
):
    n_ctx = lax.axis_size("ctx")
    n_exp = lax.axis_size("exp")
    here = lax.axis_index("ctx")
    block_rows = queries.shape[0]
    group = HEADS // KV_HEADS
    kv_local = key_rows.shape[1] // HD
    width = kv_local * HD
    offsets = jnp.arange(block_rows, dtype=jnp.int32)
    query_pos = span_order[here] * block_rows + offsets
    packed = jnp.concatenate([key_rows, values], axis=1)
    collected = [packed]
    positions = [query_pos]
    current = packed
    for step in range(1, CYCLE_STEPS):
        current = passed_along(current, "ctx", 1)
        collected.append(current)
        positions.append(span_order[(here - step) % n_ctx] * block_rows + offsets)
    stacked = jnp.concatenate(collected, axis=0)
    key_all = stacked[:, :width].reshape(-1, kv_local, HD)
    value_all = stacked[:, width:].reshape(-1, kv_local, HD)
    key_pos = jnp.concatenate(positions)
    query_heads = queries.reshape(block_rows, kv_local, group, HD)
    scores = jnp.einsum(
        "qkgd,lkd->kgql", query_heads, key_all, preferred_element_type=jnp.float32
    ) * (1.0 / math.sqrt(HD))
    admitted = key_pos[None, :] <= query_pos[:, None]
    scores = jnp.where(admitted[None, None], scores, -1e30)
    row_max = jnp.max(scores, axis=-1, keepdims=True)
    exp_scores = jnp.exp(scores - row_max)
    attend_probs = (exp_scores / jnp.sum(exp_scores, axis=-1, keepdims=True)).astype(jnp.bfloat16)
    mixed = jnp.einsum(
        "kgql,lkd->qkgd", attend_probs, value_all, preferred_element_type=jnp.float32
    )
    attended = mixed.astype(jnp.bfloat16).reshape(block_rows, kv_local * group * HD)
    token_count = residual.shape[0]
    partial_value = jnp.dot(
        attended,
        lax.all_gather(out_weight, "ctx", axis=1, tiled=True),
        preferred_element_type=jnp.float32,
    )
    projected = lax.psum_scatter(
        partial_value.astype(jnp.bfloat16), "exp", scatter_dimension=0, tiled=True
    ).astype(jnp.float32)
    hidden_wide = (
        (residual.astype(jnp.float32) + projected).astype(jnp.bfloat16).astype(jnp.float32)
    )
    inverse = lax.rsqrt(jnp.mean(hidden_wide * hidden_wide, axis=-1, keepdims=True) + 1e-06)
    normed = (hidden_wide * inverse * norm_gain.astype(jnp.float32)).astype(jnp.bfloat16)
    slots = n_exp * CAP
    flat_routes = routes.reshape(-1)
    pair_ids = jnp.arange(flat_routes.shape[0], dtype=jnp.int32)
    same_expert = flat_routes[:, None] == flat_routes[None, :]
    earlier = pair_ids[None, :] < pair_ids[:, None]
    slot_number = jnp.sum(jnp.where(same_expert & earlier, 1, 0), axis=1).astype(jnp.int32)
    target = flat_routes * CAP + slot_number
    match_table = jnp.where(
        target[:, None] == jnp.arange(slots, dtype=jnp.int32)[None, :], 1.0, 0.0
    ).astype(jnp.bfloat16)
    assign = match_table.reshape(token_count, 2, slots).sum(axis=1)
    send_rows = jnp.einsum("ts,td->sd", assign, normed, preferred_element_type=jnp.float32).astype(
        jnp.bfloat16
    )
    outgoing = jnp.broadcast_to(send_rows[None], (n_ctx, slots, send_rows.shape[1])).reshape(
        n_ctx * slots, -1
    )
    incoming = lax.all_to_all(outgoing, ("ctx", "exp"), split_axis=0, concat_axis=0, tiled=True)
    gate_act = jnp.dot(incoming, gate_proj[0], preferred_element_type=jnp.float32)
    up_act = jnp.dot(incoming, up_proj[0], preferred_element_type=jnp.float32)
    inner = (jax.nn.silu(gate_act) * up_act).astype(jnp.bfloat16)
    partial_out = jnp.dot(inner, down_proj[0], preferred_element_type=jnp.float32)
    returned = lax.all_to_all(
        partial_out.astype(jnp.bfloat16), ("ctx", "exp"), split_axis=0, concat_axis=0, tiled=True
    ).astype(partial_out.dtype)
    expert_rows = returned.reshape(n_ctx, slots, -1).sum(axis=0).astype(jnp.bfloat16)
    picked = jnp.dot(match_table, expert_rows, preferred_element_type=jnp.float32).reshape(
        token_count, 2, -1
    )
    total = hidden_wide + route_gates[:, 0:1] * picked[:, 0] + route_gates[:, 1:2] * picked[:, 1]
    return total.astype(jnp.bfloat16)


def solution(mesh):
    return jax.shard_map(
        per_device,
        mesh=mesh,
        in_specs=(
            P("ctx", "exp"),
            P("ctx", "exp"),
            P("ctx", "exp"),
            P(),
            P(("ctx", "exp"), None),
            P("exp", "ctx"),
            P(),
            P(("ctx", "exp"), None),
            P(("ctx", "exp"), None),
            P("exp", None, "ctx"),
            P("exp", None, "ctx"),
            P("exp", "ctx", None),
        ),
        out_specs=P(("ctx", "exp"), None),
        check_vma=False,
    )
```

profile of v0, /device:TPU:0, one launch (start us, length us, event | category | flops | bytes accessed | tf_op | source)
XLA Modules:
  0.0 313.9 jit_solution(12227354756179570839)
XLA Ops:
  6.5 0.7 all-gather.2.cloned.1.call-update
  7.3 0.7 constant_dynamic-update-slice_fusion.1
  8.0 0.7 constant_dynamic-update-slice_fusion
  8.8 1.7 collective-permute-start
  10.4 1.4 fusion.42
  14.2 1.7 collective-permute-done
  16.1 7.2 %collective-permute-done.1 = bf16[64,256]{1,0:T(8,128)(2,1)S(1)} collective-permute-done((bf16[64,256]{1,0:T(8,128)(2,1)S(1)}, bf16[64,256]{1,0:T(8,128)(2,1)S(1)}, u32[]{:S(2)}, u32[]{:S(2)}) %collective-permute-start.1) | collective-permute-done | bytes 32800 | tf_op jit(solution)/shard_map/ppermute | solution.py:17
  23.3 7.8 %collective-permute-done.2 = bf16[64,256]{1,0:T(8,128)(2,1)S(1)} collective-permute-done((bf16[64,256]{1,0:T(8,128)(2,1)S(1)}, bf16[64,256]{1,0:T(8,128)(2,1)S(1)}, u32[]{:S(2)}, u32[]{:S(2)}) %collective-permute-start.2) | collective-permute-done | bytes 32800 | tf_op jit(solution)/shard_map/ppermute | solution.py:17
  31.1 0.3 fusion.43
  31.4 0.3 fusion.16
  31.7 0.3 fusion.13
  32.0 0.1 copy.23
  32.1 58.6 %all-gather.2.cloned.1.call-done = bf16[1024,4096]{1,0:T(8,128)(2,1)} async-done(((bf16[1024,256]{1,0:T(8,128)(2,1)}), bf16[1024,4096]{1,0:T(8,128)(2,1)}) %all-gather.2.cloned.1.call-update) | async-done | bytes 8388624 | tf_op jit(solution)/shard_map/all_gather | solution.py:71
  90.7 5.8 %convolution_convert_fusion = bf16[64,4096]{1,0:T(8,128)(2,1)} fusion(bf16[1024,4096]{1,0:T(8,128)(2,1)} %all-gather.2.cloned.1.call-done, bf16[8,8,8,128]{3,2,1,0:T(8,128)(2,1)S(1)} %bitcast.78), kind=kOutput, calls=%fused_computation.7 | convolution fusion | flops 537133056 | bytes 9043968 | tf_op jit(solution)/shard_map/dot_general | solution.py:69
  96.7 0.2 select_reduce_fusion
  97.0 0.1 copy.26
  97.2 30.0 %reduce-scatter.2.cloned.1.call-done = bf16[8,4096]{1,0:T(8,128)(2,1)} async-done(((bf16[64,4096]{1,0:T(8,128)(2,1)}), bf16[8,4096]{1,0:T(8,128)(2,1)}) %reduce-scatter.2.cloned.1.call-update) | async-done | bytes 65552 | tf_op jit(solution)/shard_map/reduce_scatter | solution.py:74
  127.2 1.0 fusion.20
  128.2 1.1 convolution_convert_fusion.1
  129.4 2.5 broadcast_in_dim.51
  131.8 7.2 %all_to_all.16 = bf16[128,4,4096]{2,1,0:T(4,128)(2,1)} reshape(bf16[16,32,4096]{2,1,0:T(8,128)(2,1)} %broadcast_in_dim.51) | data formatting | bytes 8388608 | tf_op jit(solution)/shard_map/all_to_all | solution.py:99
  139.0 60.7 %all_to_all.24 = bf16[128,4,4096]{2,1,0:T(4,128)(2,1)} all-to-all(bf16[128,4,4096]{2,1,0:T(4,128)(2,1)} %all_to_all.16), channel_id=1, replica_groups=mesh['ctx'=16,'exp'=8] {'ctx','exp'}, dimensions={0} | all-to-all | bytes 8388608 | tf_op jit(solution)/shard_map/all_to_all | solution.py:99
  199.7 6.9 %all_to_all.18 = bf16[512,4096]{1,0:T(8,128)(2,1)} reshape(bf16[128,4,4096]{2,1,0:T(4,128)(2,1)} %all_to_all.24) | data formatting | bytes 8388608 | tf_op jit(solution)/shard_map/all_to_all | solution.py:99
  206.6 7.0 %fusion.4 = f32[512,768]{1,0:T(8,128)S(1)} fusion(bf16[512,4096]{1,0:T(8,128)(2,1)} %all_to_all.18, bf16[1,4096,768]{2,1,0:T(8,128)(2,1)} %param.21), kind=kOutput, calls=%fused_computation.4 | convolution fusion | flops 3221225472 | bytes 12058624 | tf_op jit(solution)/shard_map/dot_general | solution.py:100
  213.6 16.6 %fusion.6 = bf16[512,4096]{1,0:T(8,128)(2,1)} fusion(bf16[1,768,4096]{2,1,0:T(8,128)(2,1)} %param.23, f32[512,768]{1,0:T(8,128)S(1)} %fusion.4, bf16[512,4096]{1,0:T(8,128)(2,1)} %all_to_all.18, bf16[1,4096,768]{2,1,0:T(8,128)(2,1)} %param.22), kind=kOutput, calls=%fused_computation.6 | convolution fusion | flops 6446907392 | bytes 22544384 | tf_op jit(solution)/shard_map/dot_general | solution.py:103
  230.2 7.2 %all_to_all.19 = bf16[128,4,4096]{2,1,0:T(4,128)(2,1)} reshape(bf16[512,4096]{1,0:T(8,128)(2,1)} %fusion.6) | data formatting | bytes 8388608 | tf_op jit(solution)/shard_map/all_to_all | solution.py:104
  237.5 6.0 %all-to-all-start.1 = ((bf16[128,4,4096]{2,1,0:T(4,128)(2,1)}), bf16[128,4,4096]{2,1,0:T(4,128)(2,1)}, u32[]{:S(2)}, u32[]{:S(2)}) async-start(bf16[128,4,4096]{2,1,0:T(4,128)(2,1)} %all_to_all.19), calls=%async_computation.2 | async-start | bytes 8388608 | tf_op jit(solution)/shard_map/all_to_all | solution.py:104
  243.5 52.7 %all-to-all-done.1 = bf16[128,4,4096]{2,1,0:T(4,128)(2,1)} async-done(((bf16[128,4,4096]{2,1,0:T(4,128)(2,1)}), bf16[128,4,4096]{2,1,0:T(4,128)(2,1)}, u32[]{:S(2)}, u32[]{:S(2)}) %all-to-all-start.1) | async-done | bytes 4194336 | tf_op jit(solution)/shard_map/all_to_all | solution.py:104
  296.2 6.9 %all_to_all.21 = bf16[16,32,4096]{2,1,0:T(8,128)(2,1)} reshape(bf16[128,4,4096]{2,1,0:T(4,128)(2,1)} %all-to-all-done.1) | data formatting | bytes 8388608 | tf_op jit(solution)/shard_map/all_to_all | solution.py:104
  303.1 3.0 reduce_sum.58
  306.1 0.2 fusion.17
  306.4 0.7 fusion.24
  (31 shorter events, 0.6 us)
Async XLA Ops:
  6.5 24.6 %copy-start = (bf16[64,1024]{1,0:T(8,128)(2,1)S(1)}, bf16[64,1024]{1,0:T(8,128)(2,1)}, u32[]{:S(2)}) copy-start(bf16[64,1024]{1,0:T(8,128)(2,1)} %param.12) | copy-start | bytes 393220
  6.5 84.2 %all-gather.2.cloned.1.call-start = ((), (), s32[]{:S(2)}) async-start(), calls=%async_computation.3 | async-start | bytes 8912896 | tf_op jit(solution)/shard_map/all_gather | solution.py:71
  7.3 120.0 %reduce-scatter.2.cloned.1.call-start = ((), (), s32[]{:S(2)}) async-start(), calls=%async_computation.4 | async-start | bytes 589824 | tf_op jit(solution)/shard_map/reduce_scatter | solution.py:74
  8.8 7.2 %collective-permute-start = (bf16[64,256]{1,0:T(8,128)(2,1)S(1)}, bf16[64,256]{1,0:T(8,128)(2,1)S(1)}, u32[]{:S(2)}, u32[]{:S(2)}) collective-permute-start(bf16[64,256]{1,0:T(8,128)(2,1)S(1)} %constant_dynamic-update-slice_fusion), channel_id=1, source_target_pairs={{0,8},{8,16},{16,24},{24,32},{32,40},{40,48},{48,56},{56,64},{64,7... | collective-permute-start | bytes 98312 | tf_op jit(solution)/shard_map/ppermute | solution.py:17
  16.0 7.2 %collective-permute-start.1 = (bf16[64,256]{1,0:T(8,128)(2,1)S(1)}, bf16[64,256]{1,0:T(8,128)(2,1)S(1)}, u32[]{:S(2)}, u32[]{:S(2)}) collective-permute-start(bf16[64,256]{1,0:T(8,128)(2,1)S(1)} %collective-permute-done), channel_id=1, source_target_pairs={{0,8},{8,16},{16,24},{24,32},{32,40},{40,48},{48,56},{56,64},{64,7... | collective-permute-start | bytes 98312 | tf_op jit(solution)/shard_map/ppermute | solution.py:17
  23.2 7.8 %collective-permute-start.2 = (bf16[64,256]{1,0:T(8,128)(2,1)S(1)}, bf16[64,256]{1,0:T(8,128)(2,1)S(1)}, u32[]{:S(2)}, u32[]{:S(2)}) collective-permute-start(bf16[64,256]{1,0:T(8,128)(2,1)S(1)} %collective-permute-done.1), channel_id=1, source_target_pairs={{0,8},{8,16},{16,24},{24,32},{32,40},{40,48},{48,56},{56,64},{64,7... | collective-permute-start | bytes 98312 | tf_op jit(solution)/shard_map/ppermute | solution.py:17
  90.7 5.9 %copy-start.4 = (s32[8,2]{0,1:T(2,128)S(1)}, s32[8,2]{0,1:T(2,128)}, u32[]{:S(2)}) copy-start(s32[8,2]{0,1:T(2,128)} %param.19) | copy-start | bytes 196
  90.7 6.4 %copy-start.3 = (bf16[4096]{0:T(1024)(128)(2,1)S(1)}, bf16[4096]{0:T(1024)(128)(2,1)}, u32[]{:S(2)}) copy-start(bf16[4096]{0:T(1024)(128)(2,1)} %param.18) | copy-start | bytes 24580
  90.7 36.5 %copy-start.1 = (bf16[8,4096]{1,0:T(8,128)(2,1)S(1)}, bf16[8,4096]{1,0:T(8,128)(2,1)}, u32[]{:S(2)}) copy-start(bf16[8,4096]{1,0:T(8,128)(2,1)} %param.16) | copy-start | bytes 196612
  237.5 6.0 %copy-start.5 = (f32[8,2]{0,1:T(2,128)S(1)}, f32[8,2]{0,1:T(2,128)}, u32[]{:S(2)}) copy-start(f32[8,2]{0,1:T(2,128)} %param.20) | copy-start | bytes 196
  237.5 58.7 %all-to-all-start.1 = ((bf16[128,4,4096]{2,1,0:T(4,128)(2,1)}), bf16[128,4,4096]{2,1,0:T(4,128)(2,1)}, u32[]{:S(2)}, u32[]{:S(2)}) async-start(bf16[128,4,4096]{2,1,0:T(4,128)(2,1)} %all_to_all.19), calls=%async_computation.2 | async-start | bytes 8388608 | tf_op jit(solution)/shard_map/all_to_all | solution.py:104
  303.1 3.3 %copy-start.2 = (bf16[8,4096]{1,0:T(8,128)(2,1)S(1)}, bf16[8,4096]{1,0:T(8,128)(2,1)}, u32[]{:S(2)}) copy-start(bf16[8,4096]{1,0:T(8,128)(2,1)} %reduce-scatter.2.cloned.1.call-done) | copy-start | bytes 196612
Sparse Core Ops, SparseCore 0:
  9.5 81.1 all-gather.1
  96.7 30.5 reduce-scatter.1
where the time goes:
time: 315 us; the launch traced here: 314 us
  waiting for transfers between devices  159 us (50%)
  blocking collectives  60.7 us (19%)
  local copies, waits for them, and re-layouts  34 us (11%)
  matrix products  31.4 us (10%)
  between operations  15.9 us (5%)
  starting transfers between devices  7.68 us (2%)
  other arithmetic  5.46 us (2%)
    all_to_all x1, blocking collectives, per_device(): lax.all_to_all(outgoing, ('ctx', 'exp'), split_axis=0, concat_axis=0, til...  60.7 us
    all_gather x1, waiting for transfers between devices, per_device(): lax.all_gather(out_weight, 'ctx', axis=1, tiled=True)  58.6 us
    all_to_all x1, waiting for transfers between devices, per_device(): lax.all_to_all(partial_out.astype(jnp.bfloat16), ('ctx', 'exp'), split_ax...  52.7 us
    reduce_scatter x1, waiting for transfers between devices, per_device(): lax.psum_scatter(partial_value.astype(jnp.bfloat16), 'exp', scatter_dimen...  30 us
    ppermute x3, waiting for transfers between devices, passed_along(): lax.ppermute(shard, axis, [(i, (i + by) % length) for i in range(length)])  16.7 us
    dot_general x1, matrix products, per_device(): jnp.dot(inner, down_proj[0], preferred_element_type=jnp.float32)  16.6 us
    all_to_all x2, local copies, waits for them, and re-layouts, per_device(): lax.all_to_all(partial_out.astype(jnp.bfloat16), ('ctx', 'exp'), split_ax...  14.1 us
    all_to_all x2, local copies, waits for them, and re-layouts, per_device(): lax.all_to_all(outgoing, ('ctx', 'exp'), split_axis=0, concat_axis=0, til...  14.1 us
  transfers between devices with their start and end apart: 6, of which 6 were waited for; matrix products, arithmetic and copies ran while one was open for 1% of the time, Pallas kernels for 0%

commit v1 on v0

v1 whole, which is shorter than its diff:
```python
import math

import jax
import jax.numpy as jnp
from jax import lax
from jax.experimental import pallas as pl
from jax.experimental.pallas import tpu as pltpu
from jax.sharding import PartitionSpec as P

HEADS = 64
KV_HEADS = 8
HD = 128
CYCLE_STEPS = 4
CAP = 4
SIDE = 4
BOTH = ("ctx", "exp")
SHIFTS = (1, 3, 2)


def number(x, y, z, core):
    return (((x % SIDE) * SIDE + y % SIDE) * SIDE + z % SIDE) * 2 + core


def everyone():
    return [
        (x, y, z, core)
        for x in range(SIDE)
        for y in range(SIDE)
        for z in range(SIDE)
        for core in range(2)
    ]


def first_axis(d):
    return [
        (number(x, y, z, c), number(x + d * c, y + d * (1 - c), z, c)) for x, y, z, c in everyone()
    ]


def second_axis(d):
    return [
        (number(x, y, z, c), number(x + d * (1 - c), y + d * c, z, c)) for x, y, z, c in everyone()
    ]


def z_axis(d):
    return [(number(x, y, z, c), number(x, y, z + d, c)) for x, y, z, c in everyone()]


def sibling(shard):
    pairs = [(number(x, y, z, c), number(x, y, z, 1 - c)) for x, y, z, c in everyone()]
    return lax.ppermute(shard, BOTH, pairs)


def gathered(shard, along):
    got = {0: shard}
    for d in SHIFTS:
        got[d] = lax.ppermute(shard, BOTH, along(d))
    return [got[d] for d in range(SIDE)]


def dealt(blocks, along, sign):
    got = {0: blocks[0]}
    for d in SHIFTS:
        got[d] = lax.ppermute(blocks[d], BOTH, along(sign * d))
    return [got[d] for d in range(SIDE)]


def added(blocks):
    total = blocks[0].astype(jnp.float32)
    for block in blocks[1:]:
        total = total + block.astype(jnp.float32)
    return total


def expert_kernel(x_ref, gate_ref, up_ref, down_ref, out_ref, acc_ref):
    step = pl.program_id(0)
    x = x_ref[...]
    gate = jnp.dot(x, gate_ref[...], preferred_element_type=jnp.float32)
    up = jnp.dot(x, up_ref[...], preferred_element_type=jnp.float32)
    inner = (gate / (1.0 + jnp.exp(-gate)) * up).astype(jnp.bfloat16)
    part = jnp.dot(inner, down_ref[...], preferred_element_type=jnp.float32)

    @pl.when(step == 0)
    def _():
        acc_ref[...] = part

    @pl.when(jnp.logical_and(step > 0, step < pl.num_programs(0) - 1))
    def _():
        acc_ref[...] += part

    @pl.when(step == pl.num_programs(0) - 1)
    def _():
        out_ref[...] = (acc_ref[...] + part).astype(out_ref.dtype)


def expert(x, gate, up, down):
    rows, width = x.shape
    hidden = gate.shape[1]
    tile = 256
    steps = hidden // tile
    return pl.pallas_call(
        expert_kernel,
        grid=(steps,),
        in_specs=[
            pl.BlockSpec((rows, width), lambda j: (0, 0)),
            pl.BlockSpec((width, tile), lambda j: (0, j)),
            pl.BlockSpec((width, tile), lambda j: (0, j)),
            pl.BlockSpec((tile, width), lambda j: (j, 0)),
        ],
        out_specs=pl.BlockSpec((rows, width), lambda j: (0, 0)),
        out_shape=jax.ShapeDtypeStruct((rows, width), jnp.bfloat16),
        scratch_shapes=[pltpu.VMEM((rows, width), jnp.float32)],
        compiler_params=pltpu.CompilerParams(vmem_limit_bytes=56 * 1024 * 1024),
        cost_estimate=pl.CostEstimate(
            flops=6 * rows * width * hidden,
            bytes_accessed=6 * width * hidden + 4 * rows * width,
            transcendentals=rows * hidden,
        ),
    )(x, gate, up, down)


def per_device(
    queries,
    key_rows,
    values,
    span_order,
    residual,
    out_weight,
    norm_gain,
    routes,
    route_gates,
    gate_proj,
    up_proj,
    down_proj,
):
    n_ctx = lax.axis_size("ctx")
    n_exp = lax.axis_size("exp")
    here = lax.axis_index("ctx")
    column = lax.axis_index("exp")
    core = column % 2
    z_here = column // 2
    block_rows = queries.shape[0]
    group = HEADS // KV_HEADS
    kv_local = key_rows.shape[1] // HD
    width = kv_local * HD
    token_count, model = residual.shape
    offsets = jnp.arange(block_rows, dtype=jnp.int32)
    query_pos = span_order[here] * block_rows + offsets

    packed = jnp.concatenate([key_rows, values], axis=1)
    collected = [packed]
    positions = [query_pos]
    for step in range(1, CYCLE_STEPS):
        pairs = [(i, (i + step) % n_ctx) for i in range(n_ctx)]
        collected.append(lax.ppermute(packed, "ctx", pairs))
        positions.append(span_order[(here - step) % n_ctx] * block_rows + offsets)
    weight_other = sibling(out_weight)
    stacked = jnp.concatenate(collected, axis=0)
    key_all = stacked[:, :width].reshape(-1, kv_local, HD)
    value_all = stacked[:, width:].reshape(-1, kv_local, HD)
    key_pos = jnp.concatenate(positions)
    query_heads = queries.reshape(block_rows, kv_local, group, HD)
    scores = jnp.einsum(
        "qkgd,lkd->kgql", query_heads, key_all, preferred_element_type=jnp.float32
    ) * (1.0 / math.sqrt(HD))
    admitted = key_pos[None, :] <= query_pos[:, None]
    scores = jnp.where(admitted[None, None], scores, -1e30)
    row_max = jnp.max(scores, axis=-1, keepdims=True)
    exp_scores = jnp.exp(scores - row_max)
    attend_probs = (exp_scores / jnp.sum(exp_scores, axis=-1, keepdims=True)).astype(jnp.bfloat16)
    mixed = jnp.einsum(
        "kgql,lkd->qkgd", attend_probs, value_all, preferred_element_type=jnp.float32
    )
    attended = mixed.astype(jnp.bfloat16).reshape(SIDE, 2, token_count, kv_local * group * HD)

    half = SIDE * token_count
    rows_0 = attended[:, 0].reshape(half, -1)
    rows_1 = attended[:, 1].reshape(half, -1)
    kept = jnp.where(core == 0, rows_0, rows_1)
    given = jnp.where(core == 0, rows_1, rows_0)
    paired = jnp.concatenate([kept, sibling(given)], axis=1)
    weight = jnp.concatenate([out_weight, weight_other], axis=0)
    line = jnp.concatenate(gathered(paired, first_axis), axis=0)
    plane = jnp.concatenate(gathered(line, second_axis), axis=0)
    partial_value = jnp.dot(plane, weight, preferred_element_type=jnp.float32)
    columns = partial_value.shape[1]
    partial_value = partial_value.reshape(n_ctx, SIDE, token_count, columns)
    by_z = jnp.roll(jnp.moveaxis(partial_value, 1, 0), -z_here, axis=0)
    others = dealt([by_z[0]] + [by_z[d].astype(jnp.bfloat16) for d in range(1, SIDE)], z_axis, 1)
    slab = added(others).astype(jnp.bfloat16)
    x_here, y_here = here // SIDE, here % SIDE
    target = jnp.arange(n_ctx, dtype=jnp.int32)
    back_x = (x_here - target // SIDE) % SIDE
    back_y = (y_here - target % SIDE) % SIDE
    place = jnp.where(core == 0, back_x * SIDE + back_y, back_y * SIDE + back_x)
    slab = jnp.take(slab, place, axis=0)
    owned = lax.all_to_all(slab, "ctx", split_axis=0, concat_axis=0, tiled=True)
    projected = jnp.moveaxis(owned, 0, 1).reshape(token_count, model).astype(jnp.float32)
    hidden_wide = (
        (residual.astype(jnp.float32) + projected).astype(jnp.bfloat16).astype(jnp.float32)
    )
    inverse = lax.rsqrt(jnp.mean(hidden_wide * hidden_wide, axis=-1, keepdims=True) + 1e-06)
    normed = (hidden_wide * inverse * norm_gain.astype(jnp.float32)).astype(jnp.bfloat16)

    slots = n_exp * CAP
    flat_routes = routes.reshape(-1)
    pair_ids = jnp.arange(flat_routes.shape[0], dtype=jnp.int32)
    same_expert = flat_routes[:, None] == flat_routes[None, :]
    earlier = pair_ids[None, :] < pair_ids[:, None]
    slot_number = jnp.sum(jnp.where(same_expert & earlier, 1, 0), axis=1).astype(jnp.int32)
    ahead = (flat_routes // 2 - z_here) % SIDE
    target = (ahead * 2 + (flat_routes + core) % 2) * CAP + slot_number
    match_table = jnp.where(
        target[:, None] == jnp.arange(slots, dtype=jnp.int32)[None, :], 1.0, 0.0
    ).astype(jnp.bfloat16)
    assign = match_table.reshape(token_count, 2, slots).sum(axis=1)
    send_rows = jnp.einsum("ts,td->sd", assign, normed, preferred_element_type=jnp.float32).astype(
        jnp.bfloat16
    )
    per_z = 2 * CAP
    sent = dealt([send_rows[d * per_z : (d + 1) * per_z] for d in range(SIDE)], z_axis, 1)
    column_rows = jnp.concatenate([r[:CAP] for r in sent] + [r[CAP:] for r in sent], axis=0)
    n1 = SIDE * CAP
    line = gathered(column_rows, first_axis)
    line = jnp.concatenate([r[:n1] for r in line] + [r[n1:] for r in line], axis=0)
    n2 = SIDE * n1
    plane = gathered(line, second_axis)
    mine = [r[:n2] for r in plane]
    theirs = sibling(jnp.concatenate([r[n2:] for r in plane], axis=0))
    rows_in = jnp.concatenate(mine + [theirs], axis=0)
    rows_out = expert(rows_in, gate_proj[0], up_proj[0], down_proj[0])
    n3 = SIDE * n2
    swapped = sibling(rows_out[n3:])
    plane = [
        jnp.concatenate([rows_out[d * n2 : (d + 1) * n2], swapped[d * n2 : (d + 1) * n2]], axis=0)
        for d in range(SIDE)
    ]
    line = added(dealt(plane, second_axis, -1)).astype(jnp.bfloat16)
    line = [
        jnp.concatenate([line[d * n1 : (d + 1) * n1], line[n2 + d * n1 : n2 + (d + 1) * n1]], axis=0)
        for d in range(SIDE)
    ]
    column_rows = added(dealt(line, first_axis, -1)).astype(jnp.bfloat16)
    sent = [
        jnp.concatenate(
            [column_rows[d * CAP : (d + 1) * CAP], column_rows[n1 + d * CAP : n1 + (d + 1) * CAP]],
            axis=0,
        )
        for d in range(SIDE)
    ]
    expert_rows = jnp.concatenate(dealt(sent, z_axis, -1), axis=0)
    picked = jnp.dot(match_table, expert_rows, preferred_element_type=jnp.float32).reshape(
        token_count, 2, -1
    )
    total = hidden_wide + route_gates[:, 0:1] * picked[:, 0] + route_gates[:, 1:2] * picked[:, 1]
    return total.astype(jnp.bfloat16)


def solution(mesh):
    return jax.shard_map(
        per_device,
        mesh=mesh,
        in_specs=(
            P("ctx", "exp"),
            P("ctx", "exp"),
            P("ctx", "exp"),
            P(),
            P(("ctx", "exp"), None),
            P("exp", "ctx"),
            P(),
            P(("ctx", "exp"), None),
            P(("ctx", "exp"), None),
            P("exp", None, "ctx"),
            P("exp", None, "ctx"),
            P("exp", "ctx", None),
        ),
        out_specs=P(("ctx", "exp"), None),
        check_vma=False,
    )
```

time: 315 us -> 246 us (0.78)
  blocking collectives: 60.7 us -> 0 us
  starting transfers between devices: 7.68 us -> 45.8 us
  waiting for transfers between devices: 159 us -> 127 us
  matrix products: 31.4 us -> 2.9 us
  Pallas kernels: 0 us -> 19.1 us
  between operations: 15.9 us -> 3.35 us
  local copies, waits for them, and re-layouts: 34 us -> 43.6 us
    ppermute x3 -> x34, waiting for transfers between devices: 16.7 us -> 119 us  [the longest x12 64.1 us: gathered(): got[d] = lax.ppermute(shard, BOTH, along(d))]
    all_to_all x1 -> x0, blocking collectives: 60.7 us -> none  [per_device(): lax.all_to_all(outgoing, ('ctx', 'exp'), split_axis=0, concat_axis=0, til...]
    all_gather x1 -> x0, waiting for transfers between devices: 58.6 us -> none  [per_device(): lax.all_gather(out_weight, 'ctx', axis=1, tiled=True)]
    all_to_all x1, waiting for transfers between devices: 52.7 us -> 7.59 us  [per_device(): owned = lax.all_to_all(slab, 'ctx', split_axis=0, concat_axis=0, tiled=True)]
    ppermute x3 -> x34, starting transfers between devices: 1.66 us -> 40.6 us  [the longest x15 20.4 us: dealt(): got[d] = lax.ppermute(blocks[d], BOTH, along(sign * d))]
    concatenate x0 -> x6, local copies, waits for them, and re-layouts: none -> 30.9 us  [the longest x1 20.2 us: per_device(): rows_in = jnp.concatenate(mine + [theirs], axis=0)]
    reduce_scatter x1 -> x0, waiting for transfers between devices: 30 us -> none  [per_device(): lax.psum_scatter(partial_value.astype(jnp.bfloat16), 'exp', scatter_dimen...]
    all_to_all x4 -> x0, local copies, waits for them, and re-layouts: 28.2 us -> none  [the longest x2 14.1 us: per_device(): lax.all_to_all(partial_out.astype(jnp.bfloat16), ('ctx', 'exp'), split_ax...]
  transfers between devices with their start and end apart: 6 -> 35, of which waited for: 6 -> 29; matrix products, arithmetic and copies ran while one was open for 1% -> 3% of each run, Pallas kernels for 0% -> 0%
where the time goes in v1:
time: 246 us; the launch traced here: 245 us
  waiting for transfers between devices  127 us (52%)
  starting transfers between devices  45.8 us (19%)
  local copies, waits for them, and re-layouts  43.6 us (18%)
  Pallas kernels  19.1 us (8%)
  other arithmetic  3.91 us (2%)
  between operations  3.35 us (1%)
  matrix products  2.9 us (1%)
    ppermute x12, waiting for transfers between devices, gathered(): got[d] = lax.ppermute(shard, BOTH, along(d))  64.1 us
    ppermute x15, waiting for transfers between devices, dealt(): got[d] = lax.ppermute(blocks[d], BOTH, along(sign * d))  45.6 us
    ppermute x15, starting transfers between devices, dealt(): got[d] = lax.ppermute(blocks[d], BOTH, along(sign * d))  20.4 us
    concatenate x1, local copies, waits for them, and re-layouts, per_device(): rows_in = jnp.concatenate(mine + [theirs], axis=0)  20.2 us
    pallas_call x1, Pallas kernels, expert(): pl.pallas_call(expert_kernel, grid=(steps,), in_specs=[pl.BlockSpec((rows...  19.1 us
    ppermute x12, starting transfers between devices, gathered(): got[d] = lax.ppermute(shard, BOTH, along(d))  14.2 us
    concatenate x1, local copies, waits for them, and re-layouts, per_device(): theirs = sibling(jnp.concatenate([r[n2:] for r in plane], axis=0))  10.2 us
    ppermute x4, waiting for transfers between devices, sibling(): return lax.ppermute(shard, BOTH, pairs)  8.51 us
  transfers between devices with their start and end apart: 35, of which 29 were waited for; matrix products, arithmetic and copies ran while one was open for 3% of the time, Pallas kernels for 0%

profile of v1, /device:TPU:0, one launch (start us, length us, event | category | flops | bytes accessed | tf_op | source)
XLA Modules:
  0.0 245.4 jit_solution(6978324563590160227)
XLA Ops:
  1.5 3.1 %collective-permute-start.2 = (bf16[64,256]{1,0:T(8,128)(2,1)S(1)}, bf16[64,256]{1,0:T(8,128)(2,1)S(1)}, u32[]{:S(2)}, u32[]{:S(2)}) collective-permute-start(bf16[64,256]{1,0:T(8,128)(2,1)S(1)} %constant_dynamic-update-slice_fusion), channel_id=1, source_target_pairs={{0,24},{8,32},{16,40},{24,48},{32,56},{40,64},{48,72},{56,80},{64,... | collective-permute-start | bytes 98312 | tf_op jit(solution)/shard_map/ppermute | solution.py:156
  15.9 1.9 collective-permute-start.5
  24.3 1.8 collective-permute-start.9
  27.7 14.7 %collective-permute-done.7 = bf16[128,2048]{1,0:T(8,128)(2,1)S(1)} collective-permute-done((bf16[128,2048]{1,0:T(8,128)(2,1)S(1)}, bf16[128,2048]{1,0:T(8,128)(2,1)S(1)}, u32[]{:S(2)}, u32[]{:S(2)}) %collective-permute-start.7) | collective-permute-done | bytes 524320 | tf_op jit(solution)/shard_map/ppermute | solution.py:58
  44.6 2.0 collective-permute-start.11
  46.6 2.2 collective-permute-start.13
  48.8 1.8 collective-permute-start.12
  51.3 3.2 %collective-permute-done.12 = bf16[16,8,256]{2,1,0:T(8,128)(2,1)S(1)} collective-permute-done((bf16[16,8,256]{2,1,0:T(8,128)(2,1)S(1)}, bf16[16,8,256]{2,1,0:T(8,128)(2,1)S(1)}, u32[]{:S(2)}, u32[]{:S(2)}) %collective-permute-start.12) | collective-permute-done | bytes 65568 | tf_op jit(solution)/shard_map/ppermute | solution.py:65
  55.9 5.2 %all-to-all-start = ((bf16[16,8,256]{2,1,0:T(8,128)(2,1)}), bf16[16,8,256]{2,1,0:T(8,128)(2,1)S(1)}, u32[]{:S(2)}, u32[]{:S(2)}) async-start(bf16[16,8,256]{2,1,0:T(8,128)(2,1)} %broadcast_select_fusion), calls=%async_computation | async-start | bytes 131072 | tf_op jit(solution)/shard_map/all_to_all | solution.py:198
  61.1 7.6 %all-to-all-done = bf16[16,8,256]{2,1,0:T(8,128)(2,1)S(1)} async-done(((bf16[16,8,256]{2,1,0:T(8,128)(2,1)}), bf16[16,8,256]{2,1,0:T(8,128)(2,1)S(1)}, u32[]{:S(2)}, u32[]{:S(2)}) %all-to-all-start) | async-done | bytes 65568 | tf_op jit(solution)/shard_map/all_to_all | solution.py:198
  69.2 2.0 collective-permute-start.16
  73.6 3.6 %collective-permute-done.15 = bf16[8,4096]{1,0:T(8,128)(2,1)S(1)} collective-permute-done((bf16[8,4096]{1,0:T(8,128)(2,1)S(1)}, bf16[8,4096]{1,0:T(8,128)(2,1)S(1)}, u32[]{:S(2)}, u32[]{:S(2)}) %collective-permute-start.15) | collective-permute-done | bytes 65568 | tf_op jit(solution)/shard_map/ppermute | solution.py:65
  80.8 3.6 %collective-permute-done.19 = bf16[32,4096]{1,0:T(8,128)(2,1)S(1)} collective-permute-done((bf16[32,4096]{1,0:T(8,128)(2,1)S(1)}, bf16[32,4096]{1,0:T(8,128)(2,1)S(1)}, u32[]{:S(2)}, u32[]{:S(2)}) %collective-permute-start.19) | collective-permute-done | bytes 262176 | tf_op jit(solution)/shard_map/ppermute | solution.py:58
  84.4 2.8 %collective-permute-done.18 = bf16[32,4096]{1,0:T(8,128)(2,1)S(1)} collective-permute-done((bf16[32,4096]{1,0:T(8,128)(2,1)S(1)}, bf16[32,4096]{1,0:T(8,128)(2,1)S(1)}, u32[]{:S(2)}, u32[]{:S(2)}) %collective-permute-start.18) | collective-permute-done | bytes 262176 | tf_op jit(solution)/shard_map/ppermute | solution.py:58
  87.2 15.5 %collective-permute-done.17 = bf16[32,4096]{1,0:T(8,128)(2,1)S(1)} collective-permute-done((bf16[32,4096]{1,0:T(8,128)(2,1)S(1)}, bf16[32,4096]{1,0:T(8,128)(2,1)S(1)}, u32[]{:S(2)}, u32[]{:S(2)}) %collective-permute-start.17) | collective-permute-done | bytes 262176 | tf_op jit(solution)/shard_map/ppermute | solution.py:58
  106.1 11.9 %collective-permute-done.22 = bf16[128,4096]{1,0:T(8,128)(2,1)S(1)} collective-permute-done((bf16[128,4096]{1,0:T(8,128)(2,1)S(1)}, bf16[128,4096]{1,0:T(8,128)(2,1)S(1)}, u32[]{:S(2)}, u32[]{:S(2)}) %collective-permute-start.22) | collective-permute-done | bytes 1048608 | tf_op jit(solution)/shard_map/ppermute | solution.py:58
  118.9 2.1 collective-permute-done.21
  121.9 10.3 %collective-permute-done.20 = bf16[128,4096]{1,0:T(8,128)(2,1)S(1)} collective-permute-done((bf16[128,4096]{1,0:T(8,128)(2,1)S(1)}, bf16[128,4096]{1,0:T(8,128)(2,1)S(1)}, u32[]{:S(2)}, u32[]{:S(2)}) %collective-permute-start.20) | collective-permute-done | bytes 1048608 | tf_op jit(solution)/shard_map/ppermute | solution.py:58
  133.2 10.2 %concatenate.93 = bf16[256,4096]{1,0:T(8,128)(2,1)S(1)} concatenate(bf16[4,4096]{1,0:T(4,128)(2,1)} %copy-done.11, bf16[4,4096]{1,0:T(4,128)(2,1)} %copy-done.16, bf16[4,4096]{1,0:T(4,128)(2,1)} %copy-done.15, bf16[4,4096]{1,0:T(4,128)(2,1)} %copy-done.14, bf16[16,4096]{1,0:T(8,128)(2,1)} %copy-done.6, bf16[16,4096]{1,0:T(8,128)(2,1)} %copy-done.5, bf16[16,4096]{1,0:T(8,128)(2,1)} %copy-done.4, ...), dimensions={0} | concatenate | bytes 4194304 | tf_op jit(solution)/shard_map/concatenate | solution.py:230
  143.5 4.1 %collective-permute-done.23 = bf16[256,4096]{1,0:T(8,128)(2,1)S(1)} collective-permute-done((bf16[256,4096]{1,0:T(8,128)(2,1)S(1)}, bf16[256,4096]{1,0:T(8,128)(2,1)S(1)}, u32[]{:S(2)}, u32[]{:S(2)}) %collective-permute-start.23) | collective-permute-done | bytes 2097184 | tf_op jit(solution)/shard_map/ppermute | solution.py:52
  149.0 20.2 %concatenate.94.x_ref = bf16[512,4096]{1,0:T(8,128)(2,1)} concatenate(bf16[4,4096]{1,0:T(4,128)(2,1)} %copy-done.9, bf16[4,4096]{1,0:T(4,128)(2,1)} %copy-done.13, bf16[4,4096]{1,0:T(4,128)(2,1)} %copy-done.12, bf16[4,4096]{1,0:T(4,128)(2,1)} %copy-done.10, bf16[16,4096]{1,0:T(8,128)(2,1)S(1)} %get-tuple-element.46, bf16[16,4096]{1,0:T(8,128)(2,1)S(1)} %get-tuple-element.44, ...), dimensions={0} | concatenate | bytes 8388608 | tf_op jit(solution)/shard_map/concatenate | solution.py:231
  169.2 19.1 %shard_map.118 = bf16[512,4096]{1,0:T(8,128)(2,1)} custom-call(bf16[512,4096]{1,0:T(8,128)(2,1)} %concatenate.94.x_ref, bf16[4096,768]{1,0:T(8,128)(2,1)} %bitcast.96, bf16[4096,768]{1,0:T(8,128)(2,1)} %bitcast.97, bf16[768,4096]{1,0:T(8,128)(2,1)} %bitcast.98), custom_call_target="tpu_custom_call" | custom-call | flops 9663676416 | bytes 27262976 | tf_op jit(solution)/shard_map/pallas_call | solution.py:102
  188.3 1.9 slice.288
  191.3 3.2 %collective-permute-done.24 = bf16[256,4096]{1,0:T(8,128)(2,1)S(1)} collective-permute-done((bf16[256,4096]{1,0:T(8,128)(2,1)S(1)}, bf16[256,4096]{1,0:T(8,128)(2,1)S(1)}, u32[]{:S(2)}, u32[]{:S(2)}) %collective-permute-start.24) | collective-permute-done | bytes 2097184 | tf_op jit(solution)/shard_map/ppermute | solution.py:52
  198.0 11.6 %collective-permute-done.25 = bf16[128,4096]{1,0:T(8,128)(2,1)S(1)} collective-permute-done((bf16[128,4096]{1,0:T(8,128)(2,1)S(1)}, bf16[128,4096]{1,0:T(8,128)(2,1)S(1)}, u32[]{:S(2)}, u32[]{:S(2)}) %collective-permute-start.25) | collective-permute-done | bytes 1048608 | tf_op jit(solution)/shard_map/ppermute | solution.py:65
  209.6 2.4 collective-permute-done.26
  212.0 11.1 %collective-permute-done.27 = bf16[128,4096]{1,0:T(8,128)(2,1)S(1)} collective-permute-done((bf16[128,4096]{1,0:T(8,128)(2,1)S(1)}, bf16[128,4096]{1,0:T(8,128)(2,1)S(1)}, u32[]{:S(2)}, u32[]{:S(2)}) %collective-permute-start.27) | collective-permute-done | bytes 1048608 | tf_op jit(solution)/shard_map/ppermute | solution.py:65
  227.2 3.1 %collective-permute-done.28 = bf16[32,4096]{1,0:T(8,128)(2,1)S(1)} collective-permute-done((bf16[32,4096]{1,0:T(8,128)(2,1)S(1)}, bf16[32,4096]{1,0:T(8,128)(2,1)S(1)}, u32[]{:S(2)}, u32[]{:S(2)}) %collective-permute-start.28) | collective-permute-done | bytes 262176 | tf_op jit(solution)/shard_map/ppermute | solution.py:65
  232.0 2.7 %collective-permute-done.30 = bf16[32,4096]{1,0:T(8,128)(2,1)S(1)} collective-permute-done((bf16[32,4096]{1,0:T(8,128)(2,1)S(1)}, bf16[32,4096]{1,0:T(8,128)(2,1)S(1)}, u32[]{:S(2)}, u32[]{:S(2)}) %collective-permute-start.30) | collective-permute-done | bytes 262176 | tf_op jit(solution)/shard_map/ppermute | solution.py:65
  236.1 2.2 collective-permute-start.32
  239.8 2.1 collective-permute-done.32
  242.0 1.9 collective-permute-done.33
  (163 shorter events, 50.9 us)
Async XLA Ops:
  1.5 11.0 %collective-permute-start.2 = (bf16[64,256]{1,0:T(8,128)(2,1)S(1)}, bf16[64,256]{1,0:T(8,128)(2,1)S(1)}, u32[]{:S(2)}, u32[]{:S(2)}) collective-permute-start(bf16[64,256]{1,0:T(8,128)(2,1)S(1)} %constant_dynamic-update-slice_fusion), channel_id=1, source_target_pairs={{0,24},{8,32},{16,40},{24,48},{32,56},{40,64},{48,72},{56,80},{64,... | collective-permute-start | bytes 98312 | tf_op jit(solution)/shard_map/ppermute | solution.py:156
  4.6 7.9 %collective-permute-start.1 = (bf16[64,256]{1,0:T(8,128)(2,1)S(1)}, bf16[64,256]{1,0:T(8,128)(2,1)S(1)}, u32[]{:S(2)}, u32[]{:S(2)}) collective-permute-start(bf16[64,256]{1,0:T(8,128)(2,1)S(1)} %constant_dynamic-update-slice_fusion), channel_id=1, source_target_pairs={{0,16},{8,24},{16,32},{24,40},{32,48},{40,56},{48,64},{56,72},{64,... | collective-permute-start | bytes 98312 | tf_op jit(solution)/shard_map/ppermute | solution.py:156
  6.1 7.2 %collective-permute-start = (bf16[64,256]{1,0:T(8,128)(2,1)S(1)}, bf16[64,256]{1,0:T(8,128)(2,1)S(1)}, u32[]{:S(2)}, u32[]{:S(2)}) collective-permute-start(bf16[64,256]{1,0:T(8,128)(2,1)S(1)} %constant_dynamic-update-slice_fusion), channel_id=1, source_target_pairs={{0,8},{8,16},{16,24},{24,32},{32,40},{40,48},{48,56},{56,64},{64,7... | collective-permute-start | bytes 98312 | tf_op jit(solution)/shard_map/ppermute | solution.py:156
  7.1 35.5 %collective-permute-start.10 = (bf16[1024,256]{1,0:T(8,128)(2,1)}, bf16[1024,256]{1,0:T(8,128)(2,1)}, u32[]{:S(2)}, u32[]{:S(2)}) collective-permute-start(bf16[1024,256]{1,0:T(8,128)(2,1)} %param.17), channel_id=1, source_target_pairs={{0,1},{1,0},{2,3},{3,2},{4,5},{5,4},{6,7},{7,6},{8,9},{9,8},{10,11... | collective-permute-start | bytes 1572872 | tf_op jit(solution)/shard_map/ppermute | solution.py:52
  15.9 6.6 %collective-permute-start.5 = (bf16[32,2048]{1,0:T(8,128)(2,1)S(1)}, bf16[32,2048]{1,0:T(8,128)(2,1)S(1)}, u32[]{:S(2)}, u32[]{:S(2)}) collective-permute-start(bf16[32,2048]{1,0:T(8,128)(2,1)S(1)} %get-tuple-element.55), channel_id=1, source_target_pairs={{0,16},{1,65},{2,18},{3,67},{4,20},{5,69},{6,22},{7,71},{8,24},{9,... | collective-permute-start | bytes 393224 | tf_op jit(solution)/shard_map/ppermute | solution.py:58
  17.7 6.2 %collective-permute-start.4 = (bf16[32,2048]{1,0:T(8,128)(2,1)S(1)}, bf16[32,2048]{1,0:T(8,128)(2,1)S(1)}, u32[]{:S(2)}, u32[]{:S(2)}) collective-permute-start(bf16[32,2048]{1,0:T(8,128)(2,1)S(1)} %get-tuple-element.55), channel_id=1, source_target_pairs={{0,8},{1,33},{2,10},{3,35},{4,12},{5,37},{6,14},{7,39},{8,16},{9,4... | collective-permute-start | bytes 393224 | tf_op jit(solution)/shard_map/ppermute | solution.py:58
  19.3 5.0 %collective-permute-start.6 = (bf16[32,2048]{1,0:T(8,128)(2,1)S(1)}, bf16[32,2048]{1,0:T(8,128)(2,1)S(1)}, u32[]{:S(2)}, u32[]{:S(2)}) collective-permute-start(bf16[32,2048]{1,0:T(8,128)(2,1)S(1)} %get-tuple-element.55), channel_id=1, source_target_pairs={{0,24},{1,97},{2,26},{3,99},{4,28},{5,101},{6,30},{7,103},{8,0},{9... | collective-permute-start | bytes 393224 | tf_op jit(solution)/shard_map/ppermute | solution.py:58
  24.3 18.2 %collective-permute-start.9 = (bf16[128,2048]{1,0:T(8,128)(2,1)S(1)}, bf16[128,2048]{1,0:T(8,128)(2,1)S(1)}, u32[]{:S(2)}, u32[]{:S(2)}) collective-permute-start(bf16[128,2048]{1,0:T(8,128)(2,1)S(1)} %pad_maximum_fusion.3), channel_id=1, source_target_pairs={{0,96},{1,25},{2,98},{3,27},{4,100},{5,29},{6,102},{7,31},{8,104},... | collective-permute-start | bytes 1572872 | tf_op jit(solution)/shard_map/ppermute | solution.py:58
  26.1 16.3 %collective-permute-start.8 = (bf16[128,2048]{1,0:T(8,128)(2,1)S(1)}, bf16[128,2048]{1,0:T(8,128)(2,1)S(1)}, u32[]{:S(2)}, u32[]{:S(2)}) collective-permute-start(bf16[128,2048]{1,0:T(8,128)(2,1)S(1)} %pad_maximum_fusion.3), channel_id=1, source_target_pairs={{0,64},{1,17},{2,66},{3,19},{4,68},{5,21},{6,70},{7,23},{8,72},{9,... | collective-permute-start | bytes 1572872 | tf_op jit(solution)/shard_map/ppermute | solution.py:58
  27.7 14.8 %collective-permute-start.7 = (bf16[128,2048]{1,0:T(8,128)(2,1)S(1)}, bf16[128,2048]{1,0:T(8,128)(2,1)S(1)}, u32[]{:S(2)}, u32[]{:S(2)}) collective-permute-start(bf16[128,2048]{1,0:T(8,128)(2,1)S(1)} %pad_maximum_fusion.3), channel_id=1, source_target_pairs={{0,32},{1,9},{2,34},{3,11},{4,36},{5,13},{6,38},{7,15},{8,40},{9,1... | collective-permute-start | bytes 1572872 | tf_op jit(solution)/shard_map/ppermute | solution.py:58
  44.6 6.4 %collective-permute-start.11 = (bf16[16,8,256]{2,1,0:T(8,128)(2,1)S(1)}, bf16[16,8,256]{2,1,0:T(8,128)(2,1)S(1)}, u32[]{:S(2)}, u32[]{:S(2)}) collective-permute-start(bf16[16,8,256]{2,1,0:T(8,128)(2,1)S(1)} %get-tuple-element.52), channel_id=1, source_target_pairs={{0,2},{1,3},{2,4},{3,5},{4,6},{5,7},{6,0},{7,1},{8,10},{9,11},{10,... | collective-permute-start | bytes 196616 | tf_op jit(solution)/shard_map/ppermute | solution.py:65
  46.6 4.8 %collective-permute-start.13 = (bf16[16,8,256]{2,1,0:T(8,128)(2,1)S(1)}, bf16[16,8,256]{2,1,0:T(8,128)(2,1)S(1)}, u32[]{:S(2)}, u32[]{:S(2)}) collective-permute-start(bf16[16,8,256]{2,1,0:T(8,128)(2,1)S(1)} %get-tuple-element.53), channel_id=1, source_target_pairs={{0,6},{1,7},{2,0},{3,1},{4,2},{5,3},{6,4},{7,5},{8,14},{9,15},{10,... | collective-permute-start | bytes 196616 | tf_op jit(solution)/shard_map/ppermute | solution.py:65
  48.8 5.8 %collective-permute-start.12 = (bf16[16,8,256]{2,1,0:T(8,128)(2,1)S(1)}, bf16[16,8,256]{2,1,0:T(8,128)(2,1)S(1)}, u32[]{:S(2)}, u32[]{:S(2)}) collective-permute-start(bf16[16,8,256]{2,1,0:T(8,128)(2,1)S(1)} %get-tuple-element.54), channel_id=1, source_target_pairs={{0,4},{1,5},{2,6},{3,7},{4,0},{5,1},{6,2},{7,3},{8,12},{9,13},{10,... | collective-permute-start | bytes 196616 | tf_op jit(solution)/shard_map/ppermute | solution.py:65
  55.9 12.9 %all-to-all-start = ((bf16[16,8,256]{2,1,0:T(8,128)(2,1)}), bf16[16,8,256]{2,1,0:T(8,128)(2,1)S(1)}, u32[]{:S(2)}, u32[]{:S(2)}) async-start(bf16[16,8,256]{2,1,0:T(8,128)(2,1)} %broadcast_select_fusion), calls=%async_computation | async-start | bytes 131072 | tf_op jit(solution)/shard_map/all_to_all | solution.py:198
  69.2 4.3 %collective-permute-start.16 = (bf16[8,4096]{1,0:T(8,128)(2,1)S(1)}, bf16[8,4096]{1,0:T(8,128)(2,1)S(1)}, u32[]{:S(2)}, u32[]{:S(2)}) collective-permute-start(bf16[8,4096]{1,0:T(8,128)(2,1)S(1)} %get-tuple-element.49), channel_id=1, source_target_pairs={{0,6},{1,7},{2,0},{3,1},{4,2},{5,3},{6,4},{7,5},{8,14},{9,15},{10,... | collective-permute-start | bytes 196616 | tf_op jit(solution)/shard_map/ppermute | solution.py:65
  71.3 6.0 %collective-permute-start.15 = (bf16[8,4096]{1,0:T(8,128)(2,1)S(1)}, bf16[8,4096]{1,0:T(8,128)(2,1)S(1)}, u32[]{:S(2)}, u32[]{:S(2)}) collective-permute-start(bf16[8,4096]{1,0:T(8,128)(2,1)S(1)} %get-tuple-element.50), channel_id=1, source_target_pairs={{0,4},{1,5},{2,6},{3,7},{4,0},{5,1},{6,2},{7,3},{8,12},{9,13},{10,... | collective-permute-start | bytes 196616 | tf_op jit(solution)/shard_map/ppermute | solution.py:65
  71.5 6.2 %collective-permute-start.14 = (bf16[8,4096]{1,0:T(8,128)(2,1)S(1)}, bf16[8,4096]{1,0:T(8,128)(2,1)S(1)}, u32[]{:S(2)}, u32[]{:S(2)}) collective-permute-start(bf16[8,4096]{1,0:T(8,128)(2,1)S(1)} %get-tuple-element.51), channel_id=1, source_target_pairs={{0,2},{1,3},{2,4},{3,5},{4,6},{5,7},{6,0},{7,1},{8,10},{9,11},{10,... | collective-permute-start | bytes 196616 | tf_op jit(solution)/shard_map/ppermute | solution.py:65
  77.9 6.4 %collective-permute-start.19 = (bf16[32,4096]{1,0:T(8,128)(2,1)S(1)}, bf16[32,4096]{1,0:T(8,128)(2,1)S(1)}, u32[]{:S(2)}, u32[]{:S(2)}) collective-permute-start(bf16[32,4096]{1,0:T(8,128)(2,1)S(1)} %concatenate.91), channel_id=1, source_target_pairs={{0,24},{1,97},{2,26},{3,99},{4,28},{5,101},{6,30},{7,103},{8,0},{9... | collective-permute-start | bytes 786440 | tf_op jit(solution)/shard_map/ppermute | solution.py:58
  79.2 8.0 %collective-permute-start.18 = (bf16[32,4096]{1,0:T(8,128)(2,1)S(1)}, bf16[32,4096]{1,0:T(8,128)(2,1)S(1)}, u32[]{:S(2)}, u32[]{:S(2)}) collective-permute-start(bf16[32,4096]{1,0:T(8,128)(2,1)S(1)} %concatenate.91), channel_id=1, source_target_pairs={{0,16},{1,65},{2,18},{3,67},{4,20},{5,69},{6,22},{7,71},{8,24},{9,... | collective-permute-start | bytes 786440 | tf_op jit(solution)/shard_map/ppermute | solution.py:58
  80.6 22.2 %collective-permute-start.17 = (bf16[32,4096]{1,0:T(8,128)(2,1)S(1)}, bf16[32,4096]{1,0:T(8,128)(2,1)S(1)}, u32[]{:S(2)}, u32[]{:S(2)}) collective-permute-start(bf16[32,4096]{1,0:T(8,128)(2,1)S(1)} %concatenate.91), channel_id=1, source_target_pairs={{0,8},{1,33},{2,10},{3,35},{4,12},{5,37},{6,14},{7,39},{8,16},{9,4... | collective-permute-start | bytes 786440 | tf_op jit(solution)/shard_map/ppermute | solution.py:58
  103.2 14.9 %collective-permute-start.22 = (bf16[128,4096]{1,0:T(8,128)(2,1)S(1)}, bf16[128,4096]{1,0:T(8,128)(2,1)S(1)}, u32[]{:S(2)}, u32[]{:S(2)}) collective-permute-start(bf16[128,4096]{1,0:T(8,128)(2,1)S(1)} %concatenate.92), channel_id=1, source_target_pairs={{0,96},{1,25},{2,98},{3,27},{4,100},{5,29},{6,102},{7,31},{8,104},... | collective-permute-start | bytes 3145736 | tf_op jit(solution)/shard_map/ppermute | solution.py:58
  104.6 16.4 %collective-permute-start.21 = (bf16[128,4096]{1,0:T(8,128)(2,1)S(1)}, bf16[128,4096]{1,0:T(8,128)(2,1)S(1)}, u32[]{:S(2)}, u32[]{:S(2)}) collective-permute-start(bf16[128,4096]{1,0:T(8,128)(2,1)S(1)} %concatenate.92), channel_id=1, source_target_pairs={{0,64},{1,17},{2,66},{3,19},{4,68},{5,21},{6,70},{7,23},{8,72},{9,... | collective-permute-start | bytes 3145736 | tf_op jit(solution)/shard_map/ppermute | solution.py:58
  106.1 26.1 %collective-permute-start.20 = (bf16[128,4096]{1,0:T(8,128)(2,1)S(1)}, bf16[128,4096]{1,0:T(8,128)(2,1)S(1)}, u32[]{:S(2)}, u32[]{:S(2)}) collective-permute-start(bf16[128,4096]{1,0:T(8,128)(2,1)S(1)} %concatenate.92), channel_id=1, source_target_pairs={{0,32},{1,9},{2,34},{3,11},{4,36},{5,13},{6,38},{7,15},{8,40},{9,1... | collective-permute-start | bytes 3145736 | tf_op jit(solution)/shard_map/ppermute | solution.py:58
  194.7 14.9 %collective-permute-start.25 = (bf16[128,4096]{1,0:T(8,128)(2,1)S(1)}, bf16[128,4096]{1,0:T(8,128)(2,1)S(1)}, u32[]{:S(2)}, u32[]{:S(2)}) collective-permute-start(bf16[128,4096]{1,0:T(8,128)(2,1)S(1)} %pad_maximum_fusion), channel_id=1, source_target_pairs={{0,96},{1,25},{2,98},{3,27},{4,100},{5,29},{6,102},{7,31},{8,104},... | collective-permute-start | bytes 3145736 | tf_op jit(solution)/shard_map/ppermute | solution.py:65
  195.5 16.5 %collective-permute-start.26 = (bf16[128,4096]{1,0:T(8,128)(2,1)S(1)}, bf16[128,4096]{1,0:T(8,128)(2,1)S(1)}, u32[]{:S(2)}, u32[]{:S(2)}) collective-permute-start(bf16[128,4096]{1,0:T(8,128)(2,1)S(1)} %pad_maximum_fusion.1), channel_id=1, source_target_pairs={{0,64},{1,17},{2,66},{3,19},{4,68},{5,21},{6,70},{7,23},{8,72},{9,... | collective-permute-start | bytes 3145736 | tf_op jit(solution)/shard_map/ppermute | solution.py:65
  197.1 26.0 %collective-permute-start.27 = (bf16[128,4096]{1,0:T(8,128)(2,1)S(1)}, bf16[128,4096]{1,0:T(8,128)(2,1)S(1)}, u32[]{:S(2)}, u32[]{:S(2)}) collective-permute-start(bf16[128,4096]{1,0:T(8,128)(2,1)S(1)} %pad_maximum_fusion.2), channel_id=1, source_target_pairs={{0,32},{1,9},{2,34},{3,11},{4,36},{5,13},{6,38},{7,15},{8,40},{9,1... | collective-permute-start | bytes 3145736 | tf_op jit(solution)/shard_map/ppermute | solution.py:65
  223.9 6.4 %collective-permute-start.28 = (bf16[32,4096]{1,0:T(8,128)(2,1)S(1)}, bf16[32,4096]{1,0:T(8,128)(2,1)S(1)}, u32[]{:S(2)}, u32[]{:S(2)}) collective-permute-start(bf16[32,4096]{1,0:T(8,128)(2,1)S(1)} %pad_maximum_fusion.4), channel_id=1, source_target_pairs={{0,24},{1,97},{2,26},{3,99},{4,28},{5,101},{6,30},{7,103},{8,0},{9... | collective-permute-start | bytes 786440 | tf_op jit(solution)/shard_map/ppermute | solution.py:65
  224.0 8.1 %collective-permute-start.29 = (bf16[32,4096]{1,0:T(8,128)(2,1)S(1)}, bf16[32,4096]{1,0:T(8,128)(2,1)S(1)}, u32[]{:S(2)}, u32[]{:S(2)}) collective-permute-start(bf16[32,4096]{1,0:T(8,128)(2,1)S(1)} %pad_maximum_fusion.5), channel_id=1, source_target_pairs={{0,16},{1,65},{2,18},{3,67},{4,20},{5,69},{6,22},{7,71},{8,24},{9,... | collective-permute-start | bytes 786440 | tf_op jit(solution)/shard_map/ppermute | solution.py:65
  225.8 9.0 %collective-permute-start.30 = (bf16[32,4096]{1,0:T(8,128)(2,1)S(1)}, bf16[32,4096]{1,0:T(8,128)(2,1)S(1)}, u32[]{:S(2)}, u32[]{:S(2)}) collective-permute-start(bf16[32,4096]{1,0:T(8,128)(2,1)S(1)} %pad_maximum_fusion.6), channel_id=1, source_target_pairs={{0,8},{1,33},{2,10},{3,35},{4,12},{5,37},{6,14},{7,39},{8,16},{9,4... | collective-permute-start | bytes 786440 | tf_op jit(solution)/shard_map/ppermute | solution.py:65
  235.0 4.8 %collective-permute-start.31 = (bf16[8,4096]{1,0:T(8,128)(2,1)S(1)}, bf16[8,4096]{1,0:T(8,128)(2,1)S(1)}, u32[]{:S(2)}, u32[]{:S(2)}) collective-permute-start(bf16[8,4096]{1,0:T(8,128)(2,1)S(1)} %pad_maximum_fusion.9), channel_id=1, source_target_pairs={{0,6},{1,7},{2,0},{3,1},{4,2},{5,3},{6,4},{7,5},{8,14},{9,15},{10,... | collective-permute-start | bytes 196616 | tf_op jit(solution)/shard_map/ppermute | solution.py:65
  236.1 5.8 %collective-permute-start.32 = (bf16[8,4096]{1,0:T(8,128)(2,1)S(1)}, bf16[8,4096]{1,0:T(8,128)(2,1)S(1)}, u32[]{:S(2)}, u32[]{:S(2)}) collective-permute-start(bf16[8,4096]{1,0:T(8,128)(2,1)S(1)} %pad_maximum_fusion.10), channel_id=1, source_target_pairs={{0,4},{1,5},{2,6},{3,7},{4,0},{5,1},{6,2},{7,3},{8,12},{9,13},{10,... | collective-permute-start | bytes 196616 | tf_op jit(solution)/shard_map/ppermute | solution.py:65
  238.3 5.5 %collective-permute-start.33 = (bf16[8,4096]{1,0:T(8,128)(2,1)S(1)}, bf16[8,4096]{1,0:T(8,128)(2,1)S(1)}, u32[]{:S(2)}, u32[]{:S(2)}) collective-permute-start(bf16[8,4096]{1,0:T(8,128)(2,1)S(1)} %pad_maximum_fusion.11), channel_id=1, source_target_pairs={{0,2},{1,3},{2,4},{3,5},{4,6},{5,7},{6,0},{7,1},{8,10},{9,11},{10,... | collective-permute-start | bytes 196616 | tf_op jit(solution)/shard_map/ppermute | solution.py:65
  (24 other events, 382.3 us)

commit v2 on v1

--- a/solution.py
+++ b/solution.py
@@ -2,6 +2,7 @@
 
 import jax
 import jax.numpy as jnp
+import numpy as np
 from jax import lax
 from jax.experimental import pallas as pl
 from jax.experimental.pallas import tpu as pltpu
@@ -43,6 +44,16 @@
     ]
 
 
+def crossed(d):
+    return [
+        (number(x, y, z, c), number(x + d * (1 - c), y + d * c, z, 1 - c)) for x, y, z, c in everyone()
+    ]
+
+
+def uncrossed(d):
+    return [(to, start) for start, to in crossed(d)]
+
+
 def z_axis(d):
     return [(number(x, y, z, c), number(x, y, z + d, c)) for x, y, z, c in everyone()]
 
@@ -73,51 +84,42 @@
     return total
 
 
-def expert_kernel(x_ref, gate_ref, up_ref, down_ref, out_ref, acc_ref):
-    step = pl.program_id(0)
-    x = x_ref[...]
+def expert_kernel(pieces, extra, *refs):
+    x_refs = refs[:pieces]
+    gate_ref, up_ref, down_ref = refs[pieces : pieces + 3]
+    out_refs = refs[pieces + 3 + extra : 2 * pieces + 3 + extra]
+    x_all = refs[2 * pieces + 3 + extra]
+    piece = out_refs[0].shape[0]
+    for i in range(pieces):
+        x_all[i * piece : (i + 1) * piece, :] = x_refs[i][...]
+    x = x_all[...]
     gate = jnp.dot(x, gate_ref[...], preferred_element_type=jnp.float32)
     up = jnp.dot(x, up_ref[...], preferred_element_type=jnp.float32)
     inner = (gate / (1.0 + jnp.exp(-gate)) * up).astype(jnp.bfloat16)
-    part = jnp.dot(inner, down_ref[...], preferred_element_type=jnp.float32)
-
-    @pl.when(step == 0)
-    def _():
-        acc_ref[...] = part
-
-    @pl.when(jnp.logical_and(step > 0, step < pl.num_programs(0) - 1))
-    def _():
-        acc_ref[...] += part
-
-    @pl.when(step == pl.num_programs(0) - 1)
-    def _():
-        out_ref[...] = (acc_ref[...] + part).astype(out_ref.dtype)
-
-
-def expert(x, gate, up, down):
-    rows, width = x.shape
-    hidden = gate.shape[1]
-    tile = 256
-    steps = hidden // tile
+    part = jnp.dot(inner, down_ref[...], preferred_element_type=jnp.float32).astype(jnp.bfloat16)
+    for i in range(pieces):
+        out_refs[i][...] = part[i * piece : (i + 1) * piece]
+
+
+def expert(xs, gate, up, down, after=()):
+    width, hidden = gate.shape
+    pieces = len(xs)
+    piece = xs[0].shape[0]
+    rows = pieces * piece
+    vmem = pl.BlockSpec(memory_space=pltpu.VMEM)
     return pl.pallas_call(
-        expert_kernel,
-        grid=(steps,),
-        in_specs=[
-            pl.BlockSpec((rows, width), lambda j: (0, 0)),
-            pl.BlockSpec((width, tile), lambda j: (0, j)),
-            pl.BlockSpec((width, tile), lambda j: (0, j)),
-            pl.BlockSpec((tile, width), lambda j: (j, 0)),
-        ],
-        out_specs=pl.BlockSpec((rows, width), lambda j: (0, 0)),
-        out_shape=jax.ShapeDtypeStruct((rows, width), jnp.bfloat16),
-        scratch_shapes=[pltpu.VMEM((rows, width), jnp.float32)],
-        compiler_params=pltpu.CompilerParams(vmem_limit_bytes=56 * 1024 * 1024),
+        lambda *refs: expert_kernel(pieces, len(after), *refs),
+        in_specs=[vmem] * (pieces + 3) + [pl.BlockSpec(memory_space=pl.ANY)] * len(after),
+        out_specs=[vmem] * pieces,
+        out_shape=[jax.ShapeDtypeStruct((piece, width), jnp.bfloat16)] * pieces,
+        scratch_shapes=[pltpu.VMEM((rows, width), jnp.bfloat16)],
+        compiler_params=pltpu.CompilerParams(vmem_limit_bytes=40 * 1024 * 1024),
         cost_estimate=pl.CostEstimate(
             flops=6 * rows * width * hidden,
             bytes_accessed=6 * width * hidden + 4 * rows * width,
             transcendentals=rows * hidden,
         ),
-    )(x, gate, up, down)
+    )(*xs, gate, up, down, *after)
 
 
 def per_device(
@@ -220,35 +222,42 @@
     )
     per_z = 2 * CAP
     sent = dealt([send_rows[d * per_z : (d + 1) * per_z] for d in range(SIDE)], z_axis, 1)
-    column_rows = jnp.concatenate([r[:CAP] for r in sent] + [r[CAP:] for r in sent], axis=0)
     n1 = SIDE * CAP
+    order = [k * per_z + part * CAP + i for part in range(2) for k in range(SIDE) for i in range(CAP)]
+    reorder = jnp.asarray(np.eye(2 * n1)[order], jnp.bfloat16)
+    column_rows = jnp.dot(
+        reorder, jnp.concatenate(sent, axis=0), preferred_element_type=jnp.float32
+    ).astype(jnp.bfloat16)
     line = gathered(column_rows, first_axis)
-    line = jnp.concatenate([r[:n1] for r in line] + [r[n1:] for r in line], axis=0)
+    own = jnp.concatenate([r[:n1] for r in line], axis=0)
+    other = jnp.concatenate([r[n1:] for r in line], axis=0)
+    mine, theirs = {0: own}, {0: sibling(other)}
+    for d in (1, -1):
+        mine[d] = lax.ppermute(own, BOTH, second_axis(d))
+        theirs[d] = lax.ppermute(other, BOTH, crossed(d))
+    mine[2] = lax.ppermute(mine[1], BOTH, second_axis(1))
+    theirs[2] = lax.ppermute(theirs[-1], BOTH, first_axis(-1))
+    weights = (gate_proj[0], up_proj[0], down_proj[0])
+    sides = expert([mine[1], theirs[1], mine[-1], theirs[-1]], *weights)
+    own, other = [], []
+    for d, pair in ((1, sides[:2]), (-1, sides[2:])):
+        own.append(lax.ppermute(pair[0], BOTH, second_axis(-d)))
+        other.append(lax.ppermute(pair[1], BOTH, uncrossed(d)))
+    far = expert([mine[2], theirs[2]], *weights, after=(sides[0],))
+    own.append(lax.ppermute(far[0], BOTH, second_axis(-2)))
+    other.append(lax.ppermute(far[1], BOTH, uncrossed(2)))
+    near = expert([mine[0], theirs[0]], *weights, after=(far[0],))
+    own.append(near[0])
+    other.append(sibling(near[1]))
+    line = jnp.concatenate([added(own), added(other)], axis=0).astype(jnp.bfloat16)
     n2 = SIDE * n1
-    plane = gathered(line, second_axis)
-    mine = [r[:n2] for r in plane]
-    theirs = sibling(jnp.concatenate([r[n2:] for r in plane], axis=0))
-    rows_in = jnp.concatenate(mine + [theirs], axis=0)
-    rows_out = expert(rows_in, gate_proj[0], up_proj[0], down_proj[0])
-    n3 = SIDE * n2
-    swapped = sibling(rows_out[n3:])
-    plane = [
-        jnp.concatenate([rows_out[d * n2 : (d + 1) * n2], swapped[d * n2 : (d + 1) * n2]], axis=0)
-        for d in range(SIDE)
-    ]
-    line = added(dealt(plane, second_axis, -1)).astype(jnp.bfloat16)
     line = [
         jnp.concatenate([line[d * n1 : (d + 1) * n1], line[n2 + d * n1 : n2 + (d + 1) * n1]], axis=0)
         for d in range(SIDE)
     ]
     column_rows = added(dealt(line, first_axis, -1)).astype(jnp.bfloat16)
-    sent = [
-        jnp.concatenate(
-            [column_rows[d * CAP : (d + 1) * CAP], column_rows[n1 + d * CAP : n1 + (d + 1) * CAP]],
-            axis=0,
-        )
-        for d in range(SIDE)
-    ]
+    sent = jnp.dot(reorder.T, column_rows, preferred_element_type=jnp.float32).astype(jnp.bfloat16)
+    sent = [sent[d * per_z : (d + 1) * per_z] for d in range(SIDE)]
     expert_rows = jnp.concatenate(dealt(sent, z_axis, -1), axis=0)
     picked = jnp.dot(match_table, expert_rows, preferred_element_type=jnp.float32).reshape(
         token_count, 2, -1

time: 246 us -> 174 us (0.71)
  waiting for transfers between devices: 127 us -> 70.3 us
  local copies, waits for them, and re-layouts: 43.6 us -> 8.23 us
  starting transfers between devices: 45.8 us -> 61.3 us
  Pallas kernels: 19.1 us -> 24.4 us
    ppermute x12 -> x9, waiting for transfers between devices: 64.1 us -> 23 us  [gathered(): got[d] = lax.ppermute(shard, BOTH, along(d))]
    concatenate x5 -> x0, local copies, waits for them, and re-layouts: 30.9 us -> none  [the longest x1 20.2 us: per_device(): rows_in = jnp.concatenate(mine + [theirs], axis=0)]
    ppermute x15 -> x12, waiting for transfers between devices: 45.6 us -> 22.9 us  [dealt(): got[d] = lax.ppermute(blocks[d], BOTH, along(sign * d))]
    ppermute x0 -> x12, starting transfers between devices: none -> 16.8 us  [the longest x1 3.84 us: per_device(): theirs[2] = lax.ppermute(theirs[-1], BOTH, first_axis(-1))]
    ppermute x0 -> x12, waiting for transfers between devices: none -> 15.9 us  [the longest x2 7.74 us: per_device(): theirs[d] = lax.ppermute(other, BOTH, crossed(d))]
    ppermute x4, waiting for transfers between devices: 8.51 us -> 0.87 us  [sibling(): return lax.ppermute(shard, BOTH, pairs)]
    pallas_call x1 -> x3, Pallas kernels: 19.1 us -> 24.4 us  [expert(): pl.pallas_call(lambda *refs: expert_kernel(pieces, len(after), *refs), in...]
    slice x14 -> x6, local copies, waits for them, and re-layouts: 5.2 us -> 0.13 us  [the longest x4 0.07 us: per_device(): other = jnp.concatenate([r[n1:] for r in line], axis=0)]
  transfers between devices with their start and end apart: 35 -> 41, of which waited for: 29 -> 24; matrix products, arithmetic and copies ran while one was open for 3% -> 3% of each run, Pallas kernels for 0% -> 14%
where the time goes in v2:
time: 174 us
  waiting for transfers between devices  70.3 us (40%)
  starting transfers between devices  61.3 us (35%)
  Pallas kernels  24.4 us (14%)
  local copies, waits for them, and re-layouts  8.23 us (5%)
  other arithmetic  3.39 us (2%)
  between operations  3.1 us (2%)
  matrix products  2.93 us (2%)
    pallas_call x3, Pallas kernels, expert(): pl.pallas_call(lambda *refs: expert_kernel(pieces, len(after), *refs), in...  24.4 us
    ppermute x9, waiting for transfers between devices, gathered(): got[d] = lax.ppermute(shard, BOTH, along(d))  23 us
    ppermute x12, waiting for transfers between devices, dealt(): got[d] = lax.ppermute(blocks[d], BOTH, along(sign * d))  22.9 us
    ppermute x12, starting transfers between devices, dealt(): got[d] = lax.ppermute(blocks[d], BOTH, along(sign * d))  15.8 us
    ppermute x9, starting transfers between devices, gathered(): got[d] = lax.ppermute(shard, BOTH, along(d))  13.5 us
    ppermute x2, waiting for transfers between devices, per_device(): theirs[d] = lax.ppermute(other, BOTH, crossed(d))  7.74 us
    all_to_all x1, waiting for transfers between devices, per_device(): owned = lax.all_to_all(slab, 'ctx', split_axis=0, concat_axis=0, tiled=True)  7.59 us
    ppermute x3, starting transfers between devices, per_device(): collected.append(lax.ppermute(packed, 'ctx', pairs))  6.84 us
  transfers between devices with their start and end apart: 41, of which 24 were waited for; matrix products, arithmetic and copies ran while one was open for 3% of the time, Pallas kernels for 14%

profile of v2, /device:TPU:0, one launch (start us, length us, event | category | flops | bytes accessed | tf_op | source)
XLA Modules:
  0.0 173.6 jit_solution(13208707270750053092)
XLA Ops:
  3.1 2.9 %collective-permute-start.1 = (bf16[64,256]{1,0:T(8,128)(2,1)S(1)}, bf16[64,256]{1,0:T(8,128)(2,1)S(1)}, u32[]{:S(2)}, u32[]{:S(2)}) collective-permute-start(bf16[64,256]{1,0:T(8,128)(2,1)S(1)} %constant_dynamic-update-slice_fusion), channel_id=1, source_target_pairs={{0,16},{8,24},{16,32},{24,40},{32,48},{40,56},{48,64},{56,72},{64,... | collective-permute-start | bytes 98312 | tf_op jit(solution)/shard_map/ppermute | solution.py:158
  6.0 2.3 %collective-permute-start.2 = (bf16[64,256]{1,0:T(8,128)(2,1)S(1)}, bf16[64,256]{1,0:T(8,128)(2,1)S(1)}, u32[]{:S(2)}, u32[]{:S(2)}) collective-permute-start(bf16[64,256]{1,0:T(8,128)(2,1)S(1)} %constant_dynamic-update-slice_fusion), channel_id=1, source_target_pairs={{0,24},{8,32},{16,40},{24,48},{32,56},{40,64},{48,72},{56,80},{64,... | collective-permute-start | bytes 98312 | tf_op jit(solution)/shard_map/ppermute | solution.py:158
  20.4 3.5 %collective-permute-done.4 = bf16[32,2048]{1,0:T(8,128)(2,1)S(1)} collective-permute-done((bf16[32,2048]{1,0:T(8,128)(2,1)S(1)}, bf16[32,2048]{1,0:T(8,128)(2,1)S(1)}, u32[]{:S(2)}, u32[]{:S(2)}) %collective-permute-start.4) | collective-permute-done | bytes 131104 | tf_op jit(solution)/shard_map/ppermute | solution.py:69
  26.4 1.7 collective-permute-start.8
  28.1 2.2 %collective-permute-start.9 = (bf16[128,2048]{1,0:T(8,128)(2,1)S(1)}, bf16[128,2048]{1,0:T(8,128)(2,1)S(1)}, u32[]{:S(2)}, u32[]{:S(2)}) collective-permute-start(bf16[128,2048]{1,0:T(8,128)(2,1)S(1)} %pad_maximum_fusion), channel_id=1, source_target_pairs={{0,96},{1,25},{2,98},{3,27},{4,100},{5,29},{6,102},{7,31},{8,104},... | collective-permute-start | bytes 1572872 | tf_op jit(solution)/shard_map/ppermute | solution.py:69
  30.4 4.9 %collective-permute-done.7 = bf16[128,2048]{1,0:T(8,128)(2,1)S(1)} collective-permute-done((bf16[128,2048]{1,0:T(8,128)(2,1)S(1)}, bf16[128,2048]{1,0:T(8,128)(2,1)S(1)}, u32[]{:S(2)}, u32[]{:S(2)}) %collective-permute-start.7) | collective-permute-done | bytes 524320 | tf_op jit(solution)/shard_map/ppermute | solution.py:69
  35.3 5.6 %collective-permute-done.8 = bf16[128,2048]{1,0:T(8,128)(2,1)S(1)} collective-permute-done((bf16[128,2048]{1,0:T(8,128)(2,1)S(1)}, bf16[128,2048]{1,0:T(8,128)(2,1)S(1)}, u32[]{:S(2)}, u32[]{:S(2)}) %collective-permute-start.8) | collective-permute-done | bytes 524320 | tf_op jit(solution)/shard_map/ppermute | solution.py:69
  42.8 2.0 %collective-permute-start.11 = (bf16[16,8,256]{2,1,0:T(8,128)(2,1)S(1)}, bf16[16,8,256]{2,1,0:T(8,128)(2,1)S(1)}, u32[]{:S(2)}, u32[]{:S(2)}) collective-permute-start(bf16[16,8,256]{2,1,0:T(8,128)(2,1)S(1)} %get-tuple-element.50), channel_id=1, source_target_pairs={{0,2},{1,3},{2,4},{3,5},{4,6},{5,7},{6,0},{7,1},{8,10},{9,11},{10,... | collective-permute-start | bytes 196616 | tf_op jit(solution)/shard_map/ppermute | solution.py:76
  44.8 3.6 %collective-permute-start.12 = (bf16[16,8,256]{2,1,0:T(8,128)(2,1)S(1)}, bf16[16,8,256]{2,1,0:T(8,128)(2,1)S(1)}, u32[]{:S(2)}, u32[]{:S(2)}) collective-permute-start(bf16[16,8,256]{2,1,0:T(8,128)(2,1)S(1)} %get-tuple-element.52), channel_id=1, source_target_pairs={{0,4},{1,5},{2,6},{3,7},{4,0},{5,1},{6,2},{7,3},{8,12},{9,13},{10,... | collective-permute-start | bytes 196616 | tf_op jit(solution)/shard_map/ppermute | solution.py:76
  49.4 1.9 %collective-permute-done.12 = bf16[16,8,256]{2,1,0:T(8,128)(2,1)S(1)} collective-permute-done((bf16[16,8,256]{2,1,0:T(8,128)(2,1)S(1)}, bf16[16,8,256]{2,1,0:T(8,128)(2,1)S(1)}, u32[]{:S(2)}, u32[]{:S(2)}) %collective-permute-start.12) | collective-permute-done | bytes 65568 | tf_op jit(solution)/shard_map/ppermute | solution.py:76
  54.0 6.1 %all-to-all-start = ((bf16[16,8,256]{2,1,0:T(8,128)(2,1)}), bf16[16,8,256]{2,1,0:T(8,128)(2,1)S(1)}, u32[]{:S(2)}, u32[]{:S(2)}) async-start(bf16[16,8,256]{2,1,0:T(8,128)(2,1)} %broadcast_select_fusion), calls=%async_computation | async-start | bytes 131072 | tf_op jit(solution)/shard_map/all_to_all | solution.py:200
  60.2 7.6 %all-to-all-done = bf16[16,8,256]{2,1,0:T(8,128)(2,1)S(1)} async-done(((bf16[16,8,256]{2,1,0:T(8,128)(2,1)}), bf16[16,8,256]{2,1,0:T(8,128)(2,1)S(1)}, u32[]{:S(2)}, u32[]{:S(2)}) %all-to-all-start) | async-done | bytes 65568 | tf_op jit(solution)/shard_map/all_to_all | solution.py:200
  68.7 3.1 %collective-permute-start.16 = (bf16[8,4096]{1,0:T(8,128)(2,1)S(1)}, bf16[8,4096]{1,0:T(8,128)(2,1)S(1)}, u32[]{:S(2)}, u32[]{:S(2)}) collective-permute-start(bf16[8,4096]{1,0:T(8,128)(2,1)S(1)} %get-tuple-element.48), channel_id=1, source_target_pairs={{0,6},{1,7},{2,0},{3,1},{4,2},{5,3},{6,4},{7,5},{8,14},{9,15},{10,... | collective-permute-start | bytes 196616 | tf_op jit(solution)/shard_map/ppermute | solution.py:76
  74.3 3.4 %collective-permute-done.15 = bf16[8,4096]{1,0:T(8,128)(2,1)S(1)} collective-permute-done((bf16[8,4096]{1,0:T(8,128)(2,1)S(1)}, bf16[8,4096]{1,0:T(8,128)(2,1)S(1)}, u32[]{:S(2)}, u32[]{:S(2)}) %collective-permute-start.15) | collective-permute-done | bytes 65568 | tf_op jit(solution)/shard_map/ppermute | solution.py:76
  78.5 2.2 %collective-permute-start.18 = (bf16[32,4096]{1,0:T(8,128)(2,1)S(1)}, bf16[32,4096]{1,0:T(8,128)(2,1)S(1)}, u32[]{:S(2)}, u32[]{:S(2)}) collective-permute-start(bf16[32,4096]{1,0:T(8,128)(2,1)S(1)} %fusion.3), channel_id=1, source_target_pairs={{0,16},{1,65},{2,18},{3,67},{4,20},{5,69},{6,22},{7,71},{8,24},{9,... | collective-permute-start | bytes 786440 | tf_op jit(solution)/shard_map/ppermute | solution.py:69
  81.9 6.4 %collective-permute-done.17 = bf16[32,4096]{1,0:T(8,128)(2,1)S(1)} collective-permute-done((bf16[32,4096]{1,0:T(8,128)(2,1)S(1)}, bf16[32,4096]{1,0:T(8,128)(2,1)S(1)}, u32[]{:S(2)}, u32[]{:S(2)}) %collective-permute-start.17) | collective-permute-done | bytes 262176 | tf_op jit(solution)/shard_map/ppermute | solution.py:69
  90.0 2.4 %collective-permute-start.21 = (bf16[64,4096]{1,0:T(8,128)(2,1)S(1)}, bf16[64,4096]{1,0:T(8,128)(2,1)S(1)}, u32[]{:S(2)}, u32[]{:S(2)}) collective-permute-start(bf16[64,4096]{1,0:T(8,128)(2,1)S(1)} %pad_maximum_fusion.2), channel_id=1, source_target_pairs={{0,33},{1,8},{2,35},{3,10},{4,37},{5,12},{6,39},{7,14},{8,41},{9,1... | collective-permute-start | bytes 1572872 | tf_op jit(solution)/shard_map/ppermute | solution.py:237
  92.4 2.7 %collective-permute-start.22 = (bf16[64,4096]{1,0:T(8,128)(2,1)S(1)}, bf16[64,4096]{1,0:T(8,128)(2,1)S(1)}, u32[]{:S(2)}, u32[]{:S(2)}) collective-permute-start(bf16[64,4096]{1,0:T(8,128)(2,1)S(1)} %pad_maximum_fusion.1.refs_0_), channel_id=1, source_target_pairs={{0,96},{1,25},{2,98},{3,27},{4,100},{5,29},{6,102},{7,31},{8,104},... | collective-permute-start | bytes 1572872 | tf_op jit(solution)/shard_map/ppermute | solution.py:236
  95.1 2.8 %collective-permute-done.23.refs_3_ = bf16[64,4096]{1,0:T(8,128)(2,1)S(1)} collective-permute-done((bf16[64,4096]{1,0:T(8,128)(2,1)S(1)}, bf16[64,4096]{1,0:T(8,128)(2,1)S(1)}, u32[]{:S(2)}, u32[]{:S(2)}) %collective-permute-start.23) | collective-permute-done | bytes 524320 | tf_op jit(solution)/shard_map/ppermute | solution.py:237
  97.9 3.8 %collective-permute-start.27 = (bf16[64,4096]{1,0:T(8,128)(2,1)S(1)}, bf16[64,4096]{1,0:T(8,128)(2,1)S(1)}, u32[]{:S(2)}, u32[]{:S(2)}) collective-permute-start(bf16[64,4096]{1,0:T(8,128)(2,1)S(1)} %collective-permute-done.23.refs_3_), channel_id=1, source_target_pairs={{0,24},{1,97},{2,26},{3,99},{4,28},{5,101},{6,30},{7,103},{8,0},{9... | collective-permute-start | bytes 1572872 | tf_op jit(solution)/shard_map/ppermute | solution.py:239
  102.3 4.9 %collective-permute-done.21.refs_1_ = bf16[64,4096]{1,0:T(8,128)(2,1)S(1)} collective-permute-done((bf16[64,4096]{1,0:T(8,128)(2,1)S(1)}, bf16[64,4096]{1,0:T(8,128)(2,1)S(1)}, u32[]{:S(2)}, u32[]{:S(2)}) %collective-permute-start.21) | collective-permute-done | bytes 524320 | tf_op jit(solution)/shard_map/ppermute | solution.py:237
  107.2 2.8 %copy-done.1 = bf16[1,4096,768]{2,1,0:T(8,128)(2,1)S(1)} copy-done((bf16[1,4096,768]{2,1,0:T(8,128)(2,1)S(1)}, bf16[1,4096,768]{2,1,0:T(8,128)(2,1)}, u32[]{:S(2)}) %copy-start.1) | copy-done | bytes 6291480
  110.0 9.8 %shard_map.127 = (bf16[64,4096]{1,0:T(8,128)(2,1)S(1)}, bf16[64,4096]{1,0:T(8,128)(2,1)S(1)}, bf16[64,4096]{1,0:T(8,128)(2,1)S(1)}, bf16[64,4096]{1,0:T(8,128)(2,1)S(1)}) custom-call(bf16[64,4096]{1,0:T(8,128)(2,1)S(1)} %collective-permute-done.20.refs_0_, bf16[64,4096]{1,0:T(8,128)(2,1)S(1)} %collective-permute-done.21.refs_1_, ...), custom_call_target="tpu_custom_call" | custom-call | flops 4831838208 | bytes 23068672 | tf_op jit(solution)/shard_map/pallas_call | solution.py:110
  121.9 7.3 %shard_map.128 = (bf16[64,4096]{1,0:T(8,128)(2,1)S(1)}, bf16[64,4096]{1,0:T(8,128)(2,1)S(1)}) custom-call(bf16[64,4096]{1,0:T(8,128)(2,1)S(1)} %collective-permute-done.26.refs_0_, bf16[64,4096]{1,0:T(8,128)(2,1)S(1)} %collective-permute-done.27.refs_1_, bf16[4096,768]{1,0:T(8,128)(2,1)S(1)} %bitcast.108, bf16[4096,768]{1,0:T(8,128)(2,1)} %bitcast.111, ...), custom_call_target="tpu_custom_call" | custom-call | flops 2415919104 | bytes 20971520 | tf_op jit(solution)/shard_map/pallas_call | solution.py:110
  131.4 7.3 %shard_map.129 = (bf16[64,4096]{1,0:T(8,128)(2,1)S(1)}, bf16[64,4096]{1,0:T(8,128)(2,1)S(1)}) custom-call(bf16[64,4096]{1,0:T(8,128)(2,1)S(1)} %pad_maximum_fusion.1.refs_0_, bf16[64,4096]{1,0:T(8,128)(2,1)S(1)} %collective-permute-done.29.refs_1_, bf16[4096,768]{1,0:T(8,128)(2,1)S(1)} %bitcast.109, bf16[4096,768]{1,0:T(8,128)(2,1)} %bitcast.112, ...), custom_call_target="tpu_custom_call" | custom-call | flops 2415919104 | bytes 20971520 | tf_op jit(solution)/shard_map/pallas_call | solution.py:110
  140.3 2.5 %collective-permute-start.32 = (bf16[64,4096]{1,0:T(8,128)(2,1)S(1)}, bf16[64,4096]{1,0:T(8,128)(2,1)S(1)}, u32[]{:S(2)}, u32[]{:S(2)}) collective-permute-start(bf16[64,4096]{1,0:T(8,128)(2,1)S(1)} %get-tuple-element.19), channel_id=1, source_target_pairs={{65,0},{16,1},{67,2},{18,3},{69,4},{20,5},{71,6},{22,7},{73,8},{24... | collective-permute-start | bytes 1572872 | tf_op jit(solution)/shard_map/ppermute | solution.py:248
  145.6 5.6 %collective-permute-done.32 = bf16[64,4096]{1,0:T(8,128)(2,1)S(1)} collective-permute-done((bf16[64,4096]{1,0:T(8,128)(2,1)S(1)}, bf16[64,4096]{1,0:T(8,128)(2,1)S(1)}, u32[]{:S(2)}, u32[]{:S(2)}) %collective-permute-start.32) | collective-permute-done | bytes 524320 | tf_op jit(solution)/shard_map/ppermute | solution.py:248
  151.6 2.1 %collective-permute-start.34 = (bf16[32,4096]{1,0:T(8,128)(2,1)S(1)}, bf16[32,4096]{1,0:T(8,128)(2,1)S(1)}, u32[]{:S(2)}, u32[]{:S(2)}) collective-permute-start(bf16[32,4096]{1,0:T(8,128)(2,1)S(1)} %pad_maximum_fusion.3), channel_id=1, source_target_pairs={{0,24},{1,97},{2,26},{3,99},{4,28},{5,101},{6,30},{7,103},{8,0},{9... | collective-permute-start | bytes 786440 | tf_op jit(solution)/shard_map/ppermute | solution.py:76
  154.8 5.6 %collective-permute-done.34 = bf16[32,4096]{1,0:T(8,128)(2,1)S(1)} collective-permute-done((bf16[32,4096]{1,0:T(8,128)(2,1)S(1)}, bf16[32,4096]{1,0:T(8,128)(2,1)S(1)}, u32[]{:S(2)}, u32[]{:S(2)}) %collective-permute-start.34) | collective-permute-done | bytes 262176 | tf_op jit(solution)/shard_map/ppermute | solution.py:76
  161.8 2.5 %collective-permute-done.36 = bf16[32,4096]{1,0:T(8,128)(2,1)S(1)} collective-permute-done((bf16[32,4096]{1,0:T(8,128)(2,1)S(1)}, bf16[32,4096]{1,0:T(8,128)(2,1)S(1)}, u32[]{:S(2)}, u32[]{:S(2)}) %collective-permute-start.36) | collective-permute-done | bytes 262176 | tf_op jit(solution)/shard_map/ppermute | solution.py:76
  166.8 2.2 %collective-permute-done.37 = bf16[8,4096]{1,0:T(8,128)(2,1)S(1)} collective-permute-done((bf16[8,4096]{1,0:T(8,128)(2,1)S(1)}, bf16[8,4096]{1,0:T(8,128)(2,1)S(1)}, u32[]{:S(2)}, u32[]{:S(2)}) %collective-permute-start.37) | collective-permute-done | bytes 65568 | tf_op jit(solution)/shard_map/ppermute | solution.py:76
  169.0 2.6 %collective-permute-done.38 = bf16[8,4096]{1,0:T(8,128)(2,1)S(1)} collective-permute-done((bf16[8,4096]{1,0:T(8,128)(2,1)S(1)}, bf16[8,4096]{1,0:T(8,128)(2,1)S(1)}, u32[]{:S(2)}, u32[]{:S(2)}) %collective-permute-start.38) | collective-permute-done | bytes 65568 | tf_op jit(solution)/shard_map/ppermute | solution.py:76
  (150 shorter events, 44.2 us)
Async XLA Ops:
  1.5 12.1 %collective-permute-start = (bf16[64,256]{1,0:T(8,128)(2,1)S(1)}, bf16[64,256]{1,0:T(8,128)(2,1)S(1)}, u32[]{:S(2)}, u32[]{:S(2)}) collective-permute-start(bf16[64,256]{1,0:T(8,128)(2,1)S(1)} %constant_dynamic-update-slice_fusion), channel_id=1, source_target_pairs={{0,8},{8,16},{16,24},{24,32},{32,40},{40,48},{48,56},{56,64},{64,7... | collective-permute-start | bytes 98312 | tf_op jit(solution)/shard_map/ppermute | solution.py:158
  3.1 10.4 %collective-permute-start.1 = (bf16[64,256]{1,0:T(8,128)(2,1)S(1)}, bf16[64,256]{1,0:T(8,128)(2,1)S(1)}, u32[]{:S(2)}, u32[]{:S(2)}) collective-permute-start(bf16[64,256]{1,0:T(8,128)(2,1)S(1)} %constant_dynamic-update-slice_fusion), channel_id=1, source_target_pairs={{0,16},{8,24},{16,32},{24,40},{32,48},{40,56},{48,64},{56,72},{64,... | collective-permute-start | bytes 98312 | tf_op jit(solution)/shard_map/ppermute | solution.py:158
  6.0 7.5 %collective-permute-start.2 = (bf16[64,256]{1,0:T(8,128)(2,1)S(1)}, bf16[64,256]{1,0:T(8,128)(2,1)S(1)}, u32[]{:S(2)}, u32[]{:S(2)}) collective-permute-start(bf16[64,256]{1,0:T(8,128)(2,1)S(1)} %constant_dynamic-update-slice_fusion), channel_id=1, source_target_pairs={{0,24},{8,32},{16,40},{24,48},{32,56},{40,64},{48,72},{56,80},{64,... | collective-permute-start | bytes 98312 | tf_op jit(solution)/shard_map/ppermute | solution.py:158
  8.3 33.5 %collective-permute-start.10 = (bf16[1024,256]{1,0:T(8,128)(2,1)}, bf16[1024,256]{1,0:T(8,128)(2,1)S(1)}, u32[]{:S(2)}, u32[]{:S(2)}) collective-permute-start(bf16[1024,256]{1,0:T(8,128)(2,1)} %param.18), channel_id=1, source_target_pairs={{0,1},{1,0},{2,3},{3,2},{4,5},{5,4},{6,7},{7,6},{8,9},{9,8},{10,11... | collective-permute-start | bytes 1572872 | tf_op jit(solution)/shard_map/ppermute | solution.py:63
  16.3 7.7 %collective-permute-start.4 = (bf16[32,2048]{1,0:T(8,128)(2,1)S(1)}, bf16[32,2048]{1,0:T(8,128)(2,1)S(1)}, u32[]{:S(2)}, u32[]{:S(2)}) collective-permute-start(bf16[32,2048]{1,0:T(8,128)(2,1)S(1)} %get-tuple-element.53), channel_id=1, source_target_pairs={{0,8},{1,33},{2,10},{3,35},{4,12},{5,37},{6,14},{7,39},{8,16},{9,4... | collective-permute-start | bytes 393224 | tf_op jit(solution)/shard_map/ppermute | solution.py:69
  17.0 6.9 %collective-permute-start.5 = (bf16[32,2048]{1,0:T(8,128)(2,1)S(1)}, bf16[32,2048]{1,0:T(8,128)(2,1)S(1)}, u32[]{:S(2)}, u32[]{:S(2)}) collective-permute-start(bf16[32,2048]{1,0:T(8,128)(2,1)S(1)} %get-tuple-element.53), channel_id=1, source_target_pairs={{0,16},{1,65},{2,18},{3,67},{4,20},{5,69},{6,22},{7,71},{8,24},{9,... | collective-permute-start | bytes 393224 | tf_op jit(solution)/shard_map/ppermute | solution.py:69
  24.8 10.5 %collective-permute-start.7 = (bf16[128,2048]{1,0:T(8,128)(2,1)S(1)}, bf16[128,2048]{1,0:T(8,128)(2,1)S(1)}, u32[]{:S(2)}, u32[]{:S(2)}) collective-permute-start(bf16[128,2048]{1,0:T(8,128)(2,1)S(1)} %pad_maximum_fusion), channel_id=1, source_target_pairs={{0,32},{1,9},{2,34},{3,11},{4,36},{5,13},{6,38},{7,15},{8,40},{9,1... | collective-permute-start | bytes 1572872 | tf_op jit(solution)/shard_map/ppermute | solution.py:69
  26.4 14.5 %collective-permute-start.8 = (bf16[128,2048]{1,0:T(8,128)(2,1)S(1)}, bf16[128,2048]{1,0:T(8,128)(2,1)S(1)}, u32[]{:S(2)}, u32[]{:S(2)}) collective-permute-start(bf16[128,2048]{1,0:T(8,128)(2,1)S(1)} %pad_maximum_fusion), channel_id=1, source_target_pairs={{0,64},{1,17},{2,66},{3,19},{4,68},{5,21},{6,70},{7,23},{8,72},{9,... | collective-permute-start | bytes 1572872 | tf_op jit(solution)/shard_map/ppermute | solution.py:69
  28.1 13.7 %collective-permute-start.9 = (bf16[128,2048]{1,0:T(8,128)(2,1)S(1)}, bf16[128,2048]{1,0:T(8,128)(2,1)S(1)}, u32[]{:S(2)}, u32[]{:S(2)}) collective-permute-start(bf16[128,2048]{1,0:T(8,128)(2,1)S(1)} %pad_maximum_fusion), channel_id=1, source_target_pairs={{0,96},{1,25},{2,98},{3,27},{4,100},{5,29},{6,102},{7,31},{8,104},... | collective-permute-start | bytes 1572872 | tf_op jit(solution)/shard_map/ppermute | solution.py:69
  42.8 6.6 %collective-permute-start.11 = (bf16[16,8,256]{2,1,0:T(8,128)(2,1)S(1)}, bf16[16,8,256]{2,1,0:T(8,128)(2,1)S(1)}, u32[]{:S(2)}, u32[]{:S(2)}) collective-permute-start(bf16[16,8,256]{2,1,0:T(8,128)(2,1)S(1)} %get-tuple-element.50), channel_id=1, source_target_pairs={{0,2},{1,3},{2,4},{3,5},{4,6},{5,7},{6,0},{7,1},{8,10},{9,11},{10,... | collective-permute-start | bytes 196616 | tf_op jit(solution)/shard_map/ppermute | solution.py:76
  44.8 6.5 %collective-permute-start.12 = (bf16[16,8,256]{2,1,0:T(8,128)(2,1)S(1)}, bf16[16,8,256]{2,1,0:T(8,128)(2,1)S(1)}, u32[]{:S(2)}, u32[]{:S(2)}) collective-permute-start(bf16[16,8,256]{2,1,0:T(8,128)(2,1)S(1)} %get-tuple-element.52), channel_id=1, source_target_pairs={{0,4},{1,5},{2,6},{3,7},{4,0},{5,1},{6,2},{7,3},{8,12},{9,13},{10,... | collective-permute-start | bytes 196616 | tf_op jit(solution)/shard_map/ppermute | solution.py:76
  54.0 13.8 %all-to-all-start = ((bf16[16,8,256]{2,1,0:T(8,128)(2,1)}), bf16[16,8,256]{2,1,0:T(8,128)(2,1)S(1)}, u32[]{:S(2)}, u32[]{:S(2)}) async-start(bf16[16,8,256]{2,1,0:T(8,128)(2,1)} %broadcast_select_fusion), calls=%async_computation | async-start | bytes 131072 | tf_op jit(solution)/shard_map/all_to_all | solution.py:200
  77.8 10.5 %collective-permute-start.17 = (bf16[32,4096]{1,0:T(8,128)(2,1)S(1)}, bf16[32,4096]{1,0:T(8,128)(2,1)S(1)}, u32[]{:S(2)}, u32[]{:S(2)}) collective-permute-start(bf16[32,4096]{1,0:T(8,128)(2,1)S(1)} %fusion.3), channel_id=1, source_target_pairs={{0,8},{1,33},{2,10},{3,35},{4,12},{5,37},{6,14},{7,39},{8,16},{9,4... | collective-permute-start | bytes 786440 | tf_op jit(solution)/shard_map/ppermute | solution.py:69
  78.5 9.9 %collective-permute-start.18 = (bf16[32,4096]{1,0:T(8,128)(2,1)S(1)}, bf16[32,4096]{1,0:T(8,128)(2,1)S(1)}, u32[]{:S(2)}, u32[]{:S(2)}) collective-permute-start(bf16[32,4096]{1,0:T(8,128)(2,1)S(1)} %fusion.3), channel_id=1, source_target_pairs={{0,16},{1,65},{2,18},{3,67},{4,20},{5,69},{6,22},{7,71},{8,24},{9,... | collective-permute-start | bytes 786440 | tf_op jit(solution)/shard_map/ppermute | solution.py:69
  80.6 8.6 %collective-permute-start.19 = (bf16[32,4096]{1,0:T(8,128)(2,1)S(1)}, bf16[32,4096]{1,0:T(8,128)(2,1)S(1)}, u32[]{:S(2)}, u32[]{:S(2)}) collective-permute-start(bf16[32,4096]{1,0:T(8,128)(2,1)S(1)} %fusion.3), channel_id=1, source_target_pairs={{0,24},{1,97},{2,26},{3,99},{4,28},{5,101},{6,30},{7,103},{8,0},{9... | collective-permute-start | bytes 786440 | tf_op jit(solution)/shard_map/ppermute | solution.py:69
  89.3 8.7 %collective-permute-start.23 = (bf16[64,4096]{1,0:T(8,128)(2,1)S(1)}, bf16[64,4096]{1,0:T(8,128)(2,1)S(1)}, u32[]{:S(2)}, u32[]{:S(2)}) collective-permute-start(bf16[64,4096]{1,0:T(8,128)(2,1)S(1)} %pad_maximum_fusion.2), channel_id=1, source_target_pairs={{0,97},{1,24},{2,99},{3,26},{4,101},{5,28},{6,103},{7,30},{8,105},... | collective-permute-start | bytes 1572872 | tf_op jit(solution)/shard_map/ppermute | solution.py:237
  89.4 12.4 %collective-permute-start.20 = (bf16[64,4096]{1,0:T(8,128)(2,1)S(1)}, bf16[64,4096]{1,0:T(8,128)(2,1)S(1)}, u32[]{:S(2)}, u32[]{:S(2)}) collective-permute-start(bf16[64,4096]{1,0:T(8,128)(2,1)S(1)} %pad_maximum_fusion.1.refs_0_), channel_id=1, source_target_pairs={{0,32},{1,9},{2,34},{3,11},{4,36},{5,13},{6,38},{7,15},{8,40},{9,1... | collective-permute-start | bytes 1572872 | tf_op jit(solution)/shard_map/ppermute | solution.py:236
  90.0 17.2 %collective-permute-start.21 = (bf16[64,4096]{1,0:T(8,128)(2,1)S(1)}, bf16[64,4096]{1,0:T(8,128)(2,1)S(1)}, u32[]{:S(2)}, u32[]{:S(2)}) collective-permute-start(bf16[64,4096]{1,0:T(8,128)(2,1)S(1)} %pad_maximum_fusion.2), channel_id=1, source_target_pairs={{0,33},{1,8},{2,35},{3,10},{4,37},{5,12},{6,39},{7,14},{8,41},{9,1... | collective-permute-start | bytes 1572872 | tf_op jit(solution)/shard_map/ppermute | solution.py:237
  92.4 14.8 %collective-permute-start.22 = (bf16[64,4096]{1,0:T(8,128)(2,1)S(1)}, bf16[64,4096]{1,0:T(8,128)(2,1)S(1)}, u32[]{:S(2)}, u32[]{:S(2)}) collective-permute-start(bf16[64,4096]{1,0:T(8,128)(2,1)S(1)} %pad_maximum_fusion.1.refs_0_), channel_id=1, source_target_pairs={{0,96},{1,25},{2,98},{3,27},{4,100},{5,29},{6,102},{7,31},{8,104},... | collective-permute-start | bytes 1572872 | tf_op jit(solution)/shard_map/ppermute | solution.py:236
  97.9 24.0 %collective-permute-start.27 = (bf16[64,4096]{1,0:T(8,128)(2,1)S(1)}, bf16[64,4096]{1,0:T(8,128)(2,1)S(1)}, u32[]{:S(2)}, u32[]{:S(2)}) collective-permute-start(bf16[64,4096]{1,0:T(8,128)(2,1)S(1)} %collective-permute-done.23.refs_3_), channel_id=1, source_target_pairs={{0,24},{1,97},{2,26},{3,99},{4,28},{5,101},{6,30},{7,103},{8,0},{9... | collective-permute-start | bytes 1572872 | tf_op jit(solution)/shard_map/ppermute | solution.py:239
  101.8 20.1 %collective-permute-start.26 = (bf16[64,4096]{1,0:T(8,128)(2,1)S(1)}, bf16[64,4096]{1,0:T(8,128)(2,1)S(1)}, u32[]{:S(2)}, u32[]{:S(2)}) collective-permute-start(bf16[64,4096]{1,0:T(8,128)(2,1)S(1)} %collective-permute-done.20.refs_0_), channel_id=1, source_target_pairs={{0,32},{1,9},{2,34},{3,11},{4,36},{5,13},{6,38},{7,15},{8,40},{9,1... | collective-permute-start | bytes 1572872 | tf_op jit(solution)/shard_map/ppermute | solution.py:238
  102.3 28.4 %collective-permute-start.29 = (bf16[64,4096]{1,0:T(8,128)(2,1)S(1)}, bf16[64,4096]{1,0:T(8,128)(2,1)S(1)}, u32[]{:S(2)}, u32[]{:S(2)}) collective-permute-start(bf16[64,4096]{1,0:T(8,128)(2,1)S(1)} %pad_maximum_fusion.2), channel_id=1, source_target_pairs={{0,1},{1,0},{2,3},{3,2},{4,5},{5,4},{6,7},{7,6},{8,9},{9,8},{10,11... | collective-permute-start | bytes 1572872 | tf_op jit(solution)/shard_map/ppermute | solution.py:63
  119.8 18.9 %collective-permute-start.24 = (bf16[64,4096]{1,0:T(8,128)(2,1)S(1)}, bf16[64,4096]{1,0:T(8,128)(2,1)S(1)}, u32[]{:S(2)}, u32[]{:S(2)}) collective-permute-start(bf16[64,4096]{1,0:T(8,128)(2,1)S(1)} %get-tuple-element.13.refs_5_), channel_id=1, source_target_pairs={{0,96},{1,25},{2,98},{3,27},{4,100},{5,29},{6,102},{7,31},{8,104},... | collective-permute-start | bytes 1572872 | tf_op jit(solution)/shard_map/ppermute | solution.py:244
  121.0 19.3 %collective-permute-start.25 = (bf16[64,4096]{1,0:T(8,128)(2,1)S(1)}, bf16[64,4096]{1,0:T(8,128)(2,1)S(1)}, u32[]{:S(2)}, u32[]{:S(2)}) collective-permute-start(bf16[64,4096]{1,0:T(8,128)(2,1)S(1)} %get-tuple-element.14), channel_id=1, source_target_pairs={{0,32},{1,9},{2,34},{3,11},{4,36},{5,13},{6,38},{7,15},{8,40},{9,1... | collective-permute-start | bytes 1572872 | tf_op jit(solution)/shard_map/ppermute | solution.py:244
  129.2 15.2 %collective-permute-start.28 = (bf16[64,4096]{1,0:T(8,128)(2,1)S(1)}, bf16[64,4096]{1,0:T(8,128)(2,1)S(1)}, u32[]{:S(2)}, u32[]{:S(2)}) collective-permute-start(bf16[64,4096]{1,0:T(8,128)(2,1)S(1)} %get-tuple-element.15.refs_5_), channel_id=1, source_target_pairs={{0,64},{1,17},{2,66},{3,19},{4,68},{5,21},{6,70},{7,23},{8,72},{9,... | collective-permute-start | bytes 1572872 | tf_op jit(solution)/shard_map/ppermute | solution.py:247
  130.5 14.2 %collective-permute-start.30 = (bf16[64,4096]{1,0:T(8,128)(2,1)S(1)}, bf16[64,4096]{1,0:T(8,128)(2,1)S(1)}, u32[]{:S(2)}, u32[]{:S(2)}) collective-permute-start(bf16[64,4096]{1,0:T(8,128)(2,1)S(1)} %get-tuple-element.17), channel_id=1, source_target_pairs={{33,0},{8,1},{35,2},{10,3},{37,4},{12,5},{39,6},{14,7},{41,8},{16,... | collective-permute-start | bytes 1572872 | tf_op jit(solution)/shard_map/ppermute | solution.py:245
  130.7 14.9 %collective-permute-start.31 = (bf16[64,4096]{1,0:T(8,128)(2,1)S(1)}, bf16[64,4096]{1,0:T(8,128)(2,1)S(1)}, u32[]{:S(2)}, u32[]{:S(2)}) collective-permute-start(bf16[64,4096]{1,0:T(8,128)(2,1)S(1)} %get-tuple-element.18), channel_id=1, source_target_pairs={{97,0},{24,1},{99,2},{26,3},{101,4},{28,5},{103,6},{30,7},{105,8},... | collective-permute-start | bytes 1572872 | tf_op jit(solution)/shard_map/ppermute | solution.py:245
  138.7 6.9 %collective-permute-start.33 = (bf16[64,4096]{1,0:T(8,128)(2,1)S(1)}, bf16[64,4096]{1,0:T(8,128)(2,1)S(1)}, u32[]{:S(2)}, u32[]{:S(2)}) collective-permute-start(bf16[64,4096]{1,0:T(8,128)(2,1)S(1)} %get-tuple-element.20), channel_id=1, source_target_pairs={{0,1},{1,0},{2,3},{3,2},{4,5},{5,4},{6,7},{7,6},{8,9},{9,8},{10,11... | collective-permute-start | bytes 1572872 | tf_op jit(solution)/shard_map/ppermute | solution.py:63
  140.3 11.0 %collective-permute-start.32 = (bf16[64,4096]{1,0:T(8,128)(2,1)S(1)}, bf16[64,4096]{1,0:T(8,128)(2,1)S(1)}, u32[]{:S(2)}, u32[]{:S(2)}) collective-permute-start(bf16[64,4096]{1,0:T(8,128)(2,1)S(1)} %get-tuple-element.19), channel_id=1, source_target_pairs={{65,0},{16,1},{67,2},{18,3},{69,4},{20,5},{71,6},{22,7},{73,8},{24... | collective-permute-start | bytes 1572872 | tf_op jit(solution)/shard_map/ppermute | solution.py:248
  151.6 8.9 %collective-permute-start.34 = (bf16[32,4096]{1,0:T(8,128)(2,1)S(1)}, bf16[32,4096]{1,0:T(8,128)(2,1)S(1)}, u32[]{:S(2)}, u32[]{:S(2)}) collective-permute-start(bf16[32,4096]{1,0:T(8,128)(2,1)S(1)} %pad_maximum_fusion.3), channel_id=1, source_target_pairs={{0,24},{1,97},{2,26},{3,99},{4,28},{5,101},{6,30},{7,103},{8,0},{9... | collective-permute-start | bytes 786440 | tf_op jit(solution)/shard_map/ppermute | solution.py:76
  153.7 8.1 %collective-permute-start.35 = (bf16[32,4096]{1,0:T(8,128)(2,1)S(1)}, bf16[32,4096]{1,0:T(8,128)(2,1)S(1)}, u32[]{:S(2)}, u32[]{:S(2)}) collective-permute-start(bf16[32,4096]{1,0:T(8,128)(2,1)S(1)} %pad_maximum_fusion.4), channel_id=1, source_target_pairs={{0,16},{1,65},{2,18},{3,67},{4,20},{5,69},{6,22},{7,71},{8,24},{9,... | collective-permute-start | bytes 786440 | tf_op jit(solution)/shard_map/ppermute | solution.py:76
  153.9 10.5 %collective-permute-start.36 = (bf16[32,4096]{1,0:T(8,128)(2,1)S(1)}, bf16[32,4096]{1,0:T(8,128)(2,1)S(1)}, u32[]{:S(2)}, u32[]{:S(2)}) collective-permute-start(bf16[32,4096]{1,0:T(8,128)(2,1)S(1)} %pad_maximum_fusion.5), channel_id=1, source_target_pairs={{0,8},{1,33},{2,10},{3,35},{4,12},{5,37},{6,14},{7,39},{8,16},{9,4... | collective-permute-start | bytes 786440 | tf_op jit(solution)/shard_map/ppermute | solution.py:76
  (22 other events, 318.5 us)

commit v3 on v1

v3 whole, which is shorter than its diff:
```python
import math

import jax
import jax.numpy as jnp
from jax import lax
from jax.experimental import pallas as pl
from jax.experimental.pallas import tpu as pltpu
from jax.sharding import PartitionSpec as P

HEADS = 64
KV_HEADS = 8
HD = 128
CYCLE_STEPS = 4
CAP = 4
SIDE = 4
BOTH = ("ctx", "exp")
SHIFTS = (1, 3, 2)


def number(x, y, z, core):
    return (((x % SIDE) * SIDE + y % SIDE) * SIDE + z % SIDE) * 2 + core


def everyone():
    return [
        (x, y, z, core)
        for x in range(SIDE)
        for y in range(SIDE)
        for z in range(SIDE)
        for core in range(2)
    ]


def first_axis(d):
    return [
        (number(x, y, z, c), number(x + d * c, y + d * (1 - c), z, c)) for x, y, z, c in everyone()
    ]


def second_axis(d):
    return [
        (number(x, y, z, c), number(x + d * (1 - c), y + d * c, z, c)) for x, y, z, c in everyone()
    ]


def crossed(d):
    return [
        (number(x, y, z, c), number(x + d * (1 - c), y + d * c, z, 1 - c)) for x, y, z, c in everyone()
    ]


def uncrossed(d):
    return [(to, start) for start, to in crossed(d)]


def z_axis(d):
    return [(number(x, y, z, c), number(x, y, z + d, c)) for x, y, z, c in everyone()]


def z_exchange(bit):
    return [(number(x, y, z, c), number(x, y, z ^ bit, c)) for x, y, z, c in everyone()]


def sibling(shard):
    pairs = [(number(x, y, z, c), number(x, y, z, 1 - c)) for x, y, z, c in everyone()]
    return lax.ppermute(shard, BOTH, pairs)


def gathered(shard, along):
    got = {0: shard}
    for d in SHIFTS:
        got[d] = lax.ppermute(shard, BOTH, along(d))
    return [got[d] for d in range(SIDE)]


def dealt(blocks, along, sign):
    got = {0: blocks[0]}
    for d in SHIFTS:
        got[d] = lax.ppermute(blocks[d], BOTH, along(sign * d))
    return [got[d] for d in range(SIDE)]


def added(blocks):
    total = blocks[0].astype(jnp.float32)
    for block in blocks[1:]:
        total = total + block.astype(jnp.float32)
    return total


def whole(*names):
    spaces = {"v": pltpu.VMEM, "s": pltpu.SMEM}
    return [pl.BlockSpec(memory_space=spaces[n]) for n in names]


def project_kernel(where, place, p0, p1, p2, p3, w0, w1, res, codes_ref, spread, wide, named_by):
    depth = w0.shape[0]
    for k2, piece in enumerate((p0, p1, p2, p3)):
        part = jnp.dot(piece[:, :depth], w0[...], preferred_element_type=jnp.float32)
        part += jnp.dot(piece[:, depth : 2 * depth], w1[...], preferred_element_type=jnp.float32)
        for k1 in range(SIDE):
            at = place[k2 * SIDE + k1]
            residual = res[at].astype(jnp.float32)
            for zt in range(SIDE):
                lo = (k1 * SIDE + zt) * 8
                seg = part[lo : lo + 8]
                named_by[lo : lo + 8] = codes_ref[zt ^ where[2], at].astype(jnp.float32)
                wide[lo : lo + 8] = seg + jnp.where(zt == where[2], residual, 0.0)
        rows = wide[...].astype(jnp.bfloat16)
        codes = named_by[...]
        shape = (rows.shape[0], 16 * 2 * SIDE * CAP)
        slot = lax.broadcasted_iota(jnp.int32, shape, 1)
        group = lax.broadcasted_iota(jnp.int32, shape, 0) // 8
        code = ((slot // 64) * CAP + slot % CAP).astype(jnp.float32)
        named = jnp.logical_or(codes[:, 0:1] == code, codes[:, 1:2] == code)
        hit = jnp.logical_and(named, (slot % 64) // CAP == group)
        table = jnp.where(hit, 1.0, 0.0).astype(jnp.bfloat16)
        chosen = lax.dot_general(
            table, rows, (((0,), (0,)), ((), ())), preferred_element_type=jnp.float32
        ).astype(spread.dtype)
        i2 = (where[0] - k2 + SIDE) % SIDE
        for zt in range(SIDE):
            ahead = (zt - where[2] + SIDE) % SIDE
            for p in range(2):
                for k1 in range(SIDE):
                    lo = (zt * 2 + p) * 64 + k1 * 16
                    spread[ahead, p, i2, (where[1] - k1 + SIDE) % SIDE] = chosen[lo : lo + 16]


def project(where, place, pieces, w0, w1, res, codes):
    columns = w0.shape[1]
    return pl.pallas_call(
        project_kernel,
        in_specs=whole(*"ssvvvvvvvv"),
        out_specs=whole("v")[0],
        out_shape=jax.ShapeDtypeStruct((SIDE, 2, SIDE, SIDE, 4 * CAP, columns), jnp.bfloat16),
        scratch_shapes=[
            pltpu.VMEM((pieces[0].shape[0], columns), jnp.float32),
            pltpu.VMEM((pieces[0].shape[0], HD), jnp.float32),
        ],
        compiler_params=pltpu.CompilerParams(vmem_limit_bytes=16 * 1024 * 1024),
        cost_estimate=pl.CostEstimate(
            flops=2 * 512 * 2048 * 256 + 2 * 2048 * 128 * 256,
            bytes_accessed=6 * 1024 * 1024,
            transcendentals=0,
        ),
    )(where, place, *pieces, w0, w1, res, codes)


def hidden_step(blocks, at, row, gate_ref, up_ref, gain_ref, gate_in, up_in, sq_in, outs):
    gate_out, up_out, sq_out = outs
    rows = pl.ds(row, 256)
    gate = up = sq = None
    for block, c in zip(blocks, at):
        wide = block.astype(jnp.float32)
        square = wide * wide
        square = square[:, :128] + square[:, 128:]
        x = (wide * gain_ref[c]).astype(jnp.bfloat16)
        k = pl.ds(pl.multiple_of(c * 256, 256), 256)
        g = jnp.dot(x, gate_ref[k, :], preferred_element_type=jnp.float32)
        u = jnp.dot(x, up_ref[k, :], preferred_element_type=jnp.float32)
        gate = g if gate is None else gate + g
        up = u if up is None else up + u
        sq = square if sq is None else sq + square
    if gate_in is not None:
        gate, up, sq = gate + gate_in[rows], up + up_in[rows], sq + sq_in[rows]
    gate_out[rows], up_out[rows], sq_out[rows] = gate, up, sq


def first_kernel(count, has_sums, *refs):
    at_ref = refs[0]
    shards = refs[1 : 1 + 2 * count]
    gain_ref, gate_ref, up_ref = refs[1 + 2 * count : 4 + 2 * count]
    sums = refs[4 + 2 * count : 7 + 2 * count] if has_sums else (None, None, None)
    outs = refs[-3:]
    for half in range(2):
        blocks = [shards[half * count + i][k] for i in range(count) for k in range(SIDE)]
        at = [at_ref[(half * count + i) * SIDE + k] for i in range(count) for k in range(SIDE)]
        hidden_step(blocks, at, half * 256, gate_ref, up_ref, gain_ref, *sums, outs)


def first_products(at, mine, theirs, gain, gate, up, sums=()):
    count = len(mine)
    hidden = gate.shape[1]
    wide = jax.ShapeDtypeStruct((512, hidden), jnp.float32)
    return pl.pallas_call(
        lambda *refs: first_kernel(count, bool(sums), *refs),
        in_specs=whole("s", *("v" * (2 * count + 3 + len(sums)))),
        out_specs=whole(*"vvv"),
        out_shape=[wide, wide, jax.ShapeDtypeStruct((512, 128), jnp.float32)],
        input_output_aliases={4 + 2 * count + i: i for i in range(len(sums))},
        compiler_params=pltpu.CompilerParams(vmem_limit_bytes=12 * 1024 * 1024),
        cost_estimate=pl.CostEstimate(
            flops=4 * 512 * 1024 * count * hidden,
            bytes_accessed=4096 * count * hidden,
            transcendentals=0,
        ),
    )(at, *mine, *theirs, gain, gate, up, *sums)


def last_kernel(width, at_ref, mine, theirs, gain, gate_w, up_w, gate_in, up_in, sq_in, down, where, *refs):
    out_mine, out_theirs, rest, gate, up, sq, inner = refs
    for half, shard in enumerate((mine, theirs)):
        blocks = [shard[k] for k in range(SIDE)]
        at = [at_ref[half * SIDE + k] for k in range(SIDE)]
        hidden_step(blocks, at, half * 256, gate_w, up_w, gain, gate_in, up_in, sq_in, (gate, up, sq))
    for half in range(2):
        rows = pl.ds(half * 256, 256)
        mean = jnp.sum(sq[rows], axis=1, keepdims=True) * (1.0 / width)
        scale = lax.rsqrt(mean + 1e-06)
        g = gate[rows] * scale
        u = up[rows] * scale
        act = (g / (1.0 + jnp.exp(-g)) * u).astype(jnp.bfloat16)
        for i in range(16):
            inner[half * 16 + i] = act[i * 16 : (i + 1) * 16]
    for half in range(2):
        for d in range(SIDE):
            i2 = (where[half] - d + SIDE) % SIDE
            for j in range(SIDE):
                i1 = (where[1 - half] - j + SIDE) % SIDE
                rest[((d * 2 + half) * SIDE + j) * 16 : ((d * 2 + half) * SIDE + j + 1) * 16, :] = inner[
                    half * 16 + i2 * SIDE + i1
                ]
    part = jnp.dot(rest[256:384, :], down[...], preferred_element_type=jnp.float32)
    part = part.astype(jnp.bfloat16)
    out_mine[...] = part[:64]
    out_theirs[...] = part[64:]


def last_products(at, mine, theirs, gain, gate, up, sums, down, where):
    hidden, width = down.shape
    return pl.pallas_call(
        lambda *refs: last_kernel(width, *refs),
        in_specs=whole(*"svvvvvvvvvs"),
        out_specs=whole(*"vvv"),
        out_shape=[jax.ShapeDtypeStruct((64, width), jnp.bfloat16)] * 2
        + [jax.ShapeDtypeStruct((512, hidden), jnp.bfloat16)],
        scratch_shapes=[
            pltpu.VMEM((512, hidden), jnp.float32),
            pltpu.VMEM((512, hidden), jnp.float32),
            pltpu.VMEM((512, 128), jnp.float32),
            pltpu.VMEM((32, 16, hidden), jnp.bfloat16),
        ],
        compiler_params=pltpu.CompilerParams(vmem_limit_bytes=16 * 1024 * 1024),
        cost_estimate=pl.CostEstimate(
            flops=4 * 512 * 1024 * hidden + 2 * 128 * hidden * width,
            bytes_accessed=4096 * hidden + 2 * hidden * width,
            transcendentals=512 * hidden,
        ),
    )(at, mine, theirs, gain, gate, up, *sums, down, where)


def down_kernel(picks, inner, down, after, *outs):
    for i, d in enumerate(picks):
        part = jnp.dot(
            inner[d * 128 : (d + 1) * 128, :], down[...], preferred_element_type=jnp.float32
        ).astype(jnp.bfloat16)
        outs[2 * i][...] = part[:64]
        outs[2 * i + 1][...] = part[64:]


def down_products(picks, inner, down, after):
    hidden, width = down.shape
    return pl.pallas_call(
        lambda *refs: down_kernel(picks, *refs),
        in_specs=whole(*"vv") + [pl.BlockSpec(memory_space=pl.ANY)],
        out_specs=whole(*("vv" * len(picks))),
        out_shape=[jax.ShapeDtypeStruct((64, width), jnp.bfloat16)] * (2 * len(picks)),
        compiler_params=pltpu.CompilerParams(vmem_limit_bytes=10 * 1024 * 1024),
        cost_estimate=pl.CostEstimate(
            flops=2 * 128 * len(picks) * hidden * width,
            bytes_accessed=2 * hidden * width,
            transcendentals=0,
        ),
    )(inner, down, after)


def pack_kernel(terms, *refs):
    outs = refs[2 * terms :]
    for half in range(2):
        total = refs[half * terms][...].astype(jnp.float32)
        for i in range(1, terms):
            total = total + refs[half * terms + i][...].astype(jnp.float32)
        total = total.astype(jnp.bfloat16)
        for d in range(SIDE):
            outs[d][half * 16 : half * 16 + 16, :] = total[d * 16 : (d + 1) * 16]


def packed_sums(own, other):
    terms, width = len(own), own[0].shape[1]
    return pl.pallas_call(
        lambda *refs: pack_kernel(terms, *refs),
        in_specs=whole(*("v" * 2 * terms)),
        out_specs=whole(*("v" * SIDE)),
        out_shape=[jax.ShapeDtypeStruct((32, width), jnp.bfloat16)] * SIDE,
        compiler_params=pltpu.CompilerParams(vmem_limit_bytes=12582912),
    )(*own, *other)


def pick_kernel(at_ref, where, *refs):
    shards, outs = refs[: 2 * SIDE], refs[-2:]
    for half in range(2):
        for i in range(SIDE):
            for k in range(SIDE):
                columns = pl.ds(pl.multiple_of(at_ref[i * 2 * SIDE + half * SIDE + k] * 256, 256), 256)
                shard = shards[half * SIDE + i]
                outs[half][:, columns] = shard[k, where[half] * SIDE + where[1 - half]]


def pick_hidden(at, where, shards, after):
    shards = [r.reshape(SIDE, 16, 16, r.shape[-1]) for r in shards]
    return pl.pallas_call(
        pick_kernel,
        in_specs=whole("s", "s", *("v" * len(shards))) + [pl.BlockSpec(memory_space=pl.ANY)],
        out_specs=whole(*"vv"),
        out_shape=[jax.ShapeDtypeStruct((16, 16 * shards[0].shape[-1]), jnp.bfloat16)] * 2,
        compiler_params=pltpu.CompilerParams(vmem_limit_bytes=8 * 1024 * 1024),
    )(at, where, *shards, after)


def per_device(
    queries,
    key_rows,
    values,
    span_order,
    residual,
    out_weight,
    norm_gain,
    routes,
    route_gates,
    gate_proj,
    up_proj,
    down_proj,
):
    n_ctx = lax.axis_size("ctx")
    n_exp = lax.axis_size("exp")
    here = lax.axis_index("ctx")
    column = lax.axis_index("exp")
    core = column % 2
    z_here = column // 2
    block_rows = queries.shape[0]
    group = HEADS // KV_HEADS
    kv_local = key_rows.shape[1] // HD
    width = kv_local * HD
    token_count, model = residual.shape
    offsets = jnp.arange(block_rows, dtype=jnp.int32)
    back_places = (here - jnp.arange(CYCLE_STEPS, dtype=jnp.int32)) % n_ctx
    picked_place = back_places[:, None] == jnp.arange(n_ctx, dtype=jnp.int32)[None, :]
    starts = jnp.sum(jnp.where(picked_place, span_order[None, :], 0), axis=1) * block_rows
    key_pos = (starts[:, None] + offsets[None, :]).reshape(-1)
    query_pos = jnp.sum(jnp.where(picked_place[0], span_order, 0)) * block_rows + offsets

    packed = jnp.pad(key_rows, ((0, 0), (0, width))) + jnp.pad(values, ((0, 0), (width, 0)))

    def onward(shard, step):
        return lax.ppermute(shard, "ctx", [(i, (i + step) % n_ctx) for i in range(n_ctx)])

    collected = [packed] + [onward(packed, step) for step in range(1, CYCLE_STEPS)]
    flat_routes = routes.reshape(-1)
    pair_ids = jnp.arange(flat_routes.shape[0], dtype=jnp.int32)
    same_expert = flat_routes[:, None] == flat_routes[None, :]
    earlier = pair_ids[None, :] < pair_ids[:, None]
    slot_number = jnp.sum(jnp.where(same_expert & earlier, 1, 0), axis=1).astype(jnp.int32)
    other_core = (flat_routes + core) % 2
    codes = ((flat_routes // 2 * 2 + other_core) * CAP + slot_number).astype(jnp.bfloat16)
    codes = jnp.pad(codes.reshape(token_count, 2), ((0, 0), (0, HD - 2)))
    z_places = jnp.arange(SIDE, dtype=jnp.int32)
    columns = out_weight.shape[1]
    by_column = jnp.moveaxis(residual.reshape(token_count, n_ctx, columns), 1, 0)
    by_column = jnp.concatenate(
        [by_column, jnp.broadcast_to(codes[None], (n_ctx, token_count, HD))], axis=2
    )
    by_column = lax.all_to_all(by_column, "ctx", split_axis=0, concat_axis=0, tiled=True)
    residual_slab = by_column[:, :, :columns]
    codes = by_column[None, :, :, columns:]
    codes = jnp.concatenate([codes, lax.ppermute(codes, BOTH, z_exchange(1))], axis=0)
    codes = jnp.concatenate([codes, lax.ppermute(codes, BOTH, z_exchange(2))], axis=0)
    weight_other = sibling(out_weight)
    stacked = jnp.concatenate(collected, axis=0)
    key_all = stacked[:, :width].reshape(-1, kv_local, HD)
    value_all = stacked[:, width:].reshape(-1, kv_local, HD)
    query_heads = queries.reshape(block_rows, kv_local, group, HD)
    scores = jnp.einsum(
        "qkgd,lkd->kgql", query_heads, key_all, preferred_element_type=jnp.float32
    ) * (1.0 / math.sqrt(HD))
    admitted = key_pos[None, :] <= query_pos[:, None]
    scores = jnp.where(admitted[None, None], scores, -1e30)
    row_max = jnp.max(scores, axis=-1, keepdims=True)
    exp_scores = jnp.exp(scores - row_max)
    attend_probs = (exp_scores / jnp.sum(exp_scores, axis=-1, keepdims=True)).astype(jnp.bfloat16)
    mixed = jnp.einsum(
        "kgql,lkd->qkgd", attend_probs, value_all, preferred_element_type=jnp.float32
    )
    attended = mixed.astype(jnp.bfloat16).reshape(SIDE, 2, token_count, kv_local * group * HD)

    half = SIDE * token_count
    rows_0 = attended[:, 0].reshape(half, -1)
    rows_1 = attended[:, 1].reshape(half, -1)
    kept = jnp.where(core == 0, rows_0, rows_1)
    given = jnp.where(core == 0, rows_1, rows_0)
    paired = jnp.concatenate([kept, sibling(given)], axis=1)
    line = jnp.concatenate(gathered(paired, first_axis), axis=0)
    plane = gathered(line, second_axis)

    x_here, y_here = here // SIDE, here % SIDE
    second = jnp.where(core == 0, x_here, y_here)
    first = jnp.where(core == 0, y_here, x_here)
    where = jnp.stack([second, first, z_here]).astype(jnp.int32)
    k2, k1 = z_places[:, None], z_places[None, :]
    by_x = ((x_here - k2) % SIDE * SIDE + (y_here - k1) % SIDE).astype(jnp.int32)
    by_y = ((x_here - k1) % SIDE * SIDE + (y_here - k2) % SIDE).astype(jnp.int32)
    place = jnp.where(core == 0, by_x, by_y)
    place_other = jnp.where(core == 0, by_y, by_x)
    spread = project(
        where, place.reshape(-1), plane, out_weight, weight_other, residual_slab, codes
    )

    rows = added(dealt([spread[d] for d in range(SIDE)], z_axis, 1)).astype(jnp.bfloat16)
    rows = rows.reshape(2, SIDE * SIDE * SIDE * CAP, columns)
    line = gathered(rows, first_axis)
    own = jnp.stack([r[0] for r in line])
    other = jnp.stack([r[1] for r in line])
    mine, theirs = {0: own}, {0: sibling(other)}
    for d in (1, -1):
        mine[d] = lax.ppermute(own, BOTH, second_axis(d))
        theirs[d] = lax.ppermute(other, BOTH, crossed(d))
    gain = norm_gain.astype(jnp.float32).reshape(n_ctx, 1, columns)
    gate_w, up_w, down_w = gate_proj[0], up_proj[0], down_proj[0]

    def at(*shifts):
        return jnp.concatenate([place[d] for d in shifts] + [place_other[d] for d in shifts])

    near = first_products(at(0), [mine[0]], [theirs[0]], gain, gate_w, up_w)
    on_mine, on_theirs, *near = lax.optimization_barrier((mine[1], theirs[-1], *near))
    mine[2] = lax.ppermute(on_mine, BOTH, second_axis(1))
    theirs[2] = lax.ppermute(on_theirs, BOTH, first_axis(-1))
    sides = first_products(
        at(1, 3), [mine[1], mine[-1]], [theirs[1], theirs[-1]], gain, gate_w, up_w, tuple(near)
    )
    far_mine, far_theirs, inner = last_products(
        at(2), mine[2], theirs[2], gain, gate_w, up_w, tuple(sides), down_w, where
    )
    side_out = down_products((1, 3), inner, down_w, far_mine)
    far_mine = lax.ppermute(far_mine, BOTH, second_axis(-1))
    far_theirs = lax.ppermute(far_theirs, BOTH, first_axis(1))
    near_out = down_products((0,), inner, down_w, far_theirs)
    back_mine, back_theirs, front_mine, front_theirs = side_out
    own = [near_out[0], lax.ppermute(front_mine, BOTH, second_axis(1))]
    other = [sibling(near_out[1]), lax.ppermute(back_theirs, BOTH, uncrossed(1))]
    back_mine = added([back_mine, far_mine]).astype(jnp.bfloat16)
    front_theirs = added([front_theirs, far_theirs]).astype(jnp.bfloat16)
    own.append(lax.ppermute(back_mine, BOTH, second_axis(-1)))
    other.append(lax.ppermute(front_theirs, BOTH, uncrossed(-1)))
    line = packed_sums(own, other)
    n1 = SIDE * CAP

    names = (0, 1, -1, 2)
    hidden_mine, hidden_theirs = pick_hidden(
        jnp.concatenate([at(0), at(1), at(3), at(2)]),
        where,
        [mine[d] for d in names] + [theirs[d] for d in names],
        side_out[0],
    )
    hidden_rows = jnp.concatenate([hidden_mine, sibling(hidden_theirs)], axis=0)
    slots = n_exp * CAP
    ahead = (flat_routes // 2 - z_here) % SIDE
    target = (ahead * 2 + other_core) * CAP + slot_number
    match_table = jnp.where(
        target[:, None] == jnp.arange(slots, dtype=jnp.int32)[None, :], 1.0, 0.0
    ).astype(jnp.bfloat16)
    per_z = 2 * CAP
    column_rows = added(dealt(line, first_axis, -1)).astype(jnp.bfloat16)
    row = jnp.arange(slots, dtype=jnp.int32)
    source = (row // CAP % 2) * n1 + (z_here - row // per_z) % SIDE * CAP + row % CAP
    reorder = jnp.where(source[:, None] == row[None, :], 1.0, 0.0).astype(jnp.bfloat16)
    column_rows = jnp.concatenate([column_rows, hidden_rows], axis=1)
    sent = jnp.dot(reorder, column_rows, preferred_element_type=jnp.float32).astype(jnp.bfloat16)
    sent = [sent[d * per_z : (d + 1) * per_z] for d in range(SIDE)]
    expert_rows = jnp.concatenate(dealt(sent, z_axis, -1), axis=0)
    picked = jnp.dot(match_table, expert_rows, preferred_element_type=jnp.float32).reshape(
        token_count, 2, -1
    )
    total = (
        picked[:, 0, model:]
        + route_gates[:, 0:1] * picked[:, 0, :model]
        + route_gates[:, 1:2] * picked[:, 1, :model]
    )
    return total.astype(jnp.bfloat16)


def solution(mesh):
    return jax.shard_map(
        per_device,
        mesh=mesh,
        in_specs=(
            P("ctx", "exp"),
            P("ctx", "exp"),
            P("ctx", "exp"),
            P(),
            P(("ctx", "exp"), None),
            P("exp", "ctx"),
            P(),
            P(("ctx", "exp"), None),
            P(("ctx", "exp"), None),
            P("exp", None, "ctx"),
            P("exp", None, "ctx"),
            P("exp", "ctx", None),
        ),
        out_specs=P(("ctx", "exp"), None),
        check_vma=False,
    )
```

time: 246 us -> 160 us (0.65)
  waiting for transfers between devices: 127 us -> 56.3 us
  local copies, waits for them, and re-layouts: 43.6 us -> 9.71 us
  starting transfers between devices: 45.8 us -> 63.8 us
  other arithmetic: 3.91 us -> 9.44 us
    ppermute x12 -> x9, waiting for transfers between devices: 64.1 us -> 12.3 us  [gathered(): got[d] = lax.ppermute(shard, BOTH, along(d))]
    concatenate x7 -> x1, local copies, waits for them, and re-layouts: 31.7 us -> 0.78 us  [per_device(): jnp.concatenate([at(0), at(1), at(3), at(2)])]
    ppermute x15 -> x9, waiting for transfers between devices: 45.6 us -> 19.9 us  [dealt(): got[d] = lax.ppermute(blocks[d], BOTH, along(sign * d))]
    ppermute x3 -> x17, waiting for transfers between devices: 0.88 us -> 23.1 us  [the longest x1 7.9 us: per_device(): far_theirs = lax.ppermute(far_theirs, BOTH, first_axis(1))]
    ppermute x3 -> x17, starting transfers between devices: 5.63 us -> 26.4 us  [the longest x3 6.84 us: onward(): lax.ppermute(shard, 'ctx', [(i, (i + step) % n_ctx) for i in range(n_ctx)])]
    ppermute x4 -> x5, waiting for transfers between devices: 8.51 us -> 0.9 us  [sibling(): return lax.ppermute(shard, BOTH, pairs)]
    all_to_all x1, waiting for transfers between devices: 7.59 us -> 0.01 us  [per_device(): lax.all_to_all(by_column, 'ctx', split_axis=0, concat_axis=0, tiled=True)]
    ppermute x15 -> x9, starting transfers between devices: 20.4 us -> 14.9 us  [dealt(): got[d] = lax.ppermute(blocks[d], BOTH, along(sign * d))]
  transfers between devices with their start and end apart: 35 -> 41, of which waited for: 29 -> 22; matrix products, arithmetic and copies ran while one was open for 3% -> 7% of each run, Pallas kernels for 0% -> 6%
where the time goes in v3:
time: 160 us; the launch traced here: 159 us
  starting transfers between devices  63.8 us (40%)
  waiting for transfers between devices  56.3 us (35%)
  Pallas kernels  17.3 us (11%)
  local copies, waits for them, and re-layouts  9.71 us (6%)
  other arithmetic  9.44 us (6%)
    ppermute x9, waiting for transfers between devices, dealt(): got[d] = lax.ppermute(blocks[d], BOTH, along(sign * d))  19.9 us
    ppermute x9, starting transfers between devices, gathered(): got[d] = lax.ppermute(shard, BOTH, along(d))  17.1 us
    ppermute x9, starting transfers between devices, dealt(): got[d] = lax.ppermute(blocks[d], BOTH, along(sign * d))  14.9 us
    ppermute x9, waiting for transfers between devices, gathered(): got[d] = lax.ppermute(shard, BOTH, along(d))  12.3 us
    ppermute x1, waiting for transfers between devices, per_device(): far_theirs = lax.ppermute(far_theirs, BOTH, first_axis(1))  7.9 us
    ppermute x1, waiting for transfers between devices, per_device(): other.append(lax.ppermute(front_theirs, BOTH, uncrossed(-1)))  7.04 us
    unnamed x61, local copies, waits for them, and re-layouts  6.96 us
    ppermute x3, starting transfers between devices, onward(): lax.ppermute(shard, 'ctx', [(i, (i + step) % n_ctx) for i in range(n_ctx)])  6.84 us
  transfers between devices with their start and end apart: 41, of which 22 were waited for; matrix products, arithmetic and copies ran while one was open for 7% of the time, Pallas kernels for 6%

profile of v3, /device:TPU:0, one launch (start us, length us, event | category | flops | bytes accessed | tf_op | source)
XLA Modules:
  0.0 159.2 jit_solution(8052690861554745715)
XLA Ops:
  2.4 2.9 %collective-permute-start.1 = (bf16[64,256]{1,0:T(8,128)(2,1)S(1)}, bf16[64,256]{1,0:T(8,128)(2,1)S(1)}, u32[]{:S(2)}, u32[]{:S(2)}) collective-permute-start(bf16[64,256]{1,0:T(8,128)(2,1)S(1)} %pad_add_fusion), channel_id=1, source_target_pairs={{0,16},{8,24},{16,32},{24,40},{32,48},{40,56},{48,64},{56,72},{64,... | collective-permute-start | bytes 98312 | tf_op jit(solution)/shard_map/ppermute | solution.py:355
  5.3 2.3 %collective-permute-start.2 = (bf16[64,256]{1,0:T(8,128)(2,1)S(1)}, bf16[64,256]{1,0:T(8,128)(2,1)S(1)}, u32[]{:S(2)}, u32[]{:S(2)}) collective-permute-start(bf16[64,256]{1,0:T(8,128)(2,1)S(1)} %pad_add_fusion), channel_id=1, source_target_pairs={{0,24},{8,32},{16,40},{24,48},{32,56},{40,64},{48,72},{56,80},{64,... | collective-permute-start | bytes 98312 | tf_op jit(solution)/shard_map/ppermute | solution.py:355
  11.3 4.2 %all-to-all-start = ((bf16[16,8,384]{2,1,0:T(8,128)(2,1)}), bf16[16,8,384]{2,1,0:T(8,128)(2,1)S(1)}, u32[]{:S(2)}, u32[]{:S(2)}) async-start(bf16[16,8,384]{2,1,0:T(8,128)(2,1)} %pad_maximum_fusion.7), calls=%async_computation | async-start | bytes 196608 | tf_op jit(solution)/shard_map/all_to_all | solution.py:372
  23.4 2.7 %collective-permute-start.5 = (bf16[32,2048]{1,0:T(8,128)(2,1)S(1)}, bf16[32,2048]{1,0:T(8,128)(2,1)S(1)}, u32[]{:S(2)}, u32[]{:S(2)}) collective-permute-start(bf16[32,2048]{1,0:T(8,128)(2,1)S(1)} %pad_maximum_fusion.5), channel_id=1, source_target_pairs={{0,16},{1,65},{2,18},{3,67},{4,20},{5,69},{6,22},{7,71},{8,24},{9,... | collective-permute-start | bytes 393224 | tf_op jit(solution)/shard_map/ppermute | solution.py:72
  32.6 2.7 %collective-permute-start.8 = (bf16[128,2048]{1,0:T(8,128)(2,1)S(1)}, bf16[128,2048]{1,0:T(8,128)(2,1)S(1)}, u32[]{:S(2)}, u32[]{:S(2)}) collective-permute-start(bf16[128,2048]{1,0:T(8,128)(2,1)S(1)} %pad_maximum_fusion.p0), channel_id=1, source_target_pairs={{0,64},{1,17},{2,66},{3,19},{4,68},{5,21},{6,70},{7,23},{8,72},{9,... | collective-permute-start | bytes 1572872 | tf_op jit(solution)/shard_map/ppermute | solution.py:72
  36.9 4.0 %collective-permute-start.12 = (bf16[2,16,8,128]{3,2,1,0:T(8,128)(2,1)S(1)}, bf16[2,16,8,128]{3,2,1,0:T(8,128)(2,1)S(1)}, u32[]{:S(2)}, u32[]{:S(2)}) collective-permute-start(bf16[2,16,8,128]{3,2,1,0:T(8,128)(2,1)S(1)} %pad_maximum_fusion.8), channel_id=1, source_target_pairs={{0,4},{1,5},{2,6},{3,7},{4,0},{5,1},{6,2},{7,3},{8,12},{9,13},{10,... | collective-permute-start | bytes 196616 | tf_op jit(solution)/shard_map/ppermute | solution.py:376
  41.0 2.2 %collective-permute-done.12 = bf16[2,16,8,128]{3,2,1,0:T(8,128)(2,1)S(1)} collective-permute-done((bf16[2,16,8,128]{3,2,1,0:T(8,128)(2,1)S(1)}, bf16[2,16,8,128]{3,2,1,0:T(8,128)(2,1)S(1)}, u32[]{:S(2)}, u32[]{:S(2)}) %collective-permute-start.12) | collective-permute-done | bytes 65568 | tf_op jit(solution)/shard_map/ppermute | solution.py:376
  43.2 4.9 %collective-permute-done.8.p2 = bf16[128,2048]{1,0:T(8,128)(2,1)S(1)} collective-permute-done((bf16[128,2048]{1,0:T(8,128)(2,1)S(1)}, bf16[128,2048]{1,0:T(8,128)(2,1)S(1)}, u32[]{:S(2)}, u32[]{:S(2)}) %collective-permute-start.8) | collective-permute-done | bytes 524320 | tf_op jit(solution)/shard_map/ppermute | solution.py:72
  48.1 2.6 %shard_map.118 = bf16[4,2,4,4,16,256]{5,4,3,2,1,0:T(8,128)(2,1)S(1)} custom-call(s32[3]{0:T(128)S(1)} %pad_add_fusion.2.where.refs_10_, s32[16]{0:T(128)S(1)} %select_n.226.place, bf16[128,2048]{1,0:T(8,128)(2,1)S(1)} %pad_maximum_fusion.p0, bf16[128,2048]{1,0:T(8,128)(2,1)S(1)} %collective-permute-done.7.p1, ...), custom_call_target="tpu_custom_call" | custom-call | flops 671088640 | bytes 6291456 | tf_op jit(solution)/shard_map/pallas_call | solution.py:131
  52.7 3.6 %collective-permute-start.14 = (bf16[2,4,4,16,256]{4,3,2,1,0:T(8,128)(2,1)S(1)}, bf16[2,4,4,16,256]{4,3,2,1,0:T(8,128)(2,1)S(1)}, u32[]{:S(2)}, u32[]{:S(2)}) collective-permute-start(bf16[2,4,4,16,256]{4,3,2,1,0:T(8,128)(2,1)S(1)} %get-tuple-element.59), channel_id=1, source_target_pairs={{0,4},{1,5},{2,6},{3,7},{4,0},{5,1},{6,2},{7,3},{8,12},{9,13},{10,... | collective-permute-start | bytes 786440 | tf_op jit(solution)/shard_map/ppermute | solution.py:79
  57.3 3.8 %collective-permute-done.13 = bf16[2,4,4,16,256]{4,3,2,1,0:T(8,128)(2,1)S(1)} collective-permute-done((bf16[2,4,4,16,256]{4,3,2,1,0:T(8,128)(2,1)S(1)}, bf16[2,4,4,16,256]{4,3,2,1,0:T(8,128)(2,1)S(1)}, u32[]{:S(2)}, u32[]{:S(2)}) %collective-permute-start.13) | collective-permute-done | bytes 262176 | tf_op jit(solution)/shard_map/ppermute | solution.py:79
  61.2 5.0 %collective-permute-done.14 = bf16[2,4,4,16,256]{4,3,2,1,0:T(8,128)(2,1)S(1)} collective-permute-done((bf16[2,4,4,16,256]{4,3,2,1,0:T(8,128)(2,1)S(1)}, bf16[2,4,4,16,256]{4,3,2,1,0:T(8,128)(2,1)S(1)}, u32[]{:S(2)}, u32[]{:S(2)}) %collective-permute-start.14) | collective-permute-done | bytes 262176 | tf_op jit(solution)/shard_map/ppermute | solution.py:79
  67.8 2.4 %collective-permute-start.17 = (bf16[2,256,256]{2,1,0:T(8,128)(2,1)S(1)}, bf16[2,256,256]{2,1,0:T(8,128)(2,1)S(1)}, u32[]{:S(2)}, u32[]{:S(2)}) collective-permute-start(bf16[2,256,256]{2,1,0:T(8,128)(2,1)S(1)} %bitcast.148), channel_id=1, source_target_pairs={{0,16},{1,65},{2,18},{3,67},{4,20},{5,69},{6,22},{7,71},{8,24},{9,... | collective-permute-start | bytes 786440 | tf_op jit(solution)/shard_map/ppermute | solution.py:72
  71.8 2.2 %collective-permute-done.16 = bf16[2,256,256]{2,1,0:T(8,128)(2,1)S(1)} collective-permute-done((bf16[2,256,256]{2,1,0:T(8,128)(2,1)S(1)}, bf16[2,256,256]{2,1,0:T(8,128)(2,1)S(1)}, u32[]{:S(2)}, u32[]{:S(2)}) %collective-permute-start.16) | collective-permute-done | bytes 262176 | tf_op jit(solution)/shard_map/ppermute | solution.py:72
  74.1 3.3 %collective-permute-done.17 = bf16[2,256,256]{2,1,0:T(8,128)(2,1)S(1)} collective-permute-done((bf16[2,256,256]{2,1,0:T(8,128)(2,1)S(1)}, bf16[2,256,256]{2,1,0:T(8,128)(2,1)S(1)}, u32[]{:S(2)}, u32[]{:S(2)}) %collective-permute-start.17) | collective-permute-done | bytes 262176 | tf_op jit(solution)/shard_map/ppermute | solution.py:72
  77.9 2.5 %collective-permute-start.20 = (bf16[4,256,256]{2,1,0:T(8,128)(2,1)S(1)}, bf16[4,256,256]{2,1,0:T(8,128)(2,1)S(1)}, u32[]{:S(2)}, u32[]{:S(2)}) collective-permute-start(bf16[4,256,256]{2,1,0:T(8,128)(2,1)S(1)} %pad_maximum_fusion.2), channel_id=1, source_target_pairs={{0,97},{1,24},{2,99},{3,26},{4,101},{5,28},{6,103},{7,30},{8,105},... | collective-permute-start | bytes 1572872 | tf_op jit(solution)/shard_map/ppermute | solution.py:425
  81.7 2.1 %collective-permute-start.24 = (bf16[4,256,256]{2,1,0:T(8,128)(2,1)S(1)}, bf16[4,256,256]{2,1,0:T(8,128)(2,1)S(1)}, u32[]{:S(2)}, u32[]{:S(2)}) collective-permute-start(bf16[4,256,256]{2,1,0:T(8,128)(2,1)S(1)} %pad_maximum_fusion.1.refs_1_), channel_id=1, source_target_pairs={{0,96},{1,25},{2,98},{3,27},{4,100},{5,29},{6,102},{7,31},{8,104},... | collective-permute-start | bytes 1572872 | tf_op jit(solution)/shard_map/ppermute | solution.py:424
  84.0 3.0 %copy-done.1 = bf16[1,4096,768]{2,1,0:T(8,128)(2,1)S(1)} copy-done((bf16[1,4096,768]{2,1,0:T(8,128)(2,1)S(1)}, bf16[1,4096,768]{2,1,0:T(8,128)(2,1)}, u32[]{:S(2)}) %copy-start.1) | copy-done | bytes 6291480
  87.0 2.4 %shard_map.119 = (f32[512,768]{1,0:T(8,128)S(1)}, f32[512,768]{1,0:T(8,128)S(1)}, f32[512,128]{1,0:T(8,128)S(1)}) custom-call(s32[8]{0:T(128)S(1)} %pad_add_fusion.3.refs_0_, bf16[4,256,256]{2,1,0:T(8,128)(2,1)S(1)} %pad_maximum_fusion.1.refs_1_, bf16[4,256,256]{2,1,0:T(8,128)(2,1)S(1)} %collective-permute-done.21.refs_2_, f32[16,1,256]{2,1,0:T(1,128)S(1)} %bitcast.139, ...), custom_call_target="tpu_custom_call" | custom-call | flops 1610612736 | bytes 3145728 | tf_op jit(solution)/shard_map/pallas_call | solution.py:185
  91.0 2.6 %collective-permute-start.23 = (bf16[4,256,256]{2,1,0:T(8,128)(2,1)S(1)}, bf16[4,256,256]{2,1,0:T(8,128)(2,1)S(1)}, u32[]{:S(2)}, u32[]{:S(2)}) collective-permute-start(bf16[4,256,256]{2,1,0:T(8,128)(2,1)S(1)} %collective-permute-done.20.refs_4_), channel_id=1, source_target_pairs={{0,24},{1,97},{2,26},{3,99},{4,28},{5,101},{6,30},{7,103},{8,0},{9... | collective-permute-start | bytes 1572872 | tf_op jit(solution)/shard_map/ppermute | solution.py:435
  93.8 2.2 %collective-permute-done.25.refs_3_ = bf16[4,256,256]{2,1,0:T(8,128)(2,1)S(1)} collective-permute-done((bf16[4,256,256]{2,1,0:T(8,128)(2,1)S(1)}, bf16[4,256,256]{2,1,0:T(8,128)(2,1)S(1)}, u32[]{:S(2)}, u32[]{:S(2)}) %collective-permute-start.25) | collective-permute-done | bytes 524320 | tf_op jit(solution)/shard_map/ppermute | solution.py:425
  96.0 4.2 %shard_map.120 = (f32[512,768]{1,0:T(8,128)S(1)}, f32[512,768]{1,0:T(8,128)S(1)}, f32[512,128]{1,0:T(8,128)S(1)}) custom-call(s32[16]{0:T(128)S(1)} %pad_add_fusion.4.refs_0_, bf16[4,256,256]{2,1,0:T(8,128)(2,1)S(1)} %collective-permute-done.19.refs_1_, ...), custom_call_target="tpu_custom_call", output_to_operand_aliasing={{0}: (8, {}), {1}: (9, {}), {2}: (10, {})} | custom-call | flops 3221225472 | bytes 6291456 | tf_op jit(solution)/shard_map/pallas_call | solution.py:185
  100.2 2.0 %collective-permute-done.22.refs_1_ = bf16[4,256,256]{2,1,0:T(8,128)(2,1)S(1)} collective-permute-done((bf16[4,256,256]{2,1,0:T(8,128)(2,1)S(1)}, bf16[4,256,256]{2,1,0:T(8,128)(2,1)S(1)}, u32[]{:S(2)}, u32[]{:S(2)}) %collective-permute-start.22) | collective-permute-done | bytes 524320 | tf_op jit(solution)/shard_map/ppermute | solution.py:434
  102.2 3.7 %shard_map.121 = (bf16[64,4096]{1,0:T(8,128)(2,1)S(1)}, bf16[64,4096]{1,0:T(8,128)(2,1)S(1)}, bf16[512,768]{1,0:T(8,128)(2,1)S(1)}) custom-call(s32[8]{0:T(128)S(1)} %pad_add_fusion.1.refs_0_, bf16[4,256,256]{2,1,0:T(8,128)(2,1)S(1)} %collective-permute-done.22.refs_1_, bf16[4,256,256]{2,1,0:T(8,128)(2,1)S(1)} %collective-permute-done.23.refs_2_, ...), custom_call_target="tpu_custom_call" | custom-call | flops 2415919104 | bytes 9437184 | tf_op jit(solution)/shard_map/pallas_call | solution.py:231
  105.9 2.1 %collective-permute-start.26 = (bf16[64,4096]{1,0:T(8,128)(2,1)S(1)}, bf16[64,4096]{1,0:T(8,128)(2,1)S(1)}, u32[]{:S(2)}, u32[]{:S(2)}) collective-permute-start(bf16[64,4096]{1,0:T(8,128)(2,1)S(1)} %get-tuple-element.43), channel_id=1, source_target_pairs={{0,8},{1,33},{2,10},{3,35},{4,12},{5,37},{6,14},{7,39},{8,16},{9,4... | collective-permute-start | bytes 1572872 | tf_op jit(solution)/shard_map/ppermute | solution.py:444
  111.9 7.9 %collective-permute-done.26.refs_2_ = bf16[64,4096]{1,0:T(8,128)(2,1)S(1)} collective-permute-done((bf16[64,4096]{1,0:T(8,128)(2,1)S(1)}, bf16[64,4096]{1,0:T(8,128)(2,1)S(1)}, u32[]{:S(2)}, u32[]{:S(2)}) %collective-permute-start.26) | collective-permute-done | bytes 524320 | tf_op jit(solution)/shard_map/ppermute | solution.py:444
  122.8 7.0 %collective-permute-done.32.refs_5_ = bf16[64,4096]{1,0:T(8,128)(2,1)S(1)} collective-permute-done((bf16[64,4096]{1,0:T(8,128)(2,1)S(1)}, bf16[64,4096]{1,0:T(8,128)(2,1)S(1)}, u32[]{:S(2)}, u32[]{:S(2)}) %collective-permute-start.32) | collective-permute-done | bytes 524320 | tf_op jit(solution)/shard_map/ppermute | solution.py:452
  131.0 3.4 %collective-permute-start.33 = (bf16[32,4096]{1,0:T(8,128)(2,1)}, bf16[32,4096]{1,0:T(8,128)(2,1)}, u32[]{:S(2)}, u32[]{:S(2)}) collective-permute-start(bf16[32,4096]{1,0:T(8,128)(2,1)} %get-tuple-element.52), channel_id=1, source_target_pairs={{0,24},{1,97},{2,26},{3,99},{4,28},{5,101},{6,30},{7,103},{8,0},{9... | collective-permute-start | bytes 786440 | tf_op jit(solution)/shard_map/ppermute | solution.py:79
  142.7 2.7 %collective-permute-done.35 = bf16[32,4096]{1,0:T(8,128)(2,1)} collective-permute-done((bf16[32,4096]{1,0:T(8,128)(2,1)}, bf16[32,4096]{1,0:T(8,128)(2,1)}, u32[]{:S(2)}, u32[]{:S(2)}) %collective-permute-start.35) | collective-permute-done | bytes 262176 | tf_op jit(solution)/shard_map/ppermute | solution.py:79
  147.0 2.2 %collective-permute-start.37 = (bf16[8,8192]{1,0:T(8,128)(2,1)S(1)}, bf16[8,8192]{1,0:T(8,128)(2,1)S(1)}, u32[]{:S(2)}, u32[]{:S(2)}) collective-permute-start(bf16[8,8192]{1,0:T(8,128)(2,1)S(1)} %get-tuple-element.66), channel_id=1, source_target_pairs={{0,6},{1,7},{2,0},{3,1},{4,2},{5,3},{6,4},{7,5},{8,14},{9,15},{10,... | collective-permute-start | bytes 393224 | tf_op jit(solution)/shard_map/ppermute | solution.py:79
  150.8 2.9 %collective-permute-done.37 = bf16[8,8192]{1,0:T(8,128)(2,1)S(1)} collective-permute-done((bf16[8,8192]{1,0:T(8,128)(2,1)S(1)}, bf16[8,8192]{1,0:T(8,128)(2,1)S(1)}, u32[]{:S(2)}, u32[]{:S(2)}) %collective-permute-start.37) | collective-permute-done | bytes 131104 | tf_op jit(solution)/shard_map/ppermute | solution.py:79
  153.7 2.4 %collective-permute-done.38 = bf16[8,8192]{1,0:T(8,128)(2,1)S(1)} collective-permute-done((bf16[8,8192]{1,0:T(8,128)(2,1)S(1)}, bf16[8,8192]{1,0:T(8,128)(2,1)S(1)}, u32[]{:S(2)}, u32[]{:S(2)}) %collective-permute-start.38) | collective-permute-done | bytes 131104 | tf_op jit(solution)/shard_map/ppermute | solution.py:79
  (183 shorter events, 53.8 us)
Async XLA Ops:
  0.8 18.1 %collective-permute-start = (bf16[64,256]{1,0:T(8,128)(2,1)S(1)}, bf16[64,256]{1,0:T(8,128)(2,1)S(1)}, u32[]{:S(2)}, u32[]{:S(2)}) collective-permute-start(bf16[64,256]{1,0:T(8,128)(2,1)S(1)} %pad_add_fusion), channel_id=1, source_target_pairs={{0,8},{8,16},{16,24},{24,32},{32,40},{40,48},{48,56},{56,64},{64,7... | collective-permute-start | bytes 98312 | tf_op jit(solution)/shard_map/ppermute | solution.py:355
  2.4 16.4 %collective-permute-start.1 = (bf16[64,256]{1,0:T(8,128)(2,1)S(1)}, bf16[64,256]{1,0:T(8,128)(2,1)S(1)}, u32[]{:S(2)}, u32[]{:S(2)}) collective-permute-start(bf16[64,256]{1,0:T(8,128)(2,1)S(1)} %pad_add_fusion), channel_id=1, source_target_pairs={{0,16},{8,24},{16,32},{24,40},{32,48},{40,56},{48,64},{56,72},{64,... | collective-permute-start | bytes 98312 | tf_op jit(solution)/shard_map/ppermute | solution.py:355
  5.3 13.5 %collective-permute-start.2 = (bf16[64,256]{1,0:T(8,128)(2,1)S(1)}, bf16[64,256]{1,0:T(8,128)(2,1)S(1)}, u32[]{:S(2)}, u32[]{:S(2)}) collective-permute-start(bf16[64,256]{1,0:T(8,128)(2,1)S(1)} %pad_add_fusion), channel_id=1, source_target_pairs={{0,24},{8,32},{16,40},{24,48},{32,56},{40,64},{48,72},{56,80},{64,... | collective-permute-start | bytes 98312 | tf_op jit(solution)/shard_map/ppermute | solution.py:355
  11.3 16.2 %all-to-all-start = ((bf16[16,8,384]{2,1,0:T(8,128)(2,1)}), bf16[16,8,384]{2,1,0:T(8,128)(2,1)S(1)}, u32[]{:S(2)}, u32[]{:S(2)}) async-start(bf16[16,8,384]{2,1,0:T(8,128)(2,1)} %pad_maximum_fusion.7), calls=%async_computation | async-start | bytes 196608 | tf_op jit(solution)/shard_map/all_to_all | solution.py:372
  15.5 27.6 %collective-permute-start.10 = (bf16[1024,256]{1,0:T(8,128)(2,1)}, bf16[1024,256]{1,0:T(8,128)(2,1)S(1)}, u32[]{:S(2)}, u32[]{:S(2)}) collective-permute-start(bf16[1024,256]{1,0:T(8,128)(2,1)} %w0.1), channel_id=1, source_target_pairs={{0,1},{1,0},{2,3},{3,2},{4,5},{5,4},{6,7},{7,6},{8,9},{9,8},{10,11... | collective-permute-start | bytes 1572872 | tf_op jit(solution)/shard_map/ppermute | solution.py:66
  21.5 8.0 %collective-permute-start.4 = (bf16[32,2048]{1,0:T(8,128)(2,1)S(1)}, bf16[32,2048]{1,0:T(8,128)(2,1)S(1)}, u32[]{:S(2)}, u32[]{:S(2)}) collective-permute-start(bf16[32,2048]{1,0:T(8,128)(2,1)S(1)} %pad_maximum_fusion.5), channel_id=1, source_target_pairs={{0,8},{1,33},{2,10},{3,35},{4,12},{5,37},{6,14},{7,39},{8,16},{9,4... | collective-permute-start | bytes 393224 | tf_op jit(solution)/shard_map/ppermute | solution.py:72
  27.6 9.4 %collective-permute-start.11 = (bf16[1,16,8,128]{3,2,1,0:T(8,128)(2,1)S(1)}, bf16[1,16,8,128]{3,2,1,0:T(8,128)(2,1)S(1)}, u32[]{:S(2)}, u32[]{:S(2)}) collective-permute-start(bf16[1,16,8,128]{3,2,1,0:T(8,128)(2,1)S(1)} %slice_bitcast_fusion.8), channel_id=1, source_target_pairs={{0,2},{1,3},{2,0},{3,1},{4,6},{5,7},{6,4},{7,5},{8,10},{9,11},{10,... | collective-permute-start | bytes 98312 | tf_op jit(solution)/shard_map/ppermute | solution.py:375
  31.1 12.1 %collective-permute-start.7 = (bf16[128,2048]{1,0:T(8,128)(2,1)S(1)}, bf16[128,2048]{1,0:T(8,128)(2,1)S(1)}, u32[]{:S(2)}, u32[]{:S(2)}) collective-permute-start(bf16[128,2048]{1,0:T(8,128)(2,1)S(1)} %pad_maximum_fusion.p0), channel_id=1, source_target_pairs={{0,32},{1,9},{2,34},{3,11},{4,36},{5,13},{6,38},{7,15},{8,40},{9,1... | collective-permute-start | bytes 1572872 | tf_op jit(solution)/shard_map/ppermute | solution.py:72
  32.6 15.4 %collective-permute-start.8 = (bf16[128,2048]{1,0:T(8,128)(2,1)S(1)}, bf16[128,2048]{1,0:T(8,128)(2,1)S(1)}, u32[]{:S(2)}, u32[]{:S(2)}) collective-permute-start(bf16[128,2048]{1,0:T(8,128)(2,1)S(1)} %pad_maximum_fusion.p0), channel_id=1, source_target_pairs={{0,64},{1,17},{2,66},{3,19},{4,68},{5,21},{6,70},{7,23},{8,72},{9,... | collective-permute-start | bytes 1572872 | tf_op jit(solution)/shard_map/ppermute | solution.py:72
  35.3 12.8 %collective-permute-start.9 = (bf16[128,2048]{1,0:T(8,128)(2,1)S(1)}, bf16[128,2048]{1,0:T(8,128)(2,1)S(1)}, u32[]{:S(2)}, u32[]{:S(2)}) collective-permute-start(bf16[128,2048]{1,0:T(8,128)(2,1)S(1)} %pad_maximum_fusion.p0), channel_id=1, source_target_pairs={{0,96},{1,25},{2,98},{3,27},{4,100},{5,29},{6,102},{7,31},{8,104},... | collective-permute-start | bytes 1572872 | tf_op jit(solution)/shard_map/ppermute | solution.py:72
  50.8 10.4 %collective-permute-start.13 = (bf16[2,4,4,16,256]{4,3,2,1,0:T(8,128)(2,1)S(1)}, bf16[2,4,4,16,256]{4,3,2,1,0:T(8,128)(2,1)S(1)}, u32[]{:S(2)}, u32[]{:S(2)}) collective-permute-start(bf16[2,4,4,16,256]{4,3,2,1,0:T(8,128)(2,1)S(1)} %get-tuple-element.57), channel_id=1, source_target_pairs={{0,2},{1,3},{2,4},{3,5},{4,6},{5,7},{6,0},{7,1},{8,10},{9,11},{10,... | collective-permute-start | bytes 786440 | tf_op jit(solution)/shard_map/ppermute | solution.py:79
  52.7 13.5 %collective-permute-start.14 = (bf16[2,4,4,16,256]{4,3,2,1,0:T(8,128)(2,1)S(1)}, bf16[2,4,4,16,256]{4,3,2,1,0:T(8,128)(2,1)S(1)}, u32[]{:S(2)}, u32[]{:S(2)}) collective-permute-start(bf16[2,4,4,16,256]{4,3,2,1,0:T(8,128)(2,1)S(1)} %get-tuple-element.59), channel_id=1, source_target_pairs={{0,4},{1,5},{2,6},{3,7},{4,0},{5,1},{6,2},{7,3},{8,12},{9,13},{10,... | collective-permute-start | bytes 786440 | tf_op jit(solution)/shard_map/ppermute | solution.py:79
  56.3 9.9 %collective-permute-start.15 = (bf16[2,4,4,16,256]{4,3,2,1,0:T(8,128)(2,1)S(1)}, bf16[2,4,4,16,256]{4,3,2,1,0:T(8,128)(2,1)S(1)}, u32[]{:S(2)}, u32[]{:S(2)}) collective-permute-start(bf16[2,4,4,16,256]{4,3,2,1,0:T(8,128)(2,1)S(1)} %get-tuple-element.58), channel_id=1, source_target_pairs={{0,6},{1,7},{2,0},{3,1},{4,2},{5,3},{6,4},{7,5},{8,14},{9,15},{10,... | collective-permute-start | bytes 786440 | tf_op jit(solution)/shard_map/ppermute | solution.py:79
  66.4 7.7 %collective-permute-start.16 = (bf16[2,256,256]{2,1,0:T(8,128)(2,1)S(1)}, bf16[2,256,256]{2,1,0:T(8,128)(2,1)S(1)}, u32[]{:S(2)}, u32[]{:S(2)}) collective-permute-start(bf16[2,256,256]{2,1,0:T(8,128)(2,1)S(1)} %bitcast.147), channel_id=1, source_target_pairs={{0,8},{1,33},{2,10},{3,35},{4,12},{5,37},{6,14},{7,39},{8,16},{9,4... | collective-permute-start | bytes 786440 | tf_op jit(solution)/shard_map/ppermute | solution.py:72
  67.8 9.5 %collective-permute-start.17 = (bf16[2,256,256]{2,1,0:T(8,128)(2,1)S(1)}, bf16[2,256,256]{2,1,0:T(8,128)(2,1)S(1)}, u32[]{:S(2)}, u32[]{:S(2)}) collective-permute-start(bf16[2,256,256]{2,1,0:T(8,128)(2,1)S(1)} %bitcast.148), channel_id=1, source_target_pairs={{0,16},{1,65},{2,18},{3,67},{4,20},{5,69},{6,22},{7,71},{8,24},{9,... | collective-permute-start | bytes 786440 | tf_op jit(solution)/shard_map/ppermute | solution.py:72
  70.2 7.4 %collective-permute-start.18 = (bf16[2,256,256]{2,1,0:T(8,128)(2,1)S(1)}, bf16[2,256,256]{2,1,0:T(8,128)(2,1)S(1)}, u32[]{:S(2)}, u32[]{:S(2)}) collective-permute-start(bf16[2,256,256]{2,1,0:T(8,128)(2,1)S(1)} %bitcast.149), channel_id=1, source_target_pairs={{0,24},{1,97},{2,26},{3,99},{4,28},{5,101},{6,30},{7,103},{8,0},{9... | collective-permute-start | bytes 786440 | tf_op jit(solution)/shard_map/ppermute | solution.py:72
  77.9 11.5 %collective-permute-start.20 = (bf16[4,256,256]{2,1,0:T(8,128)(2,1)S(1)}, bf16[4,256,256]{2,1,0:T(8,128)(2,1)S(1)}, u32[]{:S(2)}, u32[]{:S(2)}) collective-permute-start(bf16[4,256,256]{2,1,0:T(8,128)(2,1)S(1)} %pad_maximum_fusion.2), channel_id=1, source_target_pairs={{0,97},{1,24},{2,99},{3,26},{4,101},{5,28},{6,103},{7,30},{8,105},... | collective-permute-start | bytes 1572872 | tf_op jit(solution)/shard_map/ppermute | solution.py:425
  80.5 10.5 %collective-permute-start.19 = (bf16[4,256,256]{2,1,0:T(8,128)(2,1)S(1)}, bf16[4,256,256]{2,1,0:T(8,128)(2,1)S(1)}, u32[]{:S(2)}, u32[]{:S(2)}) collective-permute-start(bf16[4,256,256]{2,1,0:T(8,128)(2,1)S(1)} %pad_maximum_fusion.1.refs_1_), channel_id=1, source_target_pairs={{0,32},{1,9},{2,34},{3,11},{4,36},{5,13},{6,38},{7,15},{8,40},{9,1... | collective-permute-start | bytes 1572872 | tf_op jit(solution)/shard_map/ppermute | solution.py:424
  80.6 15.4 %collective-permute-start.25 = (bf16[4,256,256]{2,1,0:T(8,128)(2,1)S(1)}, bf16[4,256,256]{2,1,0:T(8,128)(2,1)S(1)}, u32[]{:S(2)}, u32[]{:S(2)}) collective-permute-start(bf16[4,256,256]{2,1,0:T(8,128)(2,1)S(1)} %pad_maximum_fusion.2), channel_id=1, source_target_pairs={{0,33},{1,8},{2,35},{3,10},{4,37},{5,12},{6,39},{7,14},{8,41},{9,1... | collective-permute-start | bytes 1572872 | tf_op jit(solution)/shard_map/ppermute | solution.py:425
  81.7 14.2 %collective-permute-start.24 = (bf16[4,256,256]{2,1,0:T(8,128)(2,1)S(1)}, bf16[4,256,256]{2,1,0:T(8,128)(2,1)S(1)}, u32[]{:S(2)}, u32[]{:S(2)}) collective-permute-start(bf16[4,256,256]{2,1,0:T(8,128)(2,1)S(1)} %pad_maximum_fusion.1.refs_1_), channel_id=1, source_target_pairs={{0,96},{1,25},{2,98},{3,27},{4,100},{5,29},{6,102},{7,31},{8,104},... | collective-permute-start | bytes 1572872 | tf_op jit(solution)/shard_map/ppermute | solution.py:424
  91.0 11.2 %collective-permute-start.22 = (bf16[4,256,256]{2,1,0:T(8,128)(2,1)S(1)}, bf16[4,256,256]{2,1,0:T(8,128)(2,1)S(1)}, u32[]{:S(2)}, u32[]{:S(2)}) collective-permute-start(bf16[4,256,256]{2,1,0:T(8,128)(2,1)S(1)} %collective-permute-done.19.refs_1_), channel_id=1, source_target_pairs={{0,32},{1,9},{2,34},{3,11},{4,36},{5,13},{6,38},{7,15},{8,40},{9,1... | collective-permute-start | bytes 1572872 | tf_op jit(solution)/shard_map/ppermute | solution.py:434
  91.0 11.2 %collective-permute-start.23 = (bf16[4,256,256]{2,1,0:T(8,128)(2,1)S(1)}, bf16[4,256,256]{2,1,0:T(8,128)(2,1)S(1)}, u32[]{:S(2)}, u32[]{:S(2)}) collective-permute-start(bf16[4,256,256]{2,1,0:T(8,128)(2,1)S(1)} %collective-permute-done.20.refs_4_), channel_id=1, source_target_pairs={{0,24},{1,97},{2,26},{3,99},{4,28},{5,101},{6,30},{7,103},{8,0},{9... | collective-permute-start | bytes 1572872 | tf_op jit(solution)/shard_map/ppermute | solution.py:435
  105.9 13.9 %collective-permute-start.26 = (bf16[64,4096]{1,0:T(8,128)(2,1)S(1)}, bf16[64,4096]{1,0:T(8,128)(2,1)S(1)}, u32[]{:S(2)}, u32[]{:S(2)}) collective-permute-start(bf16[64,4096]{1,0:T(8,128)(2,1)S(1)} %get-tuple-element.43), channel_id=1, source_target_pairs={{0,8},{1,33},{2,10},{3,35},{4,12},{5,37},{6,14},{7,39},{8,16},{9,4... | collective-permute-start | bytes 1572872 | tf_op jit(solution)/shard_map/ppermute | solution.py:444
  108.0 12.0 %collective-permute-start.28 = (bf16[64,4096]{1,0:T(8,128)(2,1)S(1)}, bf16[64,4096]{1,0:T(8,128)(2,1)S(1)}, u32[]{:S(2)}, u32[]{:S(2)}) collective-permute-start(bf16[64,4096]{1,0:T(8,128)(2,1)S(1)} %get-tuple-element.45.refs_2_), channel_id=1, source_target_pairs={{0,96},{1,25},{2,98},{3,27},{4,100},{5,29},{6,102},{7,31},{8,104},... | collective-permute-start | bytes 1572872 | tf_op jit(solution)/shard_map/ppermute | solution.py:443
  111.0 11.6 %collective-permute-start.27 = (bf16[64,4096]{1,0:T(8,128)(2,1)S(1)}, bf16[64,4096]{1,0:T(8,128)(2,1)S(1)}, u32[]{:S(2)}, u32[]{:S(2)}) collective-permute-start(bf16[64,4096]{1,0:T(8,128)(2,1)S(1)} %get-tuple-element.46), channel_id=1, source_target_pairs={{0,32},{1,9},{2,34},{3,11},{4,36},{5,13},{6,38},{7,15},{8,40},{9,1... | collective-permute-start | bytes 1572872 | tf_op jit(solution)/shard_map/ppermute | solution.py:447
  111.9 10.9 %collective-permute-start.31 = (bf16[64,4096]{1,0:T(8,128)(2,1)S(1)}, bf16[64,4096]{1,0:T(8,128)(2,1)S(1)}, u32[]{:S(2)}, u32[]{:S(2)}) collective-permute-start(bf16[64,4096]{1,0:T(8,128)(2,1)S(1)} %get-tuple-element.49), channel_id=1, source_target_pairs={{33,0},{8,1},{35,2},{10,3},{37,4},{12,5},{39,6},{14,7},{41,8},{16,... | collective-permute-start | bytes 1572872 | tf_op jit(solution)/shard_map/ppermute | solution.py:448
  119.9 9.9 %collective-permute-start.32 = (bf16[64,4096]{1,0:T(8,128)(2,1)S(1)}, bf16[64,4096]{1,0:T(8,128)(2,1)S(1)}, u32[]{:S(2)}, u32[]{:S(2)}) collective-permute-start(bf16[64,4096]{1,0:T(8,128)(2,1)S(1)} %add_convert_fusion), channel_id=1, source_target_pairs={{97,0},{24,1},{99,2},{26,3},{101,4},{28,5},{103,6},{30,7},{105,8},... | collective-permute-start | bytes 1572872 | tf_op jit(solution)/shard_map/ppermute | solution.py:452
  120.2 9.7 %collective-permute-start.29 = (bf16[64,4096]{1,0:T(8,128)(2,1)S(1)}, bf16[64,4096]{1,0:T(8,128)(2,1)S(1)}, u32[]{:S(2)}, u32[]{:S(2)}) collective-permute-start(bf16[64,4096]{1,0:T(8,128)(2,1)S(1)} %add_convert_fusion.1), channel_id=1, source_target_pairs={{0,96},{1,25},{2,98},{3,27},{4,100},{5,29},{6,102},{7,31},{8,104},... | collective-permute-start | bytes 1572872 | tf_op jit(solution)/shard_map/ppermute | solution.py:451
  122.1 7.7 %collective-permute-start.30 = (bf16[64,4096]{1,0:T(8,128)(2,1)S(1)}, bf16[64,4096]{1,0:T(8,128)(2,1)S(1)}, u32[]{:S(2)}, u32[]{:S(2)}) collective-permute-start(bf16[64,4096]{1,0:T(8,128)(2,1)S(1)} %get-tuple-element.48), channel_id=1, source_target_pairs={{0,1},{1,0},{2,3},{3,2},{4,5},{5,4},{6,7},{7,6},{8,9},{9,8},{10,11... | collective-permute-start | bytes 1572872 | tf_op jit(solution)/shard_map/ppermute | solution.py:66
  131.0 10.4 %collective-permute-start.33 = (bf16[32,4096]{1,0:T(8,128)(2,1)}, bf16[32,4096]{1,0:T(8,128)(2,1)}, u32[]{:S(2)}, u32[]{:S(2)}) collective-permute-start(bf16[32,4096]{1,0:T(8,128)(2,1)} %get-tuple-element.52), channel_id=1, source_target_pairs={{0,24},{1,97},{2,26},{3,99},{4,28},{5,101},{6,30},{7,103},{8,0},{9... | collective-permute-start | bytes 786440 | tf_op jit(solution)/shard_map/ppermute | solution.py:79
  134.4 8.3 %collective-permute-start.34 = (bf16[32,4096]{1,0:T(8,128)(2,1)}, bf16[32,4096]{1,0:T(8,128)(2,1)}, u32[]{:S(2)}, u32[]{:S(2)}) collective-permute-start(bf16[32,4096]{1,0:T(8,128)(2,1)} %get-tuple-element.53), channel_id=1, source_target_pairs={{0,16},{1,65},{2,18},{3,67},{4,20},{5,69},{6,22},{7,71},{8,24},{9,... | collective-permute-start | bytes 786440 | tf_op jit(solution)/shard_map/ppermute | solution.py:79
  135.3 10.0 %collective-permute-start.35 = (bf16[32,4096]{1,0:T(8,128)(2,1)}, bf16[32,4096]{1,0:T(8,128)(2,1)}, u32[]{:S(2)}, u32[]{:S(2)}) collective-permute-start(bf16[32,4096]{1,0:T(8,128)(2,1)} %get-tuple-element.54), channel_id=1, source_target_pairs={{0,8},{1,33},{2,10},{3,35},{4,12},{5,37},{6,14},{7,39},{8,16},{9,4... | collective-permute-start | bytes 786440 | tf_op jit(solution)/shard_map/ppermute | solution.py:79
  (39 other events, 333.6 us)

commit v4 on v3

--- a/solution.py
+++ b/solution.py
@@ -369,11 +369,6 @@
     by_column = jnp.concatenate(
         [by_column, jnp.broadcast_to(codes[None], (n_ctx, token_count, HD))], axis=2
     )
-    by_column = lax.all_to_all(by_column, "ctx", split_axis=0, concat_axis=0, tiled=True)
-    residual_slab = by_column[:, :, :columns]
-    codes = by_column[None, :, :, columns:]
-    codes = jnp.concatenate([codes, lax.ppermute(codes, BOTH, z_exchange(1))], axis=0)
-    codes = jnp.concatenate([codes, lax.ppermute(codes, BOTH, z_exchange(2))], axis=0)
     weight_other = sibling(out_weight)
     stacked = jnp.concatenate(collected, axis=0)
     key_all = stacked[:, :width].reshape(-1, kv_local, HD)
@@ -398,7 +393,14 @@
     kept = jnp.where(core == 0, rows_0, rows_1)
     given = jnp.where(core == 0, rows_1, rows_0)
     paired = jnp.concatenate([kept, sibling(given)], axis=1)
-    line = jnp.concatenate(gathered(paired, first_axis), axis=0)
+    line = gathered(paired, first_axis)
+    by_column, line[1] = lax.optimization_barrier((by_column, line[1]))
+    by_column = lax.all_to_all(by_column, "ctx", split_axis=0, concat_axis=0, tiled=True)
+    residual_slab = by_column[:, :, :columns]
+    codes = by_column[None, :, :, columns:]
+    codes = jnp.concatenate([codes, lax.ppermute(codes, BOTH, z_exchange(1))], axis=0)
+    codes = jnp.concatenate([codes, lax.ppermute(codes, BOTH, z_exchange(2))], axis=0)
+    line = jnp.concatenate(line, axis=0)
     plane = gathered(line, second_axis)
 
     x_here, y_here = here // SIDE, here % SIDE

time: 160 us -> 156 us (0.975)
  starting transfers between devices: 63.8 us -> 62.1 us
    ppermute x9, waiting for transfers between devices: 12.3 us -> 9.06 us  [gathered(): got[d] = lax.ppermute(shard, BOTH, along(d))]
    ppermute x9, starting transfers between devices: 17.1 us -> 15.3 us  [gathered(): got[d] = lax.ppermute(shard, BOTH, along(d))]
    ppermute x1, waiting for transfers between devices: 0.01 us -> 1.85 us  [per_device(): lax.ppermute(codes, BOTH, z_exchange(1))]
    unnamed x61 -> x63, local copies, waits for them, and re-layouts: 6.96 us -> 6.91 us
  transfers between devices with their start and end apart: 41 -> 41, of which waited for: 22 -> 21; matrix products, arithmetic and copies ran while one was open for 7% -> 6% of each run, Pallas kernels for 6% -> 6%
where the time goes in v4:
time: 156 us; the launch traced here: 155 us
  starting transfers between devices  62.1 us (40%)
  waiting for transfers between devices  54.7 us (35%)
  Pallas kernels  17.3 us (11%)
  local copies, waits for them, and re-layouts  9.65 us (6%)
  other arithmetic  8.59 us (6%)
    ppermute x9, waiting for transfers between devices, dealt(): got[d] = lax.ppermute(blocks[d], BOTH, along(sign * d))  18.8 us
    ppermute x9, starting transfers between devices, gathered(): got[d] = lax.ppermute(shard, BOTH, along(d))  15.3 us
    ppermute x9, starting transfers between devices, dealt(): got[d] = lax.ppermute(blocks[d], BOTH, along(sign * d))  14.8 us
    ppermute x9, waiting for transfers between devices, gathered(): got[d] = lax.ppermute(shard, BOTH, along(d))  9.06 us
    ppermute x1, waiting for transfers between devices, per_device(): far_theirs = lax.ppermute(far_theirs, BOTH, first_axis(1))  7.83 us
    ppermute x1, waiting for transfers between devices, per_device(): other.append(lax.ppermute(front_theirs, BOTH, uncrossed(-1)))  6.97 us
    unnamed x63, local copies, waits for them, and re-layouts  6.91 us
    ppermute x3, starting transfers between devices, onward(): lax.ppermute(shard, 'ctx', [(i, (i + step) % n_ctx) for i in range(n_ctx)])  6.84 us
  transfers between devices with their start and end apart: 41, of which 21 were waited for; matrix products, arithmetic and copies ran while one was open for 6% of the time, Pallas kernels for 6%

profile of v4, /device:TPU:0, one launch (start us, length us, event | category | flops | bytes accessed | tf_op | source)
XLA Modules:
  0.0 155.0 jit_solution(2017489939891693379)
XLA Ops:
  2.4 2.9 %collective-permute-start.1 = (bf16[64,256]{1,0:T(8,128)(2,1)S(1)}, bf16[64,256]{1,0:T(8,128)(2,1)S(1)}, u32[]{:S(2)}, u32[]{:S(2)}) collective-permute-start(bf16[64,256]{1,0:T(8,128)(2,1)S(1)} %pad_add_fusion), channel_id=1, source_target_pairs={{0,16},{8,24},{16,32},{24,40},{32,48},{40,56},{48,64},{56,72},{64,... | collective-permute-start | bytes 98312 | tf_op jit(solution)/shard_map/ppermute | solution.py:355
  5.3 2.3 %collective-permute-start.2 = (bf16[64,256]{1,0:T(8,128)(2,1)S(1)}, bf16[64,256]{1,0:T(8,128)(2,1)S(1)}, u32[]{:S(2)}, u32[]{:S(2)}) collective-permute-start(bf16[64,256]{1,0:T(8,128)(2,1)S(1)} %pad_add_fusion), channel_id=1, source_target_pairs={{0,24},{8,32},{16,40},{24,48},{32,56},{40,64},{48,72},{56,80},{64,... | collective-permute-start | bytes 98312 | tf_op jit(solution)/shard_map/ppermute | solution.py:355
  20.2 3.0 %collective-permute-done.4 = bf16[32,2048]{1,0:T(8,128)(2,1)S(1)} collective-permute-done((bf16[32,2048]{1,0:T(8,128)(2,1)S(1)}, bf16[32,2048]{1,0:T(8,128)(2,1)S(1)}, u32[]{:S(2)}, u32[]{:S(2)}) %collective-permute-start.4) | collective-permute-done | bytes 131104 | tf_op jit(solution)/shard_map/ppermute | solution.py:72
  23.2 4.1 %all-to-all-start = ((bf16[16,8,384]{2,1,0:T(8,128)(2,1)}), bf16[16,8,384]{2,1,0:T(8,128)(2,1)S(1)}, u32[]{:S(2)}, u32[]{:S(2)}) async-start(bf16[16,8,384]{2,1,0:T(8,128)(2,1)} %pad_maximum_fusion.7), calls=%async_computation | async-start | bytes 196608 | tf_op jit(solution)/shard_map/all_to_all | solution.py:398
  27.4 2.0 %collective-permute-start.7 = (bf16[128,2048]{1,0:T(8,128)(2,1)S(1)}, bf16[128,2048]{1,0:T(8,128)(2,1)S(1)}, u32[]{:S(2)}, u32[]{:S(2)}) collective-permute-start(bf16[128,2048]{1,0:T(8,128)(2,1)S(1)} %pad_maximum_fusion.p0), channel_id=1, source_target_pairs={{0,32},{1,9},{2,34},{3,11},{4,36},{5,13},{6,38},{7,15},{8,40},{9,1... | collective-permute-start | bytes 1572872 | tf_op jit(solution)/shard_map/ppermute | solution.py:72
  29.4 2.7 %collective-permute-start.8 = (bf16[128,2048]{1,0:T(8,128)(2,1)S(1)}, bf16[128,2048]{1,0:T(8,128)(2,1)S(1)}, u32[]{:S(2)}, u32[]{:S(2)}) collective-permute-start(bf16[128,2048]{1,0:T(8,128)(2,1)S(1)} %pad_maximum_fusion.p0), channel_id=1, source_target_pairs={{0,64},{1,17},{2,66},{3,19},{4,68},{5,21},{6,70},{7,23},{8,72},{9,... | collective-permute-start | bytes 1572872 | tf_op jit(solution)/shard_map/ppermute | solution.py:72
  35.2 1.9 %collective-permute-start.11 = (bf16[1,16,8,128]{3,2,1,0:T(8,128)(2,1)S(1)}, bf16[1,16,8,128]{3,2,1,0:T(8,128)(2,1)S(1)}, u32[]{:S(2)}, u32[]{:S(2)}) collective-permute-start(bf16[1,16,8,128]{3,2,1,0:T(8,128)(2,1)S(1)} %slice_bitcast_fusion.8), channel_id=1, source_target_pairs={{0,2},{1,3},{2,0},{3,1},{4,6},{5,7},{6,4},{7,5},{8,10},{9,11},{10,... | collective-permute-start | bytes 98312 | tf_op jit(solution)/shard_map/ppermute | solution.py:401
  39.1 4.0 %collective-permute-start.12 = (bf16[2,16,8,128]{3,2,1,0:T(8,128)(2,1)S(1)}, bf16[2,16,8,128]{3,2,1,0:T(8,128)(2,1)S(1)}, u32[]{:S(2)}, u32[]{:S(2)}) collective-permute-start(bf16[2,16,8,128]{3,2,1,0:T(8,128)(2,1)S(1)} %pad_maximum_fusion.8), channel_id=1, source_target_pairs={{0,4},{1,5},{2,6},{3,7},{4,0},{5,1},{6,2},{7,3},{8,12},{9,13},{10,... | collective-permute-start | bytes 196616 | tf_op jit(solution)/shard_map/ppermute | solution.py:402
  43.1 2.2 %collective-permute-done.12 = bf16[2,16,8,128]{3,2,1,0:T(8,128)(2,1)S(1)} collective-permute-done((bf16[2,16,8,128]{3,2,1,0:T(8,128)(2,1)S(1)}, bf16[2,16,8,128]{3,2,1,0:T(8,128)(2,1)S(1)}, u32[]{:S(2)}, u32[]{:S(2)}) %collective-permute-start.12) | collective-permute-done | bytes 65568 | tf_op jit(solution)/shard_map/ppermute | solution.py:402
  45.4 2.6 %shard_map.118 = bf16[4,2,4,4,16,256]{5,4,3,2,1,0:T(8,128)(2,1)S(1)} custom-call(s32[3]{0:T(128)S(1)} %pad_add_fusion.2.where.refs_10_, s32[16]{0:T(128)S(1)} %select_n.226.place, bf16[128,2048]{1,0:T(8,128)(2,1)S(1)} %pad_maximum_fusion.p0, bf16[128,2048]{1,0:T(8,128)(2,1)S(1)} %collective-permute-done.7.p1, ...), custom_call_target="tpu_custom_call" | custom-call | flops 671088640 | bytes 6291456 | tf_op jit(solution)/shard_map/pallas_call | solution.py:131
  49.7 3.6 %collective-permute-start.14 = (bf16[2,4,4,16,256]{4,3,2,1,0:T(8,128)(2,1)S(1)}, bf16[2,4,4,16,256]{4,3,2,1,0:T(8,128)(2,1)S(1)}, u32[]{:S(2)}, u32[]{:S(2)}) collective-permute-start(bf16[2,4,4,16,256]{4,3,2,1,0:T(8,128)(2,1)S(1)} %get-tuple-element.63), channel_id=1, source_target_pairs={{0,4},{1,5},{2,6},{3,7},{4,0},{5,1},{6,2},{7,3},{8,12},{9,13},{10,... | collective-permute-start | bytes 786440 | tf_op jit(solution)/shard_map/ppermute | solution.py:79
  54.3 4.7 %collective-permute-done.13 = bf16[2,4,4,16,256]{4,3,2,1,0:T(8,128)(2,1)S(1)} collective-permute-done((bf16[2,4,4,16,256]{4,3,2,1,0:T(8,128)(2,1)S(1)}, bf16[2,4,4,16,256]{4,3,2,1,0:T(8,128)(2,1)S(1)}, u32[]{:S(2)}, u32[]{:S(2)}) %collective-permute-start.13) | collective-permute-done | bytes 262176 | tf_op jit(solution)/shard_map/ppermute | solution.py:79
  59.0 3.2 %collective-permute-done.14 = bf16[2,4,4,16,256]{4,3,2,1,0:T(8,128)(2,1)S(1)} collective-permute-done((bf16[2,4,4,16,256]{4,3,2,1,0:T(8,128)(2,1)S(1)}, bf16[2,4,4,16,256]{4,3,2,1,0:T(8,128)(2,1)S(1)}, u32[]{:S(2)}, u32[]{:S(2)}) %collective-permute-start.14) | collective-permute-done | bytes 262176 | tf_op jit(solution)/shard_map/ppermute | solution.py:79
  63.8 2.1 %collective-permute-start.17 = (bf16[2,256,256]{2,1,0:T(8,128)(2,1)S(1)}, bf16[2,256,256]{2,1,0:T(8,128)(2,1)S(1)}, u32[]{:S(2)}, u32[]{:S(2)}) collective-permute-start(bf16[2,256,256]{2,1,0:T(8,128)(2,1)S(1)} %bitcast.148), channel_id=1, source_target_pairs={{0,16},{1,65},{2,18},{3,67},{4,20},{5,69},{6,22},{7,71},{8,24},{9,... | collective-permute-start | bytes 786440 | tf_op jit(solution)/shard_map/ppermute | solution.py:72
  67.5 2.5 %collective-permute-done.16 = bf16[2,256,256]{2,1,0:T(8,128)(2,1)S(1)} collective-permute-done((bf16[2,256,256]{2,1,0:T(8,128)(2,1)S(1)}, bf16[2,256,256]{2,1,0:T(8,128)(2,1)S(1)}, u32[]{:S(2)}, u32[]{:S(2)}) %collective-permute-start.16) | collective-permute-done | bytes 262176 | tf_op jit(solution)/shard_map/ppermute | solution.py:72
  70.0 3.1 %collective-permute-done.17 = bf16[2,256,256]{2,1,0:T(8,128)(2,1)S(1)} collective-permute-done((bf16[2,256,256]{2,1,0:T(8,128)(2,1)S(1)}, bf16[2,256,256]{2,1,0:T(8,128)(2,1)S(1)}, u32[]{:S(2)}, u32[]{:S(2)}) %collective-permute-start.17) | collective-permute-done | bytes 262176 | tf_op jit(solution)/shard_map/ppermute | solution.py:72
  73.8 2.3 %collective-permute-start.20 = (bf16[4,256,256]{2,1,0:T(8,128)(2,1)S(1)}, bf16[4,256,256]{2,1,0:T(8,128)(2,1)S(1)}, u32[]{:S(2)}, u32[]{:S(2)}) collective-permute-start(bf16[4,256,256]{2,1,0:T(8,128)(2,1)S(1)} %pad_maximum_fusion.2), channel_id=1, source_target_pairs={{0,97},{1,24},{2,99},{3,26},{4,101},{5,28},{6,103},{7,30},{8,105},... | collective-permute-start | bytes 1572872 | tf_op jit(solution)/shard_map/ppermute | solution.py:427
  77.6 2.2 %collective-permute-start.24 = (bf16[4,256,256]{2,1,0:T(8,128)(2,1)S(1)}, bf16[4,256,256]{2,1,0:T(8,128)(2,1)S(1)}, u32[]{:S(2)}, u32[]{:S(2)}) collective-permute-start(bf16[4,256,256]{2,1,0:T(8,128)(2,1)S(1)} %pad_maximum_fusion.1.refs_1_), channel_id=1, source_target_pairs={{0,96},{1,25},{2,98},{3,27},{4,100},{5,29},{6,102},{7,31},{8,104},... | collective-permute-start | bytes 1572872 | tf_op jit(solution)/shard_map/ppermute | solution.py:426
  79.9 3.0 %copy-done.1 = bf16[1,4096,768]{2,1,0:T(8,128)(2,1)S(1)} copy-done((bf16[1,4096,768]{2,1,0:T(8,128)(2,1)S(1)}, bf16[1,4096,768]{2,1,0:T(8,128)(2,1)}, u32[]{:S(2)}) %copy-start.1) | copy-done | bytes 6291480
  82.9 2.4 %shard_map.119 = (f32[512,768]{1,0:T(8,128)S(1)}, f32[512,768]{1,0:T(8,128)S(1)}, f32[512,128]{1,0:T(8,128)S(1)}) custom-call(s32[8]{0:T(128)S(1)} %pad_add_fusion.3.refs_0_, bf16[4,256,256]{2,1,0:T(8,128)(2,1)S(1)} %pad_maximum_fusion.1.refs_1_, bf16[4,256,256]{2,1,0:T(8,128)(2,1)S(1)} %collective-permute-done.21.refs_2_, f32[16,1,256]{2,1,0:T(1,128)S(1)} %bitcast.139, ...), custom_call_target="tpu_custom_call" | custom-call | flops 1610612736 | bytes 3145728 | tf_op jit(solution)/shard_map/pallas_call | solution.py:185
  86.7 2.7 %collective-permute-start.23 = (bf16[4,256,256]{2,1,0:T(8,128)(2,1)S(1)}, bf16[4,256,256]{2,1,0:T(8,128)(2,1)S(1)}, u32[]{:S(2)}, u32[]{:S(2)}) collective-permute-start(bf16[4,256,256]{2,1,0:T(8,128)(2,1)S(1)} %collective-permute-done.20.refs_4_), channel_id=1, source_target_pairs={{0,24},{1,97},{2,26},{3,99},{4,28},{5,101},{6,30},{7,103},{8,0},{9... | collective-permute-start | bytes 1572872 | tf_op jit(solution)/shard_map/ppermute | solution.py:437
  89.5 2.4 %collective-permute-done.25.refs_3_ = bf16[4,256,256]{2,1,0:T(8,128)(2,1)S(1)} collective-permute-done((bf16[4,256,256]{2,1,0:T(8,128)(2,1)S(1)}, bf16[4,256,256]{2,1,0:T(8,128)(2,1)S(1)}, u32[]{:S(2)}, u32[]{:S(2)}) %collective-permute-start.25) | collective-permute-done | bytes 524320 | tf_op jit(solution)/shard_map/ppermute | solution.py:427
  91.9 4.2 %shard_map.120 = (f32[512,768]{1,0:T(8,128)S(1)}, f32[512,768]{1,0:T(8,128)S(1)}, f32[512,128]{1,0:T(8,128)S(1)}) custom-call(s32[16]{0:T(128)S(1)} %pad_add_fusion.4.refs_0_, bf16[4,256,256]{2,1,0:T(8,128)(2,1)S(1)} %collective-permute-done.19.refs_1_, ...), custom_call_target="tpu_custom_call", output_to_operand_aliasing={{0}: (8, {}), {1}: (9, {}), {2}: (10, {})} | custom-call | flops 3221225472 | bytes 6291456 | tf_op jit(solution)/shard_map/pallas_call | solution.py:185
  97.9 3.7 %shard_map.121 = (bf16[64,4096]{1,0:T(8,128)(2,1)S(1)}, bf16[64,4096]{1,0:T(8,128)(2,1)S(1)}, bf16[512,768]{1,0:T(8,128)(2,1)S(1)}) custom-call(s32[8]{0:T(128)S(1)} %pad_add_fusion.1.refs_0_, bf16[4,256,256]{2,1,0:T(8,128)(2,1)S(1)} %collective-permute-done.22.refs_1_, bf16[4,256,256]{2,1,0:T(8,128)(2,1)S(1)} %collective-permute-done.23.refs_2_, ...), custom_call_target="tpu_custom_call" | custom-call | flops 2415919104 | bytes 9437184 | tf_op jit(solution)/shard_map/pallas_call | solution.py:231
  101.6 2.1 %collective-permute-start.26 = (bf16[64,4096]{1,0:T(8,128)(2,1)S(1)}, bf16[64,4096]{1,0:T(8,128)(2,1)S(1)}, u32[]{:S(2)}, u32[]{:S(2)}) collective-permute-start(bf16[64,4096]{1,0:T(8,128)(2,1)S(1)} %get-tuple-element.47), channel_id=1, source_target_pairs={{0,8},{1,33},{2,10},{3,35},{4,12},{5,37},{6,14},{7,39},{8,16},{9,4... | collective-permute-start | bytes 1572872 | tf_op jit(solution)/shard_map/ppermute | solution.py:446
  107.6 7.8 %collective-permute-done.26.refs_2_ = bf16[64,4096]{1,0:T(8,128)(2,1)S(1)} collective-permute-done((bf16[64,4096]{1,0:T(8,128)(2,1)S(1)}, bf16[64,4096]{1,0:T(8,128)(2,1)S(1)}, u32[]{:S(2)}, u32[]{:S(2)}) %collective-permute-start.26) | collective-permute-done | bytes 524320 | tf_op jit(solution)/shard_map/ppermute | solution.py:446
  118.5 7.0 %collective-permute-done.32.refs_5_ = bf16[64,4096]{1,0:T(8,128)(2,1)S(1)} collective-permute-done((bf16[64,4096]{1,0:T(8,128)(2,1)S(1)}, bf16[64,4096]{1,0:T(8,128)(2,1)S(1)}, u32[]{:S(2)}, u32[]{:S(2)}) %collective-permute-start.32) | collective-permute-done | bytes 524320 | tf_op jit(solution)/shard_map/ppermute | solution.py:454
  126.6 3.6 %collective-permute-start.33 = (bf16[32,4096]{1,0:T(8,128)(2,1)}, bf16[32,4096]{1,0:T(8,128)(2,1)}, u32[]{:S(2)}, u32[]{:S(2)}) collective-permute-start(bf16[32,4096]{1,0:T(8,128)(2,1)} %get-tuple-element.56), channel_id=1, source_target_pairs={{0,24},{1,97},{2,26},{3,99},{4,28},{5,101},{6,30},{7,103},{8,0},{9... | collective-permute-start | bytes 786440 | tf_op jit(solution)/shard_map/ppermute | solution.py:79
  138.5 2.7 %collective-permute-done.35 = bf16[32,4096]{1,0:T(8,128)(2,1)} collective-permute-done((bf16[32,4096]{1,0:T(8,128)(2,1)}, bf16[32,4096]{1,0:T(8,128)(2,1)}, u32[]{:S(2)}, u32[]{:S(2)}) %collective-permute-start.35) | collective-permute-done | bytes 262176 | tf_op jit(solution)/shard_map/ppermute | solution.py:79
  142.9 2.2 %collective-permute-start.37 = (bf16[8,8192]{1,0:T(8,128)(2,1)S(1)}, bf16[8,8192]{1,0:T(8,128)(2,1)S(1)}, u32[]{:S(2)}, u32[]{:S(2)}) collective-permute-start(bf16[8,8192]{1,0:T(8,128)(2,1)S(1)} %get-tuple-element.70), channel_id=1, source_target_pairs={{0,6},{1,7},{2,0},{3,1},{4,2},{5,3},{6,4},{7,5},{8,14},{9,15},{10,... | collective-permute-start | bytes 393224 | tf_op jit(solution)/shard_map/ppermute | solution.py:79
  146.6 2.9 %collective-permute-done.37 = bf16[8,8192]{1,0:T(8,128)(2,1)S(1)} collective-permute-done((bf16[8,8192]{1,0:T(8,128)(2,1)S(1)}, bf16[8,8192]{1,0:T(8,128)(2,1)S(1)}, u32[]{:S(2)}, u32[]{:S(2)}) %collective-permute-start.37) | collective-permute-done | bytes 131104 | tf_op jit(solution)/shard_map/ppermute | solution.py:79
  149.5 2.4 %collective-permute-done.38 = bf16[8,8192]{1,0:T(8,128)(2,1)S(1)} collective-permute-done((bf16[8,8192]{1,0:T(8,128)(2,1)S(1)}, bf16[8,8192]{1,0:T(8,128)(2,1)S(1)}, u32[]{:S(2)}, u32[]{:S(2)}) %collective-permute-start.38) | collective-permute-done | bytes 131104 | tf_op jit(solution)/shard_map/ppermute | solution.py:79
  (185 shorter events, 53.7 us)
Async XLA Ops:
  0.8 12.1 %collective-permute-start = (bf16[64,256]{1,0:T(8,128)(2,1)S(1)}, bf16[64,256]{1,0:T(8,128)(2,1)S(1)}, u32[]{:S(2)}, u32[]{:S(2)}) collective-permute-start(bf16[64,256]{1,0:T(8,128)(2,1)S(1)} %pad_add_fusion), channel_id=1, source_target_pairs={{0,8},{8,16},{16,24},{24,32},{32,40},{40,48},{48,56},{56,64},{64,7... | collective-permute-start | bytes 98312 | tf_op jit(solution)/shard_map/ppermute | solution.py:355
  2.4 10.5 %collective-permute-start.1 = (bf16[64,256]{1,0:T(8,128)(2,1)S(1)}, bf16[64,256]{1,0:T(8,128)(2,1)S(1)}, u32[]{:S(2)}, u32[]{:S(2)}) collective-permute-start(bf16[64,256]{1,0:T(8,128)(2,1)S(1)} %pad_add_fusion), channel_id=1, source_target_pairs={{0,16},{8,24},{16,32},{24,40},{32,48},{40,56},{48,64},{56,72},{64,... | collective-permute-start | bytes 98312 | tf_op jit(solution)/shard_map/ppermute | solution.py:355
  7.6 37.7 %collective-permute-start.10 = (bf16[1024,256]{1,0:T(8,128)(2,1)}, bf16[1024,256]{1,0:T(8,128)(2,1)S(1)}, u32[]{:S(2)}, u32[]{:S(2)}) collective-permute-start(bf16[1024,256]{1,0:T(8,128)(2,1)} %w0.1), channel_id=1, source_target_pairs={{0,1},{1,0},{2,3},{3,2},{4,5},{5,4},{6,7},{7,6},{8,9},{9,8},{10,11... | collective-permute-start | bytes 1572872 | tf_op jit(solution)/shard_map/ppermute | solution.py:66
  15.6 7.7 %collective-permute-start.4 = (bf16[32,2048]{1,0:T(8,128)(2,1)S(1)}, bf16[32,2048]{1,0:T(8,128)(2,1)S(1)}, u32[]{:S(2)}, u32[]{:S(2)}) collective-permute-start(bf16[32,2048]{1,0:T(8,128)(2,1)S(1)} %pad_maximum_fusion.5), channel_id=1, source_target_pairs={{0,8},{1,33},{2,10},{3,35},{4,12},{5,37},{6,14},{7,39},{8,16},{9,4... | collective-permute-start | bytes 393224 | tf_op jit(solution)/shard_map/ppermute | solution.py:72
  16.3 11.0 %collective-permute-start.5 = (bf16[32,2048]{1,0:T(8,128)(2,1)S(1)}, bf16[32,2048]{1,0:T(8,128)(2,1)S(1)}, u32[]{:S(2)}, u32[]{:S(2)}) collective-permute-start(bf16[32,2048]{1,0:T(8,128)(2,1)S(1)} %pad_maximum_fusion.5), channel_id=1, source_target_pairs={{0,16},{1,65},{2,18},{3,67},{4,20},{5,69},{6,22},{7,71},{8,24},{9,... | collective-permute-start | bytes 393224 | tf_op jit(solution)/shard_map/ppermute | solution.py:72
  17.9 9.5 %collective-permute-start.6 = (bf16[32,2048]{1,0:T(8,128)(2,1)S(1)}, bf16[32,2048]{1,0:T(8,128)(2,1)S(1)}, u32[]{:S(2)}, u32[]{:S(2)}) collective-permute-start(bf16[32,2048]{1,0:T(8,128)(2,1)S(1)} %pad_maximum_fusion.5), channel_id=1, source_target_pairs={{0,24},{1,97},{2,26},{3,99},{4,28},{5,101},{6,30},{7,103},{8,0},{9... | collective-permute-start | bytes 393224 | tf_op jit(solution)/shard_map/ppermute | solution.py:72
  23.2 11.9 %all-to-all-start = ((bf16[16,8,384]{2,1,0:T(8,128)(2,1)}), bf16[16,8,384]{2,1,0:T(8,128)(2,1)S(1)}, u32[]{:S(2)}, u32[]{:S(2)}) async-start(bf16[16,8,384]{2,1,0:T(8,128)(2,1)} %pad_maximum_fusion.7), calls=%async_computation | async-start | bytes 196608 | tf_op jit(solution)/shard_map/all_to_all | solution.py:398
  27.4 17.9 %collective-permute-start.7 = (bf16[128,2048]{1,0:T(8,128)(2,1)S(1)}, bf16[128,2048]{1,0:T(8,128)(2,1)S(1)}, u32[]{:S(2)}, u32[]{:S(2)}) collective-permute-start(bf16[128,2048]{1,0:T(8,128)(2,1)S(1)} %pad_maximum_fusion.p0), channel_id=1, source_target_pairs={{0,32},{1,9},{2,34},{3,11},{4,36},{5,13},{6,38},{7,15},{8,40},{9,1... | collective-permute-start | bytes 1572872 | tf_op jit(solution)/shard_map/ppermute | solution.py:72
  29.4 15.9 %collective-permute-start.8 = (bf16[128,2048]{1,0:T(8,128)(2,1)S(1)}, bf16[128,2048]{1,0:T(8,128)(2,1)S(1)}, u32[]{:S(2)}, u32[]{:S(2)}) collective-permute-start(bf16[128,2048]{1,0:T(8,128)(2,1)S(1)} %pad_maximum_fusion.p0), channel_id=1, source_target_pairs={{0,64},{1,17},{2,66},{3,19},{4,68},{5,21},{6,70},{7,23},{8,72},{9,... | collective-permute-start | bytes 1572872 | tf_op jit(solution)/shard_map/ppermute | solution.py:72
  32.1 13.2 %collective-permute-start.9 = (bf16[128,2048]{1,0:T(8,128)(2,1)S(1)}, bf16[128,2048]{1,0:T(8,128)(2,1)S(1)}, u32[]{:S(2)}, u32[]{:S(2)}) collective-permute-start(bf16[128,2048]{1,0:T(8,128)(2,1)S(1)} %pad_maximum_fusion.p0), channel_id=1, source_target_pairs={{0,96},{1,25},{2,98},{3,27},{4,100},{5,29},{6,102},{7,31},{8,104},... | collective-permute-start | bytes 1572872 | tf_op jit(solution)/shard_map/ppermute | solution.py:72
  48.0 10.9 %collective-permute-start.13 = (bf16[2,4,4,16,256]{4,3,2,1,0:T(8,128)(2,1)S(1)}, bf16[2,4,4,16,256]{4,3,2,1,0:T(8,128)(2,1)S(1)}, u32[]{:S(2)}, u32[]{:S(2)}) collective-permute-start(bf16[2,4,4,16,256]{4,3,2,1,0:T(8,128)(2,1)S(1)} %get-tuple-element.61), channel_id=1, source_target_pairs={{0,2},{1,3},{2,4},{3,5},{4,6},{5,7},{6,0},{7,1},{8,10},{9,11},{10,... | collective-permute-start | bytes 786440 | tf_op jit(solution)/shard_map/ppermute | solution.py:79
  49.7 12.5 %collective-permute-start.14 = (bf16[2,4,4,16,256]{4,3,2,1,0:T(8,128)(2,1)S(1)}, bf16[2,4,4,16,256]{4,3,2,1,0:T(8,128)(2,1)S(1)}, u32[]{:S(2)}, u32[]{:S(2)}) collective-permute-start(bf16[2,4,4,16,256]{4,3,2,1,0:T(8,128)(2,1)S(1)} %get-tuple-element.63), channel_id=1, source_target_pairs={{0,4},{1,5},{2,6},{3,7},{4,0},{5,1},{6,2},{7,3},{8,12},{9,13},{10,... | collective-permute-start | bytes 786440 | tf_op jit(solution)/shard_map/ppermute | solution.py:79
  53.3 8.9 %collective-permute-start.15 = (bf16[2,4,4,16,256]{4,3,2,1,0:T(8,128)(2,1)S(1)}, bf16[2,4,4,16,256]{4,3,2,1,0:T(8,128)(2,1)S(1)}, u32[]{:S(2)}, u32[]{:S(2)}) collective-permute-start(bf16[2,4,4,16,256]{4,3,2,1,0:T(8,128)(2,1)S(1)} %get-tuple-element.62), channel_id=1, source_target_pairs={{0,6},{1,7},{2,0},{3,1},{4,2},{5,3},{6,4},{7,5},{8,14},{9,15},{10,... | collective-permute-start | bytes 786440 | tf_op jit(solution)/shard_map/ppermute | solution.py:79
  62.3 7.7 %collective-permute-start.16 = (bf16[2,256,256]{2,1,0:T(8,128)(2,1)S(1)}, bf16[2,256,256]{2,1,0:T(8,128)(2,1)S(1)}, u32[]{:S(2)}, u32[]{:S(2)}) collective-permute-start(bf16[2,256,256]{2,1,0:T(8,128)(2,1)S(1)} %bitcast.147), channel_id=1, source_target_pairs={{0,8},{1,33},{2,10},{3,35},{4,12},{5,37},{6,14},{7,39},{8,16},{9,4... | collective-permute-start | bytes 786440 | tf_op jit(solution)/shard_map/ppermute | solution.py:72
  63.8 9.3 %collective-permute-start.17 = (bf16[2,256,256]{2,1,0:T(8,128)(2,1)S(1)}, bf16[2,256,256]{2,1,0:T(8,128)(2,1)S(1)}, u32[]{:S(2)}, u32[]{:S(2)}) collective-permute-start(bf16[2,256,256]{2,1,0:T(8,128)(2,1)S(1)} %bitcast.148), channel_id=1, source_target_pairs={{0,16},{1,65},{2,18},{3,67},{4,20},{5,69},{6,22},{7,71},{8,24},{9,... | collective-permute-start | bytes 786440 | tf_op jit(solution)/shard_map/ppermute | solution.py:72
  65.9 7.7 %collective-permute-start.18 = (bf16[2,256,256]{2,1,0:T(8,128)(2,1)S(1)}, bf16[2,256,256]{2,1,0:T(8,128)(2,1)S(1)}, u32[]{:S(2)}, u32[]{:S(2)}) collective-permute-start(bf16[2,256,256]{2,1,0:T(8,128)(2,1)S(1)} %bitcast.149), channel_id=1, source_target_pairs={{0,24},{1,97},{2,26},{3,99},{4,28},{5,101},{6,30},{7,103},{8,0},{9... | collective-permute-start | bytes 786440 | tf_op jit(solution)/shard_map/ppermute | solution.py:72
  73.8 11.5 %collective-permute-start.20 = (bf16[4,256,256]{2,1,0:T(8,128)(2,1)S(1)}, bf16[4,256,256]{2,1,0:T(8,128)(2,1)S(1)}, u32[]{:S(2)}, u32[]{:S(2)}) collective-permute-start(bf16[4,256,256]{2,1,0:T(8,128)(2,1)S(1)} %pad_maximum_fusion.2), channel_id=1, source_target_pairs={{0,97},{1,24},{2,99},{3,26},{4,101},{5,28},{6,103},{7,30},{8,105},... | collective-permute-start | bytes 1572872 | tf_op jit(solution)/shard_map/ppermute | solution.py:427
  76.2 10.5 %collective-permute-start.19 = (bf16[4,256,256]{2,1,0:T(8,128)(2,1)S(1)}, bf16[4,256,256]{2,1,0:T(8,128)(2,1)S(1)}, u32[]{:S(2)}, u32[]{:S(2)}) collective-permute-start(bf16[4,256,256]{2,1,0:T(8,128)(2,1)S(1)} %pad_maximum_fusion.1.refs_1_), channel_id=1, source_target_pairs={{0,32},{1,9},{2,34},{3,11},{4,36},{5,13},{6,38},{7,15},{8,40},{9,1... | collective-permute-start | bytes 1572872 | tf_op jit(solution)/shard_map/ppermute | solution.py:426
  76.3 15.6 %collective-permute-start.25 = (bf16[4,256,256]{2,1,0:T(8,128)(2,1)S(1)}, bf16[4,256,256]{2,1,0:T(8,128)(2,1)S(1)}, u32[]{:S(2)}, u32[]{:S(2)}) collective-permute-start(bf16[4,256,256]{2,1,0:T(8,128)(2,1)S(1)} %pad_maximum_fusion.2), channel_id=1, source_target_pairs={{0,33},{1,8},{2,35},{3,10},{4,37},{5,12},{6,39},{7,14},{8,41},{9,1... | collective-permute-start | bytes 1572872 | tf_op jit(solution)/shard_map/ppermute | solution.py:427
  77.6 14.3 %collective-permute-start.24 = (bf16[4,256,256]{2,1,0:T(8,128)(2,1)S(1)}, bf16[4,256,256]{2,1,0:T(8,128)(2,1)S(1)}, u32[]{:S(2)}, u32[]{:S(2)}) collective-permute-start(bf16[4,256,256]{2,1,0:T(8,128)(2,1)S(1)} %pad_maximum_fusion.1.refs_1_), channel_id=1, source_target_pairs={{0,96},{1,25},{2,98},{3,27},{4,100},{5,29},{6,102},{7,31},{8,104},... | collective-permute-start | bytes 1572872 | tf_op jit(solution)/shard_map/ppermute | solution.py:426
  86.7 11.2 %collective-permute-start.22 = (bf16[4,256,256]{2,1,0:T(8,128)(2,1)S(1)}, bf16[4,256,256]{2,1,0:T(8,128)(2,1)S(1)}, u32[]{:S(2)}, u32[]{:S(2)}) collective-permute-start(bf16[4,256,256]{2,1,0:T(8,128)(2,1)S(1)} %collective-permute-done.19.refs_1_), channel_id=1, source_target_pairs={{0,32},{1,9},{2,34},{3,11},{4,36},{5,13},{6,38},{7,15},{8,40},{9,1... | collective-permute-start | bytes 1572872 | tf_op jit(solution)/shard_map/ppermute | solution.py:436
  86.7 11.2 %collective-permute-start.23 = (bf16[4,256,256]{2,1,0:T(8,128)(2,1)S(1)}, bf16[4,256,256]{2,1,0:T(8,128)(2,1)S(1)}, u32[]{:S(2)}, u32[]{:S(2)}) collective-permute-start(bf16[4,256,256]{2,1,0:T(8,128)(2,1)S(1)} %collective-permute-done.20.refs_4_), channel_id=1, source_target_pairs={{0,24},{1,97},{2,26},{3,99},{4,28},{5,101},{6,30},{7,103},{8,0},{9... | collective-permute-start | bytes 1572872 | tf_op jit(solution)/shard_map/ppermute | solution.py:437
  101.6 13.9 %collective-permute-start.26 = (bf16[64,4096]{1,0:T(8,128)(2,1)S(1)}, bf16[64,4096]{1,0:T(8,128)(2,1)S(1)}, u32[]{:S(2)}, u32[]{:S(2)}) collective-permute-start(bf16[64,4096]{1,0:T(8,128)(2,1)S(1)} %get-tuple-element.47), channel_id=1, source_target_pairs={{0,8},{1,33},{2,10},{3,35},{4,12},{5,37},{6,14},{7,39},{8,16},{9,4... | collective-permute-start | bytes 1572872 | tf_op jit(solution)/shard_map/ppermute | solution.py:446
  103.7 12.0 %collective-permute-start.28 = (bf16[64,4096]{1,0:T(8,128)(2,1)S(1)}, bf16[64,4096]{1,0:T(8,128)(2,1)S(1)}, u32[]{:S(2)}, u32[]{:S(2)}) collective-permute-start(bf16[64,4096]{1,0:T(8,128)(2,1)S(1)} %get-tuple-element.49.refs_2_), channel_id=1, source_target_pairs={{0,96},{1,25},{2,98},{3,27},{4,100},{5,29},{6,102},{7,31},{8,104},... | collective-permute-start | bytes 1572872 | tf_op jit(solution)/shard_map/ppermute | solution.py:445
  106.7 11.8 %collective-permute-start.27 = (bf16[64,4096]{1,0:T(8,128)(2,1)S(1)}, bf16[64,4096]{1,0:T(8,128)(2,1)S(1)}, u32[]{:S(2)}, u32[]{:S(2)}) collective-permute-start(bf16[64,4096]{1,0:T(8,128)(2,1)S(1)} %get-tuple-element.50), channel_id=1, source_target_pairs={{0,32},{1,9},{2,34},{3,11},{4,36},{5,13},{6,38},{7,15},{8,40},{9,1... | collective-permute-start | bytes 1572872 | tf_op jit(solution)/shard_map/ppermute | solution.py:449
  107.6 10.9 %collective-permute-start.31 = (bf16[64,4096]{1,0:T(8,128)(2,1)S(1)}, bf16[64,4096]{1,0:T(8,128)(2,1)S(1)}, u32[]{:S(2)}, u32[]{:S(2)}) collective-permute-start(bf16[64,4096]{1,0:T(8,128)(2,1)S(1)} %get-tuple-element.53), channel_id=1, source_target_pairs={{33,0},{8,1},{35,2},{10,3},{37,4},{12,5},{39,6},{14,7},{41,8},{16,... | collective-permute-start | bytes 1572872 | tf_op jit(solution)/shard_map/ppermute | solution.py:450
  115.6 9.9 %collective-permute-start.32 = (bf16[64,4096]{1,0:T(8,128)(2,1)S(1)}, bf16[64,4096]{1,0:T(8,128)(2,1)S(1)}, u32[]{:S(2)}, u32[]{:S(2)}) collective-permute-start(bf16[64,4096]{1,0:T(8,128)(2,1)S(1)} %add_convert_fusion), channel_id=1, source_target_pairs={{97,0},{24,1},{99,2},{26,3},{101,4},{28,5},{103,6},{30,7},{105,8},... | collective-permute-start | bytes 1572872 | tf_op jit(solution)/shard_map/ppermute | solution.py:454
  115.8 9.7 %collective-permute-start.29 = (bf16[64,4096]{1,0:T(8,128)(2,1)S(1)}, bf16[64,4096]{1,0:T(8,128)(2,1)S(1)}, u32[]{:S(2)}, u32[]{:S(2)}) collective-permute-start(bf16[64,4096]{1,0:T(8,128)(2,1)S(1)} %add_convert_fusion.1), channel_id=1, source_target_pairs={{0,96},{1,25},{2,98},{3,27},{4,100},{5,29},{6,102},{7,31},{8,104},... | collective-permute-start | bytes 1572872 | tf_op jit(solution)/shard_map/ppermute | solution.py:453
  117.9 7.6 %collective-permute-start.30 = (bf16[64,4096]{1,0:T(8,128)(2,1)S(1)}, bf16[64,4096]{1,0:T(8,128)(2,1)S(1)}, u32[]{:S(2)}, u32[]{:S(2)}) collective-permute-start(bf16[64,4096]{1,0:T(8,128)(2,1)S(1)} %get-tuple-element.52), channel_id=1, source_target_pairs={{0,1},{1,0},{2,3},{3,2},{4,5},{5,4},{6,7},{7,6},{8,9},{9,8},{10,11... | collective-permute-start | bytes 1572872 | tf_op jit(solution)/shard_map/ppermute | solution.py:66
  126.6 10.6 %collective-permute-start.33 = (bf16[32,4096]{1,0:T(8,128)(2,1)}, bf16[32,4096]{1,0:T(8,128)(2,1)}, u32[]{:S(2)}, u32[]{:S(2)}) collective-permute-start(bf16[32,4096]{1,0:T(8,128)(2,1)} %get-tuple-element.56), channel_id=1, source_target_pairs={{0,24},{1,97},{2,26},{3,99},{4,28},{5,101},{6,30},{7,103},{8,0},{9... | collective-permute-start | bytes 786440 | tf_op jit(solution)/shard_map/ppermute | solution.py:79
  130.2 8.3 %collective-permute-start.34 = (bf16[32,4096]{1,0:T(8,128)(2,1)}, bf16[32,4096]{1,0:T(8,128)(2,1)}, u32[]{:S(2)}, u32[]{:S(2)}) collective-permute-start(bf16[32,4096]{1,0:T(8,128)(2,1)} %get-tuple-element.57), channel_id=1, source_target_pairs={{0,16},{1,65},{2,18},{3,67},{4,20},{5,69},{6,22},{7,71},{8,24},{9,... | collective-permute-start | bytes 786440 | tf_op jit(solution)/shard_map/ppermute | solution.py:79
  130.9 10.3 %collective-permute-start.35 = (bf16[32,4096]{1,0:T(8,128)(2,1)}, bf16[32,4096]{1,0:T(8,128)(2,1)}, u32[]{:S(2)}, u32[]{:S(2)}) collective-permute-start(bf16[32,4096]{1,0:T(8,128)(2,1)} %get-tuple-element.58), channel_id=1, source_target_pairs={{0,8},{1,33},{2,10},{3,35},{4,12},{5,37},{6,14},{7,39},{8,16},{9,4... | collective-permute-start | bytes 786440 | tf_op jit(solution)/shard_map/ppermute | solution.py:79
  (40 other events, 333.0 us)

commit v5 on v4

--- a/solution.py
+++ b/solution.py
@@ -137,7 +137,7 @@
             pltpu.VMEM((pieces[0].shape[0], columns), jnp.float32),
             pltpu.VMEM((pieces[0].shape[0], HD), jnp.float32),
         ],
-        compiler_params=pltpu.CompilerParams(vmem_limit_bytes=16 * 1024 * 1024),
+        compiler_params=pltpu.CompilerParams(vmem_limit_bytes=10485760),
         cost_estimate=pl.CostEstimate(
             flops=2 * 512 * 2048 * 256 + 2 * 2048 * 128 * 256,
             bytes_accessed=6 * 1024 * 1024,
@@ -188,7 +188,7 @@
         out_specs=whole(*"vvv"),
         out_shape=[wide, wide, jax.ShapeDtypeStruct((512, 128), jnp.float32)],
         input_output_aliases={4 + 2 * count + i: i for i in range(len(sums))},
-        compiler_params=pltpu.CompilerParams(vmem_limit_bytes=12 * 1024 * 1024),
+        compiler_params=pltpu.CompilerParams(vmem_limit_bytes=10485760),
         cost_estimate=pl.CostEstimate(
             flops=4 * 512 * 1024 * count * hidden,
             bytes_accessed=4096 * count * hidden,
@@ -240,7 +240,7 @@
             pltpu.VMEM((512, 128), jnp.float32),
             pltpu.VMEM((32, 16, hidden), jnp.bfloat16),
         ],
-        compiler_params=pltpu.CompilerParams(vmem_limit_bytes=16 * 1024 * 1024),
+        compiler_params=pltpu.CompilerParams(vmem_limit_bytes=12582912),
         cost_estimate=pl.CostEstimate(
             flops=4 * 512 * 1024 * hidden + 2 * 128 * hidden * width,
             bytes_accessed=4096 * hidden + 2 * hidden * width,
@@ -265,7 +265,7 @@
         in_specs=whole(*"vv") + [pl.BlockSpec(memory_space=pl.ANY)],
         out_specs=whole(*("vv" * len(picks))),
         out_shape=[jax.ShapeDtypeStruct((64, width), jnp.bfloat16)] * (2 * len(picks)),
-        compiler_params=pltpu.CompilerParams(vmem_limit_bytes=10 * 1024 * 1024),
+        compiler_params=pltpu.CompilerParams(vmem_limit_bytes=8388608),
         cost_estimate=pl.CostEstimate(
             flops=2 * 128 * len(picks) * hidden * width,
             bytes_accessed=2 * hidden * width,
@@ -292,8 +292,36 @@
         in_specs=whole(*("v" * 2 * terms)),
         out_specs=whole(*("v" * SIDE)),
         out_shape=[jax.ShapeDtypeStruct((32, width), jnp.bfloat16)] * SIDE,
-        compiler_params=pltpu.CompilerParams(vmem_limit_bytes=12582912),
+        compiler_params=pltpu.CompilerParams(vmem_limit_bytes=6291456),
     )(*own, *other)
+
+
+def unpack_kernel(has_hidden, a, b, c, d, order, *refs):
+    total = a[...].astype(jnp.float32)
+    for shard in (b, c, d):
+        total = total + shard[...].astype(jnp.float32)
+    table = order[...]
+    rows = jnp.dot(table, total.astype(jnp.bfloat16), preferred_element_type=jnp.float32)
+    width = a.shape[1]
+    outs = refs[1:] if has_hidden else refs
+    for i, out in enumerate(outs):
+        out[:, :width] = rows[i * 8 : (i + 1) * 8].astype(out.dtype)
+    if has_hidden:
+        rows = jnp.dot(table, refs[0][...], preferred_element_type=jnp.float32)
+        for i, out in enumerate(outs):
+            out[:, width:] = rows[i * 8 : (i + 1) * 8].astype(out.dtype)
+
+
+def unpacked(blocks, order, hidden=None):
+    width = blocks[0].shape[1]
+    more = [] if hidden is None else [hidden]
+    return pl.pallas_call(
+        lambda *refs: unpack_kernel(bool(more), *refs),
+        in_specs=whole(*("v" * (5 + len(more)))),
+        out_specs=whole(*("v" * SIDE)),
+        out_shape=[jax.ShapeDtypeStruct((8, width * (1 + len(more))), jnp.bfloat16)] * SIDE,
+        compiler_params=pltpu.CompilerParams(vmem_limit_bytes=5242880),
+    )(*blocks, order, *more)
 
 
 def pick_kernel(at_ref, where, *refs):
@@ -313,7 +341,7 @@
         in_specs=whole("s", "s", *("v" * len(shards))) + [pl.BlockSpec(memory_space=pl.ANY)],
         out_specs=whole(*"vv"),
         out_shape=[jax.ShapeDtypeStruct((16, 16 * shards[0].shape[-1]), jnp.bfloat16)] * 2,
-        compiler_params=pltpu.CompilerParams(vmem_limit_bytes=8 * 1024 * 1024),
+        compiler_params=pltpu.CompilerParams(vmem_limit_bytes=4194304),
     )(at, where, *shards, after)
 
 
@@ -460,7 +488,7 @@
         jnp.concatenate([at(0), at(1), at(3), at(2)]),
         where,
         [mine[d] for d in names] + [theirs[d] for d in names],
-        side_out[0],
+        near_out[0],
     )
     hidden_rows = jnp.concatenate([hidden_mine, sibling(hidden_theirs)], axis=0)
     slots = n_exp * CAP
@@ -470,13 +498,10 @@
         target[:, None] == jnp.arange(slots, dtype=jnp.int32)[None, :], 1.0, 0.0
     ).astype(jnp.bfloat16)
     per_z = 2 * CAP
-    column_rows = added(dealt(line, first_axis, -1)).astype(jnp.bfloat16)
     row = jnp.arange(slots, dtype=jnp.int32)
     source = (row // CAP % 2) * n1 + (z_here - row // per_z) % SIDE * CAP + row % CAP
     reorder = jnp.where(source[:, None] == row[None, :], 1.0, 0.0).astype(jnp.bfloat16)
-    column_rows = jnp.concatenate([column_rows, hidden_rows], axis=1)
-    sent = jnp.dot(reorder, column_rows, preferred_element_type=jnp.float32).astype(jnp.bfloat16)
-    sent = [sent[d * per_z : (d + 1) * per_z] for d in range(SIDE)]
+    sent = unpacked(dealt(line, first_axis, -1), reorder, hidden_rows)
     expert_rows = jnp.concatenate(dealt(sent, z_axis, -1), axis=0)
     picked = jnp.dot(match_table, expert_rows, preferred_element_type=jnp.float32).reshape(
         token_count, 2, -1

time: 156 us -> 154 us (0.987)
  waiting for transfers between devices: 54.7 us -> 47.6 us
  local copies, waits for them, and re-layouts: 9.65 us -> 13.8 us
  starting transfers between devices: 62.1 us -> 64.8 us
    ppermute x1, waiting for transfers between devices: 7.83 us -> 0.01 us  [per_device(): far_theirs = lax.ppermute(far_theirs, BOTH, first_axis(1))]
    ppermute x1, waiting for transfers between devices: 6.97 us -> 1.57 us  [per_device(): other.append(lax.ppermute(front_theirs, BOTH, uncrossed(-1)))]
    unnamed x63 -> x79, local copies, waits for them, and re-layouts: 6.91 us -> 11.7 us
    ppermute x9, waiting for transfers between devices: 18.8 us -> 21.9 us  [dealt(): got[d] = lax.ppermute(blocks[d], BOTH, along(sign * d))]
    ppermute x1, waiting for transfers between devices: 0.01 us -> 3.01 us  [per_device(): own = [near_out[0], lax.ppermute(front_mine, BOTH, second_axis(1))]]
    ppermute x1, starting transfers between devices: 0.07 us -> 2.95 us  [per_device(): other.append(lax.ppermute(front_theirs, BOTH, uncrossed(-1)))]
  transfers between devices with their start and end apart: 41 -> 41, of which waited for: 21 -> 21; matrix products, arithmetic and copies ran while one was open for 6% -> 5% of each run, Pallas kernels for 6% -> 7%
where the time goes in v5:
time: 154 us
  starting transfers between devices  64.8 us (42%)
  waiting for transfers between devices  47.6 us (31%)
  Pallas kernels  17.8 us (12%)
  local copies, waits for them, and re-layouts  13.8 us (9%)
  other arithmetic  7.39 us (5%)
    ppermute x9, waiting for transfers between devices, dealt(): got[d] = lax.ppermute(blocks[d], BOTH, along(sign * d))  21.9 us
    ppermute x9, starting transfers between devices, gathered(): got[d] = lax.ppermute(shard, BOTH, along(d))  15.2 us
    ppermute x9, starting transfers between devices, dealt(): got[d] = lax.ppermute(blocks[d], BOTH, along(sign * d))  14.8 us
    unnamed x79, local copies, waits for them, and re-layouts  11.7 us
    ppermute x9, waiting for transfers between devices, gathered(): got[d] = lax.ppermute(shard, BOTH, along(d))  9.07 us
    ppermute x3, starting transfers between devices, onward(): lax.ppermute(shard, 'ctx', [(i, (i + step) % n_ctx) for i in range(n_ctx)])  6.84 us
    pallas_call x2, Pallas kernels, first_products(): pl.pallas_call(lambda *refs: first_kernel(count, bool(sums), *refs), in_s...  6.54 us
    pallas_call x1, Pallas kernels, last_products(): pl.pallas_call(lambda *refs: last_kernel(width, *refs), in_specs=whole(*'...  4.47 us
  transfers between devices with their start and end apart: 41, of which 21 were waited for; matrix products, arithmetic and copies ran while one was open for 5% of the time, Pallas kernels for 7%

profile of v5, /device:TPU:0, one launch (start us, length us, event | category | flops | bytes accessed | tf_op | source)
XLA Modules:
  0.0 153.8 jit_solution(13887123799282180596)
XLA Ops:
  2.4 2.9 %collective-permute-start.1 = (bf16[64,256]{1,0:T(8,128)(2,1)S(1)}, bf16[64,256]{1,0:T(8,128)(2,1)S(1)}, u32[]{:S(2)}, u32[]{:S(2)}) collective-permute-start(bf16[64,256]{1,0:T(8,128)(2,1)S(1)} %pad_add_fusion), channel_id=1, source_target_pairs={{0,16},{8,24},{16,32},{24,40},{32,48},{40,56},{48,64},{56,72},{64,... | collective-permute-start | bytes 98312 | tf_op jit(solution)/shard_map/ppermute | solution.py:383
  5.3 2.3 %collective-permute-start.2 = (bf16[64,256]{1,0:T(8,128)(2,1)S(1)}, bf16[64,256]{1,0:T(8,128)(2,1)S(1)}, u32[]{:S(2)}, u32[]{:S(2)}) collective-permute-start(bf16[64,256]{1,0:T(8,128)(2,1)S(1)} %pad_add_fusion), channel_id=1, source_target_pairs={{0,24},{8,32},{16,40},{24,48},{32,56},{40,64},{48,72},{56,80},{64,... | collective-permute-start | bytes 98312 | tf_op jit(solution)/shard_map/ppermute | solution.py:383
  19.7 3.0 %collective-permute-done.4 = bf16[32,2048]{1,0:T(8,128)(2,1)S(1)} collective-permute-done((bf16[32,2048]{1,0:T(8,128)(2,1)S(1)}, bf16[32,2048]{1,0:T(8,128)(2,1)S(1)}, u32[]{:S(2)}, u32[]{:S(2)}) %collective-permute-start.4) | collective-permute-done | bytes 131104 | tf_op jit(solution)/shard_map/ppermute | solution.py:72
  22.7 4.1 %all-to-all-start = ((bf16[16,8,384]{2,1,0:T(8,128)(2,1)}), bf16[16,8,384]{2,1,0:T(8,128)(2,1)S(1)}, u32[]{:S(2)}, u32[]{:S(2)}) async-start(bf16[16,8,384]{2,1,0:T(8,128)(2,1)} %pad_maximum_fusion.8), calls=%async_computation | async-start | bytes 196608 | tf_op jit(solution)/shard_map/all_to_all | solution.py:426
  28.9 2.7 %collective-permute-start.8 = (bf16[128,2048]{1,0:T(8,128)(2,1)S(1)}, bf16[128,2048]{1,0:T(8,128)(2,1)S(1)}, u32[]{:S(2)}, u32[]{:S(2)}) collective-permute-start(bf16[128,2048]{1,0:T(8,128)(2,1)S(1)} %pad_maximum_fusion.p0), channel_id=1, source_target_pairs={{0,64},{1,17},{2,66},{3,19},{4,68},{5,21},{6,70},{7,23},{8,72},{9,... | collective-permute-start | bytes 1572872 | tf_op jit(solution)/shard_map/ppermute | solution.py:72
  38.6 4.0 %collective-permute-start.12 = (bf16[2,16,8,128]{3,2,1,0:T(8,128)(2,1)S(1)}, bf16[2,16,8,128]{3,2,1,0:T(8,128)(2,1)S(1)}, u32[]{:S(2)}, u32[]{:S(2)}) collective-permute-start(bf16[2,16,8,128]{3,2,1,0:T(8,128)(2,1)S(1)} %pad_maximum_fusion.9), channel_id=1, source_target_pairs={{0,4},{1,5},{2,6},{3,7},{4,0},{5,1},{6,2},{7,3},{8,12},{9,13},{10,... | collective-permute-start | bytes 196616 | tf_op jit(solution)/shard_map/ppermute | solution.py:430
  42.6 2.2 %collective-permute-done.12 = bf16[2,16,8,128]{3,2,1,0:T(8,128)(2,1)S(1)} collective-permute-done((bf16[2,16,8,128]{3,2,1,0:T(8,128)(2,1)S(1)}, bf16[2,16,8,128]{3,2,1,0:T(8,128)(2,1)S(1)}, u32[]{:S(2)}, u32[]{:S(2)}) %collective-permute-start.12) | collective-permute-done | bytes 65568 | tf_op jit(solution)/shard_map/ppermute | solution.py:430
  44.8 2.6 %shard_map.118 = bf16[4,2,4,4,16,256]{5,4,3,2,1,0:T(8,128)(2,1)S(1)} custom-call(s32[3]{0:T(128)S(1)} %pad_add_fusion.2.where.refs_10_, s32[16]{0:T(128)S(1)} %select_n.220.place, bf16[128,2048]{1,0:T(8,128)(2,1)S(1)} %pad_maximum_fusion.p0, bf16[128,2048]{1,0:T(8,128)(2,1)S(1)} %collective-permute-done.7.p1, ...), custom_call_target="tpu_custom_call" | custom-call | flops 671088640 | bytes 6291456 | tf_op jit(solution)/shard_map/pallas_call | solution.py:131
  49.2 3.6 %collective-permute-start.14 = (bf16[2,4,4,16,256]{4,3,2,1,0:T(8,128)(2,1)S(1)}, bf16[2,4,4,16,256]{4,3,2,1,0:T(8,128)(2,1)S(1)}, u32[]{:S(2)}, u32[]{:S(2)}) collective-permute-start(bf16[2,4,4,16,256]{4,3,2,1,0:T(8,128)(2,1)S(1)} %get-tuple-element.71), channel_id=1, source_target_pairs={{0,4},{1,5},{2,6},{3,7},{4,0},{5,1},{6,2},{7,3},{8,12},{9,13},{10,... | collective-permute-start | bytes 786440 | tf_op jit(solution)/shard_map/ppermute | solution.py:79
  53.7 4.7 %collective-permute-done.13 = bf16[2,4,4,16,256]{4,3,2,1,0:T(8,128)(2,1)S(1)} collective-permute-done((bf16[2,4,4,16,256]{4,3,2,1,0:T(8,128)(2,1)S(1)}, bf16[2,4,4,16,256]{4,3,2,1,0:T(8,128)(2,1)S(1)}, u32[]{:S(2)}, u32[]{:S(2)}) %collective-permute-start.13) | collective-permute-done | bytes 262176 | tf_op jit(solution)/shard_map/ppermute | solution.py:79
  58.4 3.2 %collective-permute-done.14 = bf16[2,4,4,16,256]{4,3,2,1,0:T(8,128)(2,1)S(1)} collective-permute-done((bf16[2,4,4,16,256]{4,3,2,1,0:T(8,128)(2,1)S(1)}, bf16[2,4,4,16,256]{4,3,2,1,0:T(8,128)(2,1)S(1)}, u32[]{:S(2)}, u32[]{:S(2)}) %collective-permute-start.14) | collective-permute-done | bytes 262176 | tf_op jit(solution)/shard_map/ppermute | solution.py:79
  63.3 2.1 %collective-permute-start.17 = (bf16[2,256,256]{2,1,0:T(8,128)(2,1)S(1)}, bf16[2,256,256]{2,1,0:T(8,128)(2,1)S(1)}, u32[]{:S(2)}, u32[]{:S(2)}) collective-permute-start(bf16[2,256,256]{2,1,0:T(8,128)(2,1)S(1)} %bitcast.148), channel_id=1, source_target_pairs={{0,16},{1,65},{2,18},{3,67},{4,20},{5,69},{6,22},{7,71},{8,24},{9,... | collective-permute-start | bytes 786440 | tf_op jit(solution)/shard_map/ppermute | solution.py:72
  66.9 2.5 %collective-permute-done.16 = bf16[2,256,256]{2,1,0:T(8,128)(2,1)S(1)} collective-permute-done((bf16[2,256,256]{2,1,0:T(8,128)(2,1)S(1)}, bf16[2,256,256]{2,1,0:T(8,128)(2,1)S(1)}, u32[]{:S(2)}, u32[]{:S(2)}) %collective-permute-start.16) | collective-permute-done | bytes 262176 | tf_op jit(solution)/shard_map/ppermute | solution.py:72
  69.5 3.1 %collective-permute-done.17 = bf16[2,256,256]{2,1,0:T(8,128)(2,1)S(1)} collective-permute-done((bf16[2,256,256]{2,1,0:T(8,128)(2,1)S(1)}, bf16[2,256,256]{2,1,0:T(8,128)(2,1)S(1)}, u32[]{:S(2)}, u32[]{:S(2)}) %collective-permute-start.17) | collective-permute-done | bytes 262176 | tf_op jit(solution)/shard_map/ppermute | solution.py:72
  73.3 2.3 %collective-permute-start.20 = (bf16[4,256,256]{2,1,0:T(8,128)(2,1)S(1)}, bf16[4,256,256]{2,1,0:T(8,128)(2,1)S(1)}, u32[]{:S(2)}, u32[]{:S(2)}) collective-permute-start(bf16[4,256,256]{2,1,0:T(8,128)(2,1)S(1)} %pad_maximum_fusion.2), channel_id=1, source_target_pairs={{0,97},{1,24},{2,99},{3,26},{4,101},{5,28},{6,103},{7,30},{8,105},... | collective-permute-start | bytes 1572872 | tf_op jit(solution)/shard_map/ppermute | solution.py:455
  77.0 2.2 %collective-permute-start.24 = (bf16[4,256,256]{2,1,0:T(8,128)(2,1)S(1)}, bf16[4,256,256]{2,1,0:T(8,128)(2,1)S(1)}, u32[]{:S(2)}, u32[]{:S(2)}) collective-permute-start(bf16[4,256,256]{2,1,0:T(8,128)(2,1)S(1)} %pad_maximum_fusion.1.refs_1_), channel_id=1, source_target_pairs={{0,96},{1,25},{2,98},{3,27},{4,100},{5,29},{6,102},{7,31},{8,104},... | collective-permute-start | bytes 1572872 | tf_op jit(solution)/shard_map/ppermute | solution.py:454
  79.4 3.0 %copy-done.1 = bf16[1,4096,768]{2,1,0:T(8,128)(2,1)S(1)} copy-done((bf16[1,4096,768]{2,1,0:T(8,128)(2,1)S(1)}, bf16[1,4096,768]{2,1,0:T(8,128)(2,1)}, u32[]{:S(2)}) %copy-start.1) | copy-done | bytes 6291480
  82.4 2.3 %shard_map.119 = (f32[512,768]{1,0:T(8,128)S(1)}, f32[512,768]{1,0:T(8,128)S(1)}, f32[512,128]{1,0:T(8,128)S(1)}) custom-call(s32[8]{0:T(128)S(1)} %pad_add_fusion.3.refs_0_, bf16[4,256,256]{2,1,0:T(8,128)(2,1)S(1)} %pad_maximum_fusion.1.refs_1_, bf16[4,256,256]{2,1,0:T(8,128)(2,1)S(1)} %collective-permute-done.21.refs_2_, f32[16,1,256]{2,1,0:T(1,128)S(1)} %bitcast.139, ...), custom_call_target="tpu_custom_call" | custom-call | flops 1610612736 | bytes 3145728 | tf_op jit(solution)/shard_map/pallas_call | solution.py:185
  86.1 2.7 %collective-permute-start.23 = (bf16[4,256,256]{2,1,0:T(8,128)(2,1)S(1)}, bf16[4,256,256]{2,1,0:T(8,128)(2,1)S(1)}, u32[]{:S(2)}, u32[]{:S(2)}) collective-permute-start(bf16[4,256,256]{2,1,0:T(8,128)(2,1)S(1)} %collective-permute-done.20.refs_4_), channel_id=1, source_target_pairs={{0,24},{1,97},{2,26},{3,99},{4,28},{5,101},{6,30},{7,103},{8,0},{9... | collective-permute-start | bytes 1572872 | tf_op jit(solution)/shard_map/ppermute | solution.py:465
  89.0 2.4 %collective-permute-done.25.refs_3_ = bf16[4,256,256]{2,1,0:T(8,128)(2,1)S(1)} collective-permute-done((bf16[4,256,256]{2,1,0:T(8,128)(2,1)S(1)}, bf16[4,256,256]{2,1,0:T(8,128)(2,1)S(1)}, u32[]{:S(2)}, u32[]{:S(2)}) %collective-permute-start.25) | collective-permute-done | bytes 524320 | tf_op jit(solution)/shard_map/ppermute | solution.py:455
  91.4 4.2 %shard_map.120 = (f32[512,768]{1,0:T(8,128)S(1)}, f32[512,768]{1,0:T(8,128)S(1)}, f32[512,128]{1,0:T(8,128)S(1)}) custom-call(s32[16]{0:T(128)S(1)} %pad_add_fusion.4.refs_0_, bf16[4,256,256]{2,1,0:T(8,128)(2,1)S(1)} %collective-permute-done.19.refs_1_, ...), custom_call_target="tpu_custom_call", output_to_operand_aliasing={{0}: (8, {}), {1}: (9, {}), {2}: (10, {})} | custom-call | flops 3221225472 | bytes 6291456 | tf_op jit(solution)/shard_map/pallas_call | solution.py:185
  97.4 4.5 %shard_map.121 = (bf16[64,4096]{1,0:T(8,128)(2,1)S(1)}, bf16[64,4096]{1,0:T(8,128)(2,1)}, bf16[512,768]{1,0:T(8,128)(2,1)S(1)}) custom-call(s32[8]{0:T(128)S(1)} %pad_add_fusion.1.refs_0_, bf16[4,256,256]{2,1,0:T(8,128)(2,1)S(1)} %collective-permute-done.22.refs_1_, bf16[4,256,256]{2,1,0:T(8,128)(2,1)S(1)} %collective-permute-done.23.refs_2_, ...), custom_call_target="tpu_custom_call" | custom-call | flops 2415919104 | bytes 9437184 | tf_op jit(solution)/shard_map/pallas_call | solution.py:231
  102.7 2.0 %collective-permute-start.26 = (bf16[64,4096]{1,0:T(8,128)(2,1)}, bf16[64,4096]{1,0:T(8,128)(2,1)}, u32[]{:S(2)}, u32[]{:S(2)}) collective-permute-start(bf16[64,4096]{1,0:T(8,128)(2,1)} %get-tuple-element.51), channel_id=1, source_target_pairs={{0,8},{1,33},{2,10},{3,35},{4,12},{5,37},{6,14},{7,39},{8,16},{9,4... | collective-permute-start | bytes 1572872 | tf_op jit(solution)/shard_map/ppermute | solution.py:474
  106.7 2.8 %copy-done.3 = bf16[1,768,4096]{2,1,0:T(8,128)(2,1)S(1)} copy-done((bf16[1,768,4096]{2,1,0:T(8,128)(2,1)S(1)}, bf16[1,768,4096]{2,1,0:T(8,128)(2,1)}, u32[]{:S(2)}) %copy-start.3) | copy-done | bytes 6291480
  114.5 3.0 %collective-permute-start.32 = (bf16[64,4096]{1,0:T(8,128)(2,1)S(1)}, bf16[64,4096]{1,0:T(8,128)(2,1)S(1)}, u32[]{:S(2)}, u32[]{:S(2)}) collective-permute-start(bf16[64,4096]{1,0:T(8,128)(2,1)S(1)} %add_convert_fusion), channel_id=1, source_target_pairs={{97,0},{24,1},{99,2},{26,3},{101,4},{28,5},{103,6},{30,7},{105,8},... | collective-permute-start | bytes 1572872 | tf_op jit(solution)/shard_map/ppermute | solution.py:482
  117.9 2.8 %copy-done.4 = bf16[1,768,4096]{2,1,0:T(8,128)(2,1)S(1)} copy-done((bf16[1,768,4096]{2,1,0:T(8,128)(2,1)S(1)}, bf16[1,768,4096]{2,1,0:T(8,128)(2,1)}, u32[]{:S(2)}) %copy-start.4) | copy-done | bytes 6291480
  123.9 3.0 %collective-permute-done.27.refs_1_ = bf16[64,4096]{1,0:T(8,128)(2,1)S(1)} collective-permute-done((bf16[64,4096]{1,0:T(8,128)(2,1)S(1)}, bf16[64,4096]{1,0:T(8,128)(2,1)S(1)}, u32[]{:S(2)}, u32[]{:S(2)}) %collective-permute-start.27) | collective-permute-done | bytes 524320 | tf_op jit(solution)/shard_map/ppermute | solution.py:477
  133.8 3.8 %collective-permute-done.33.refs_1_ = bf16[32,4096]{1,0:T(8,128)(2,1)S(1)} collective-permute-done((bf16[32,4096]{1,0:T(8,128)(2,1)S(1)}, bf16[32,4096]{1,0:T(8,128)(2,1)S(1)}, u32[]{:S(2)}, u32[]{:S(2)}) %collective-permute-start.33) | collective-permute-done | bytes 262176 | tf_op jit(solution)/shard_map/ppermute | solution.py:79
  138.8 2.7 %collective-permute-done.35.refs_3_ = bf16[32,4096]{1,0:T(8,128)(2,1)S(1)} collective-permute-done((bf16[32,4096]{1,0:T(8,128)(2,1)S(1)}, bf16[32,4096]{1,0:T(8,128)(2,1)S(1)}, u32[]{:S(2)}, u32[]{:S(2)}) %collective-permute-start.35) | collective-permute-done | bytes 262176 | tf_op jit(solution)/shard_map/ppermute | solution.py:79
  141.9 2.2 %collective-permute-start.37 = (bf16[8,8192]{1,0:T(8,128)(2,1)S(1)}, bf16[8,8192]{1,0:T(8,128)(2,1)S(1)}, u32[]{:S(2)}, u32[]{:S(2)}) collective-permute-start(bf16[8,8192]{1,0:T(8,128)(2,1)S(1)} %get-tuple-element.66), channel_id=1, source_target_pairs={{0,6},{1,7},{2,0},{3,1},{4,2},{5,3},{6,4},{7,5},{8,14},{9,15},{10,... | collective-permute-start | bytes 393224 | tf_op jit(solution)/shard_map/ppermute | solution.py:79
  145.7 2.3 %collective-permute-done.37 = bf16[8,8192]{1,0:T(8,128)(2,1)S(1)} collective-permute-done((bf16[8,8192]{1,0:T(8,128)(2,1)S(1)}, bf16[8,8192]{1,0:T(8,128)(2,1)S(1)}, u32[]{:S(2)}, u32[]{:S(2)}) %collective-permute-start.37) | collective-permute-done | bytes 131104 | tf_op jit(solution)/shard_map/ppermute | solution.py:79
  148.0 2.6 %collective-permute-done.38 = bf16[8,8192]{1,0:T(8,128)(2,1)S(1)} collective-permute-done((bf16[8,8192]{1,0:T(8,128)(2,1)S(1)}, bf16[8,8192]{1,0:T(8,128)(2,1)S(1)}, u32[]{:S(2)}, u32[]{:S(2)}) %collective-permute-start.38) | collective-permute-done | bytes 131104 | tf_op jit(solution)/shard_map/ppermute | solution.py:79
  (201 shorter events, 58.9 us)
Async XLA Ops:
  0.8 11.6 %collective-permute-start = (bf16[64,256]{1,0:T(8,128)(2,1)S(1)}, bf16[64,256]{1,0:T(8,128)(2,1)S(1)}, u32[]{:S(2)}, u32[]{:S(2)}) collective-permute-start(bf16[64,256]{1,0:T(8,128)(2,1)S(1)} %pad_add_fusion), channel_id=1, source_target_pairs={{0,8},{8,16},{16,24},{24,32},{32,40},{40,48},{48,56},{56,64},{64,7... | collective-permute-start | bytes 98312 | tf_op jit(solution)/shard_map/ppermute | solution.py:383
  2.4 9.9 %collective-permute-start.1 = (bf16[64,256]{1,0:T(8,128)(2,1)S(1)}, bf16[64,256]{1,0:T(8,128)(2,1)S(1)}, u32[]{:S(2)}, u32[]{:S(2)}) collective-permute-start(bf16[64,256]{1,0:T(8,128)(2,1)S(1)} %pad_add_fusion), channel_id=1, source_target_pairs={{0,16},{8,24},{16,32},{24,40},{32,48},{40,56},{48,64},{56,72},{64,... | collective-permute-start | bytes 98312 | tf_op jit(solution)/shard_map/ppermute | solution.py:383
  5.3 7.0 %collective-permute-start.2 = (bf16[64,256]{1,0:T(8,128)(2,1)S(1)}, bf16[64,256]{1,0:T(8,128)(2,1)S(1)}, u32[]{:S(2)}, u32[]{:S(2)}) collective-permute-start(bf16[64,256]{1,0:T(8,128)(2,1)S(1)} %pad_add_fusion), channel_id=1, source_target_pairs={{0,24},{8,32},{16,40},{24,48},{32,56},{40,64},{48,72},{56,80},{64,... | collective-permute-start | bytes 98312 | tf_op jit(solution)/shard_map/ppermute | solution.py:383
  7.6 37.2 %collective-permute-start.10 = (bf16[1024,256]{1,0:T(8,128)(2,1)}, bf16[1024,256]{1,0:T(8,128)(2,1)S(1)}, u32[]{:S(2)}, u32[]{:S(2)}) collective-permute-start(bf16[1024,256]{1,0:T(8,128)(2,1)} %w0.1), channel_id=1, source_target_pairs={{0,1},{1,0},{2,3},{3,2},{4,5},{5,4},{6,7},{7,6},{8,9},{9,8},{10,11... | collective-permute-start | bytes 1572872 | tf_op jit(solution)/shard_map/ppermute | solution.py:66
  15.0 7.7 %collective-permute-start.4 = (bf16[32,2048]{1,0:T(8,128)(2,1)S(1)}, bf16[32,2048]{1,0:T(8,128)(2,1)S(1)}, u32[]{:S(2)}, u32[]{:S(2)}) collective-permute-start(bf16[32,2048]{1,0:T(8,128)(2,1)S(1)} %pad_maximum_fusion.6), channel_id=1, source_target_pairs={{0,8},{1,33},{2,10},{3,35},{4,12},{5,37},{6,14},{7,39},{8,16},{9,4... | collective-permute-start | bytes 393224 | tf_op jit(solution)/shard_map/ppermute | solution.py:72
  15.8 11.0 %collective-permute-start.5 = (bf16[32,2048]{1,0:T(8,128)(2,1)S(1)}, bf16[32,2048]{1,0:T(8,128)(2,1)S(1)}, u32[]{:S(2)}, u32[]{:S(2)}) collective-permute-start(bf16[32,2048]{1,0:T(8,128)(2,1)S(1)} %pad_maximum_fusion.6), channel_id=1, source_target_pairs={{0,16},{1,65},{2,18},{3,67},{4,20},{5,69},{6,22},{7,71},{8,24},{9,... | collective-permute-start | bytes 393224 | tf_op jit(solution)/shard_map/ppermute | solution.py:72
  17.3 9.5 %collective-permute-start.6 = (bf16[32,2048]{1,0:T(8,128)(2,1)S(1)}, bf16[32,2048]{1,0:T(8,128)(2,1)S(1)}, u32[]{:S(2)}, u32[]{:S(2)}) collective-permute-start(bf16[32,2048]{1,0:T(8,128)(2,1)S(1)} %pad_maximum_fusion.6), channel_id=1, source_target_pairs={{0,24},{1,97},{2,26},{3,99},{4,28},{5,101},{6,30},{7,103},{8,0},{9... | collective-permute-start | bytes 393224 | tf_op jit(solution)/shard_map/ppermute | solution.py:72
  22.7 11.9 %all-to-all-start = ((bf16[16,8,384]{2,1,0:T(8,128)(2,1)}), bf16[16,8,384]{2,1,0:T(8,128)(2,1)S(1)}, u32[]{:S(2)}, u32[]{:S(2)}) async-start(bf16[16,8,384]{2,1,0:T(8,128)(2,1)} %pad_maximum_fusion.8), calls=%async_computation | async-start | bytes 196608 | tf_op jit(solution)/shard_map/all_to_all | solution.py:426
  26.9 17.9 %collective-permute-start.7 = (bf16[128,2048]{1,0:T(8,128)(2,1)S(1)}, bf16[128,2048]{1,0:T(8,128)(2,1)S(1)}, u32[]{:S(2)}, u32[]{:S(2)}) collective-permute-start(bf16[128,2048]{1,0:T(8,128)(2,1)S(1)} %pad_maximum_fusion.p0), channel_id=1, source_target_pairs={{0,32},{1,9},{2,34},{3,11},{4,36},{5,13},{6,38},{7,15},{8,40},{9,1... | collective-permute-start | bytes 1572872 | tf_op jit(solution)/shard_map/ppermute | solution.py:72
  28.9 15.9 %collective-permute-start.8 = (bf16[128,2048]{1,0:T(8,128)(2,1)S(1)}, bf16[128,2048]{1,0:T(8,128)(2,1)S(1)}, u32[]{:S(2)}, u32[]{:S(2)}) collective-permute-start(bf16[128,2048]{1,0:T(8,128)(2,1)S(1)} %pad_maximum_fusion.p0), channel_id=1, source_target_pairs={{0,64},{1,17},{2,66},{3,19},{4,68},{5,21},{6,70},{7,23},{8,72},{9,... | collective-permute-start | bytes 1572872 | tf_op jit(solution)/shard_map/ppermute | solution.py:72
  31.6 13.2 %collective-permute-start.9 = (bf16[128,2048]{1,0:T(8,128)(2,1)S(1)}, bf16[128,2048]{1,0:T(8,128)(2,1)S(1)}, u32[]{:S(2)}, u32[]{:S(2)}) collective-permute-start(bf16[128,2048]{1,0:T(8,128)(2,1)S(1)} %pad_maximum_fusion.p0), channel_id=1, source_target_pairs={{0,96},{1,25},{2,98},{3,27},{4,100},{5,29},{6,102},{7,31},{8,104},... | collective-permute-start | bytes 1572872 | tf_op jit(solution)/shard_map/ppermute | solution.py:72
  47.5 10.9 %collective-permute-start.13 = (bf16[2,4,4,16,256]{4,3,2,1,0:T(8,128)(2,1)S(1)}, bf16[2,4,4,16,256]{4,3,2,1,0:T(8,128)(2,1)S(1)}, u32[]{:S(2)}, u32[]{:S(2)}) collective-permute-start(bf16[2,4,4,16,256]{4,3,2,1,0:T(8,128)(2,1)S(1)} %get-tuple-element.69), channel_id=1, source_target_pairs={{0,2},{1,3},{2,4},{3,5},{4,6},{5,7},{6,0},{7,1},{8,10},{9,11},{10,... | collective-permute-start | bytes 786440 | tf_op jit(solution)/shard_map/ppermute | solution.py:79
  49.2 12.4 %collective-permute-start.14 = (bf16[2,4,4,16,256]{4,3,2,1,0:T(8,128)(2,1)S(1)}, bf16[2,4,4,16,256]{4,3,2,1,0:T(8,128)(2,1)S(1)}, u32[]{:S(2)}, u32[]{:S(2)}) collective-permute-start(bf16[2,4,4,16,256]{4,3,2,1,0:T(8,128)(2,1)S(1)} %get-tuple-element.71), channel_id=1, source_target_pairs={{0,4},{1,5},{2,6},{3,7},{4,0},{5,1},{6,2},{7,3},{8,12},{9,13},{10,... | collective-permute-start | bytes 786440 | tf_op jit(solution)/shard_map/ppermute | solution.py:79
  52.7 8.9 %collective-permute-start.15 = (bf16[2,4,4,16,256]{4,3,2,1,0:T(8,128)(2,1)S(1)}, bf16[2,4,4,16,256]{4,3,2,1,0:T(8,128)(2,1)S(1)}, u32[]{:S(2)}, u32[]{:S(2)}) collective-permute-start(bf16[2,4,4,16,256]{4,3,2,1,0:T(8,128)(2,1)S(1)} %get-tuple-element.70), channel_id=1, source_target_pairs={{0,6},{1,7},{2,0},{3,1},{4,2},{5,3},{6,4},{7,5},{8,14},{9,15},{10,... | collective-permute-start | bytes 786440 | tf_op jit(solution)/shard_map/ppermute | solution.py:79
  61.8 7.7 %collective-permute-start.16 = (bf16[2,256,256]{2,1,0:T(8,128)(2,1)S(1)}, bf16[2,256,256]{2,1,0:T(8,128)(2,1)S(1)}, u32[]{:S(2)}, u32[]{:S(2)}) collective-permute-start(bf16[2,256,256]{2,1,0:T(8,128)(2,1)S(1)} %bitcast.147), channel_id=1, source_target_pairs={{0,8},{1,33},{2,10},{3,35},{4,12},{5,37},{6,14},{7,39},{8,16},{9,4... | collective-permute-start | bytes 786440 | tf_op jit(solution)/shard_map/ppermute | solution.py:72
  63.3 9.3 %collective-permute-start.17 = (bf16[2,256,256]{2,1,0:T(8,128)(2,1)S(1)}, bf16[2,256,256]{2,1,0:T(8,128)(2,1)S(1)}, u32[]{:S(2)}, u32[]{:S(2)}) collective-permute-start(bf16[2,256,256]{2,1,0:T(8,128)(2,1)S(1)} %bitcast.148), channel_id=1, source_target_pairs={{0,16},{1,65},{2,18},{3,67},{4,20},{5,69},{6,22},{7,71},{8,24},{9,... | collective-permute-start | bytes 786440 | tf_op jit(solution)/shard_map/ppermute | solution.py:72
  65.4 7.7 %collective-permute-start.18 = (bf16[2,256,256]{2,1,0:T(8,128)(2,1)S(1)}, bf16[2,256,256]{2,1,0:T(8,128)(2,1)S(1)}, u32[]{:S(2)}, u32[]{:S(2)}) collective-permute-start(bf16[2,256,256]{2,1,0:T(8,128)(2,1)S(1)} %bitcast.149), channel_id=1, source_target_pairs={{0,24},{1,97},{2,26},{3,99},{4,28},{5,101},{6,30},{7,103},{8,0},{9... | collective-permute-start | bytes 786440 | tf_op jit(solution)/shard_map/ppermute | solution.py:72
  73.3 11.5 %collective-permute-start.20 = (bf16[4,256,256]{2,1,0:T(8,128)(2,1)S(1)}, bf16[4,256,256]{2,1,0:T(8,128)(2,1)S(1)}, u32[]{:S(2)}, u32[]{:S(2)}) collective-permute-start(bf16[4,256,256]{2,1,0:T(8,128)(2,1)S(1)} %pad_maximum_fusion.2), channel_id=1, source_target_pairs={{0,97},{1,24},{2,99},{3,26},{4,101},{5,28},{6,103},{7,30},{8,105},... | collective-permute-start | bytes 1572872 | tf_op jit(solution)/shard_map/ppermute | solution.py:455
  75.7 10.5 %collective-permute-start.19 = (bf16[4,256,256]{2,1,0:T(8,128)(2,1)S(1)}, bf16[4,256,256]{2,1,0:T(8,128)(2,1)S(1)}, u32[]{:S(2)}, u32[]{:S(2)}) collective-permute-start(bf16[4,256,256]{2,1,0:T(8,128)(2,1)S(1)} %pad_maximum_fusion.1.refs_1_), channel_id=1, source_target_pairs={{0,32},{1,9},{2,34},{3,11},{4,36},{5,13},{6,38},{7,15},{8,40},{9,1... | collective-permute-start | bytes 1572872 | tf_op jit(solution)/shard_map/ppermute | solution.py:454
  75.8 15.6 %collective-permute-start.25 = (bf16[4,256,256]{2,1,0:T(8,128)(2,1)S(1)}, bf16[4,256,256]{2,1,0:T(8,128)(2,1)S(1)}, u32[]{:S(2)}, u32[]{:S(2)}) collective-permute-start(bf16[4,256,256]{2,1,0:T(8,128)(2,1)S(1)} %pad_maximum_fusion.2), channel_id=1, source_target_pairs={{0,33},{1,8},{2,35},{3,10},{4,37},{5,12},{6,39},{7,14},{8,41},{9,1... | collective-permute-start | bytes 1572872 | tf_op jit(solution)/shard_map/ppermute | solution.py:455
  77.0 14.3 %collective-permute-start.24 = (bf16[4,256,256]{2,1,0:T(8,128)(2,1)S(1)}, bf16[4,256,256]{2,1,0:T(8,128)(2,1)S(1)}, u32[]{:S(2)}, u32[]{:S(2)}) collective-permute-start(bf16[4,256,256]{2,1,0:T(8,128)(2,1)S(1)} %pad_maximum_fusion.1.refs_1_), channel_id=1, source_target_pairs={{0,96},{1,25},{2,98},{3,27},{4,100},{5,29},{6,102},{7,31},{8,104},... | collective-permute-start | bytes 1572872 | tf_op jit(solution)/shard_map/ppermute | solution.py:454
  86.1 11.2 %collective-permute-start.22 = (bf16[4,256,256]{2,1,0:T(8,128)(2,1)S(1)}, bf16[4,256,256]{2,1,0:T(8,128)(2,1)S(1)}, u32[]{:S(2)}, u32[]{:S(2)}) collective-permute-start(bf16[4,256,256]{2,1,0:T(8,128)(2,1)S(1)} %collective-permute-done.19.refs_1_), channel_id=1, source_target_pairs={{0,32},{1,9},{2,34},{3,11},{4,36},{5,13},{6,38},{7,15},{8,40},{9,1... | collective-permute-start | bytes 1572872 | tf_op jit(solution)/shard_map/ppermute | solution.py:464
  86.1 11.2 %collective-permute-start.23 = (bf16[4,256,256]{2,1,0:T(8,128)(2,1)S(1)}, bf16[4,256,256]{2,1,0:T(8,128)(2,1)S(1)}, u32[]{:S(2)}, u32[]{:S(2)}) collective-permute-start(bf16[4,256,256]{2,1,0:T(8,128)(2,1)S(1)} %collective-permute-done.20.refs_4_), channel_id=1, source_target_pairs={{0,24},{1,97},{2,26},{3,99},{4,28},{5,101},{6,30},{7,103},{8,0},{9... | collective-permute-start | bytes 1572872 | tf_op jit(solution)/shard_map/ppermute | solution.py:465
  102.7 10.7 %collective-permute-start.26 = (bf16[64,4096]{1,0:T(8,128)(2,1)}, bf16[64,4096]{1,0:T(8,128)(2,1)}, u32[]{:S(2)}, u32[]{:S(2)}) collective-permute-start(bf16[64,4096]{1,0:T(8,128)(2,1)} %get-tuple-element.51), channel_id=1, source_target_pairs={{0,8},{1,33},{2,10},{3,35},{4,12},{5,37},{6,14},{7,39},{8,16},{9,4... | collective-permute-start | bytes 1572872 | tf_op jit(solution)/shard_map/ppermute | solution.py:474
  105.5 12.0 %collective-permute-start.28 = (bf16[64,4096]{1,0:T(8,128)(2,1)}, bf16[64,4096]{1,0:T(8,128)(2,1)S(1)}, u32[]{:S(2)}, u32[]{:S(2)}) collective-permute-start(bf16[64,4096]{1,0:T(8,128)(2,1)} %copy-done.10), channel_id=1, source_target_pairs={{0,96},{1,25},{2,98},{3,27},{4,100},{5,29},{6,102},{7,31},{8,104},... | collective-permute-start | bytes 1572872 | tf_op jit(solution)/shard_map/ppermute | solution.py:473
  112.4 14.5 %collective-permute-start.27 = (bf16[64,4096]{1,0:T(8,128)(2,1)S(1)}, bf16[64,4096]{1,0:T(8,128)(2,1)S(1)}, u32[]{:S(2)}, u32[]{:S(2)}) collective-permute-start(bf16[64,4096]{1,0:T(8,128)(2,1)S(1)} %get-tuple-element.54), channel_id=1, source_target_pairs={{0,32},{1,9},{2,34},{3,11},{4,36},{5,13},{6,38},{7,15},{8,40},{9,1... | collective-permute-start | bytes 1572872 | tf_op jit(solution)/shard_map/ppermute | solution.py:477
  113.4 13.6 %collective-permute-start.31 = (bf16[64,4096]{1,0:T(8,128)(2,1)S(1)}, bf16[64,4096]{1,0:T(8,128)(2,1)S(1)}, u32[]{:S(2)}, u32[]{:S(2)}) collective-permute-start(bf16[64,4096]{1,0:T(8,128)(2,1)S(1)} %get-tuple-element.57), channel_id=1, source_target_pairs={{33,0},{8,1},{35,2},{10,3},{37,4},{12,5},{39,6},{14,7},{41,8},{16,... | collective-permute-start | bytes 1572872 | tf_op jit(solution)/shard_map/ppermute | solution.py:478
  114.5 14.0 %collective-permute-start.32 = (bf16[64,4096]{1,0:T(8,128)(2,1)S(1)}, bf16[64,4096]{1,0:T(8,128)(2,1)S(1)}, u32[]{:S(2)}, u32[]{:S(2)}) collective-permute-start(bf16[64,4096]{1,0:T(8,128)(2,1)S(1)} %add_convert_fusion), channel_id=1, source_target_pairs={{97,0},{24,1},{99,2},{26,3},{101,4},{28,5},{103,6},{30,7},{105,8},... | collective-permute-start | bytes 1572872 | tf_op jit(solution)/shard_map/ppermute | solution.py:482
  117.6 10.9 %collective-permute-start.29 = (bf16[64,4096]{1,0:T(8,128)(2,1)S(1)}, bf16[64,4096]{1,0:T(8,128)(2,1)S(1)}, u32[]{:S(2)}, u32[]{:S(2)}) collective-permute-start(bf16[64,4096]{1,0:T(8,128)(2,1)S(1)} %add_convert_fusion.1), channel_id=1, source_target_pairs={{0,96},{1,25},{2,98},{3,27},{4,100},{5,29},{6,102},{7,31},{8,104},... | collective-permute-start | bytes 1572872 | tf_op jit(solution)/shard_map/ppermute | solution.py:481
  128.9 8.7 %collective-permute-start.33 = (bf16[32,4096]{1,0:T(8,128)(2,1)S(1)}, bf16[32,4096]{1,0:T(8,128)(2,1)S(1)}, u32[]{:S(2)}, u32[]{:S(2)}) collective-permute-start(bf16[32,4096]{1,0:T(8,128)(2,1)S(1)} %get-tuple-element.60), channel_id=1, source_target_pairs={{0,24},{1,97},{2,26},{3,99},{4,28},{5,101},{6,30},{7,103},{8,0},{9... | collective-permute-start | bytes 786440 | tf_op jit(solution)/shard_map/ppermute | solution.py:79
  130.9 8.0 %collective-permute-start.34 = (bf16[32,4096]{1,0:T(8,128)(2,1)S(1)}, bf16[32,4096]{1,0:T(8,128)(2,1)S(1)}, u32[]{:S(2)}, u32[]{:S(2)}) collective-permute-start(bf16[32,4096]{1,0:T(8,128)(2,1)S(1)} %get-tuple-element.61), channel_id=1, source_target_pairs={{0,16},{1,65},{2,18},{3,67},{4,20},{5,69},{6,22},{7,71},{8,24},{9,... | collective-permute-start | bytes 786440 | tf_op jit(solution)/shard_map/ppermute | solution.py:79
  132.4 9.1 %collective-permute-start.35 = (bf16[32,4096]{1,0:T(8,128)(2,1)S(1)}, bf16[32,4096]{1,0:T(8,128)(2,1)S(1)}, u32[]{:S(2)}, u32[]{:S(2)}) collective-permute-start(bf16[32,4096]{1,0:T(8,128)(2,1)S(1)} %get-tuple-element.62), channel_id=1, source_target_pairs={{0,8},{1,33},{2,10},{3,35},{4,12},{5,37},{6,14},{7,39},{8,16},{9,4... | collective-permute-start | bytes 786440 | tf_op jit(solution)/shard_map/ppermute | solution.py:79
  (48 other events, 387.6 us)
